TPU v7x, 256 devices: a whole 4x4x8 slice. The times are simulated.
256 devices in a mesh: ep: 8 (over y, core), seq: 32 (over z, x).
Axes of the slice: x: 4, y: 4, z: 8, core: 2. Of those that a mesh axis runs over, the one named last changes fastest.
Arguments:
- frames: bfloat16 [8, 22528, 512], P('ep', 'seq'), may hold values from -6 to 6
- lengths: int32 [8], P('ep'), may hold values from 11264 to 22528
- w_in: bfloat16 [512, 1024], replicated, may hold values from -0.25 to 0.25
- kernel: float32 [31, 512], replicated, may hold values from -1 to 1
- w_out: bfloat16 [512, 512], replicated, may hold values from -0.25 to 0.25
- pool_query: bfloat16 [8, 512], replicated, may hold values from -600 to 600
- w_value: bfloat16 [512, 512], replicated, may hold values from -0.25 to 0.25
- text_emb: bfloat16 [256, 512], replicated, may hold values from -6 to 6
- teacher: float32 [8, 256], P('ep'), may hold values from -6 to 6
Outputs:
- loss: float32 [], replicated
- grad_in: float32 [512, 1024], P('seq', 'ep')
- grad_out: float32 [512, 512], P('seq', 'ep')
- grad_kernel: float32 [31, 512], replicated
- grad_query: float32 [8, 512], replicated
- grad_value: float32 [512, 512], replicated
All inputs are finite; a program needn't handle non-finite values.
Results may differ from a plain program's by a relative error of at most 0.03.
Values may be sent and summed in bfloat16 or wider, within the bound.
No kernel may reach another device: no remote copies, remote signals or barrier semaphores. Data moves between devices by JAX's collectives and lax.ppermute only.
A program may use at most 64 MiB of HBM per device.

v0:
```python
import jax
import jax.numpy as jnp
from jax import lax
from jax.sharding import PartitionSpec as P


def padded_2(block, sides, width):
    for axis, dim in sides:
        count = lax.axis_size(axis)
        forward = [(i, i + 1) for i in range(count - 1)]
        backward = [(target, source) for source, target in forward]
        low = lax.ppermute(
            lax.slice_in_dim(block, block.shape[dim] - width, None, axis=dim), axis, forward
        )
        high = lax.ppermute(lax.slice_in_dim(block, 0, width, axis=dim), axis, backward)
        block = jnp.concatenate([low, block, high], axis=dim)
    return block


def shards(frames, lengths, w_in, kernel, w_out, pool_query, w_value, text_emb, teacher):
    hi = lax.Precision.HIGHEST
    n_epis, n_rows, width = frames.shape
    n_taps = kernel.shape[0]
    rim = n_taps // 2
    n_heads = pool_query.shape[0]
    head_dim = width // n_heads
    n_cands = text_emb.shape[0]
    root_width = jnp.sqrt(jnp.float32(width))
    offset = lax.axis_index("seq") * n_rows
    positions = offset + jnp.arange(n_rows, dtype=jnp.int32)
    valid = (positions[None, :] < lengths[:, None]).astype(jnp.float32)[..., None]
    xf = frames.astype(jnp.float32)
    mean_val = jnp.mean(xf, axis=-1, keepdims=True)
    var_val = jnp.mean((xf - mean_val) ** 2, axis=-1, keepdims=True)
    normed = ((xf - mean_val) * lax.rsqrt(var_val + 1e-05)).astype(jnp.bfloat16)
    mixed = jnp.einsum("esd,df->esf", normed, w_in, preferred_element_type=jnp.float32)
    sig = jax.nn.sigmoid(mixed[..., width:])
    glu = (mixed[..., :width] * sig * valid).astype(jnp.bfloat16)
    padded = padded_2(glu, (("seq", 1),), rim)
    conv = jnp.zeros((n_epis, n_rows, width), jnp.float32)
    for k in range(n_taps):
        conv = conv + kernel[k] * padded[:, k : k + n_rows].astype(jnp.float32)
    sconv = jax.nn.sigmoid(conv)
    act = (conv * sconv).astype(jnp.bfloat16)
    resid = xf + jnp.einsum("esd,df->esf", act, w_out, preferred_element_type=jnp.float32)
    queries = pool_query.astype(jnp.float32)
    scores = jnp.einsum("esd,hd->esh", resid, queries, precision=hi) / root_width
    masked = jnp.where(valid > 0, scores, -1e30)
    top = lax.pmax(jnp.max(masked, axis=1), "seq")
    expo = jnp.where(valid > 0, jnp.exp(masked - top[:, None]), 0.0)
    vec_here = jnp.einsum("esh,esd->ehd", expo, resid, precision=hi)
    total, vec = lax.psum((jnp.sum(expo, axis=1), vec_here), "seq")
    probs = jnp.where(valid > 0, jnp.exp(masked - top[:, None]), 0.0) / total[:, None]
    vbar = vec / total[..., None]
    wvals = w_value.astype(jnp.float32).reshape(width, n_heads, head_dim)
    pooled = jnp.einsum("ehd,dhk->ehk", vbar, wvals, precision=hi).reshape(n_epis, width)
    rms = jnp.sqrt(jnp.mean(pooled * pooled, axis=-1, keepdims=True) + 1e-06)
    emb = pooled / rms
    texts = text_emb.astype(jnp.float32)
    score = jnp.einsum("ed,cd->ec", emb, texts, precision=hi) / root_width
    diff = score - teacher
    loss_here = jnp.sum(diff * diff) / n_cands
    dscore = 2.0 * diff / n_cands
    demb = jnp.einsum("ec,cd->ed", dscore, texts, precision=hi) / root_width
    dpooled = (demb - emb * jnp.mean(demb * emb, axis=-1, keepdims=True)) / rms
    dp3 = dpooled.reshape(n_epis, n_heads, head_dim)
    value_here = jnp.einsum("ehd,ehk->dhk", vbar, dp3, precision=hi).reshape(width, width)
    dvbar = jnp.einsum("dhk,ehk->ehd", wvals, dp3, precision=hi)
    proj = jnp.einsum("esd,ehd->esh", resid, dvbar, precision=hi)
    centre = jnp.sum(dvbar * vbar, axis=-1)
    dscores = probs * (proj - centre[:, None])
    query_here = jnp.einsum("esh,esd->hd", dscores, resid, precision=hi) / root_width
    dresid = (
        jnp.einsum("esh,ehd->esd", probs, dvbar, precision=hi)
        + jnp.einsum("esh,hd->esd", dscores, queries, precision=hi) / root_width
    ).astype(jnp.bfloat16)
    out_here = jnp.einsum("esd,esf->df", act, dresid, preferred_element_type=jnp.float32)
    dact = jnp.einsum("esf,df->esd", dresid, w_out, preferred_element_type=jnp.float32)
    dconv = (dact * sconv * (1.0 + conv * (1.0 - sconv))).astype(jnp.bfloat16)
    dconv_f = dconv.astype(jnp.float32)
    dpad = padded_2(dconv, (("seq", 1),), rim)
    dglu = jnp.zeros((n_epis, n_rows, width), jnp.float32)
    taps = []
    for k in range(n_taps):
        dglu = dglu + kernel[k] * dpad[:, 2 * rim - k : 2 * rim - k + n_rows].astype(jnp.float32)
        taps.append(jnp.sum(padded[:, k : k + n_rows].astype(jnp.float32) * dconv_f, axis=(0, 1)))
    kernel_here = jnp.stack(taps)
    dglu = dglu * valid
    dmixed = jnp.concatenate(
        [dglu * sig, dglu * mixed[..., :width] * sig * (1.0 - sig)], axis=-1
    ).astype(jnp.bfloat16)
    in_here = jnp.einsum("esd,esf->df", normed, dmixed, preferred_element_type=jnp.float32)
    rows_in, rows_out = (
        lax.psum_scatter(
            in_here.astype(jnp.bfloat16), "seq", scatter_dimension=0, tiled=True
        ).astype(jnp.float32),
        lax.psum_scatter(
            out_here.astype(jnp.bfloat16), "seq", scatter_dimension=0, tiled=True
        ).astype(jnp.float32),
    )
    grad_in, grad_out = (
        lax.psum_scatter(
            rows_in.astype(jnp.bfloat16), "ep", scatter_dimension=1, tiled=True
        ).astype(jnp.float32),
        lax.psum_scatter(
            rows_out.astype(jnp.bfloat16), "ep", scatter_dimension=1, tiled=True
        ).astype(jnp.float32),
    )
    grad_kernel, grad_query = lax.psum((kernel_here, query_here), ("ep", "seq"))
    grad_value, loss = (
        lax.psum(value_here.astype(jnp.bfloat16), "ep").astype(jnp.float32),
        lax.psum(loss_here.astype(jnp.bfloat16), "ep").astype(jnp.float32),
    )
    return (loss, grad_in, grad_out, grad_kernel, grad_query, grad_value)


def solution(mesh):
    return jax.shard_map(
        shards,
        mesh=mesh,
        in_specs=(P("ep", "seq", None), P("ep"), P(), P(), P(), P(), P(), P(), P("ep", None)),
        out_specs=(P(), P("seq", "ep"), P("seq", "ep"), P(), P(), P()),
        check_vma=False,
    )
```

profile of v0, /device:TPU:8, one launch (start us, length us, event | category | flops | bytes accessed | tf_op | source)
XLA Modules:
  0.0 1101.9 jit_solution(10548095060268716896)
XLA Ops:
  9.3 1.5 fusion.5
  14.0 3.4 collective-permute-start
  20.1 2.9 collective-permute-done.1
  23.2 9.4 fusion.36
  34.7 76.1 %pmax.7 = f32[8]{0:T(128)S(1)} all-reduce(f32[8]{0:T(128)S(1)} %get-tuple-element.101), channel_id=1, replica_groups=mesh['ep'=8,'seq'=32] {'seq'}, use_global_device_ids=true, to_apply=%region_3.4 | all-reduce | flops 8 | bytes 64 | tf_op jit(solution)/shard_map/pmax | solution.py:49
  112.3 137.7 %all-reduce.1 = (f32[1,8,512]{2,1,0:T(8,128)}, f32[8]{0:T(128)S(1)}) all-reduce(f32[1,8,512]{2,1,0:T(8,128)S(1)} %convolution_bitcast_fusion.3, f32[8]{0:T(128)} %fusion.164), channel_id=1, replica_groups=mesh['ep'=8,'seq'=32] {'seq'}, use_global_device_ids=true, to_apply=%region_4.5 | all-reduce | flops 4104 | bytes 32832 | tf_op jit(solution)/shard_map/psum | solution.py:52
  250.9 1.5 fusion.161
  260.4 1.4 fusion.191
  262.6 2.1 fusion.159
  264.7 2.0 fusion.94
  268.2 2.1 fusion.67
  272.8 4.7 collective-permute-start.3
  277.6 1.4 convolution_convert_fusion.1
  279.4 25.7 %fusion.96 = (bf16[704,512]{1,0:T(8,128)(2,1)S(1)}, f32[1,704,512]{2,1,0:T(8,128)S(1)}) fusion(f32[1,704,1024]{2,1,0:T(8,128)} %copy-done.3, f32[704]{0:T(1024)S(1)} %copy-done.15, bf16[1,704,512]{2,1,0:T(8,128)(2,1)} %copy-done.1, bf16[1,15,512]{2,1,0:T(8,128)(2,1)S(1)} %collective-permute-done.3, f32[512]{0:T(512)S(1)} %bitcast.173, f32[512]{0:T(512)S(1)} %bitcast.175, ...), kind=kLoop, calls=%fused_computation.235 | loop fusion | flops 67764224 | bytes 4422400 | tf_op jit(solution)/shard_map/concatenate | solution.py:89
  306.3 2.1 convolution_convert_fusion
  309.6 2.5 fusion.82
  312.1 1.7 fusion.84
  313.8 1.5 fusion.83
  315.3 179.8 %reduce-scatter.11.cloned.1.call-done = bf16[16,512]{1,0:T(8,128)(2,1)} async-done(((bf16[512,512]{1,0:T(8,128)(2,1)}), bf16[16,512]{1,0:T(8,128)(2,1)}) %reduce-scatter.11.cloned.1.call-update) | async-done | bytes 16400 | tf_op jit(solution)/shard_map/reduce_scatter | solution.py:97
  495.1 1.5 copy.28
  496.6 2.2 fusion.68
  498.9 213.7 %reduce-scatter.9.cloned.1.call-done = bf16[16,1024]{1,0:T(8,128)(2,1)} async-done(((bf16[512,1024]{1,0:T(8,128)(2,1)}), bf16[16,1024]{1,0:T(8,128)(2,1)}) %reduce-scatter.9.cloned.1.call-update) | async-done | bytes 32784 | tf_op jit(solution)/shard_map/reduce_scatter | solution.py:94
  712.6 1.6 copy.26
  714.3 1.4 convolution_multiply_fusion.2
  715.7 2.5 stack.127
  719.6 10.5 psum.44
  730.7 46.4 %all-reduce.5.cloned.1.call-done = bf16[512,512]{0,1:T(8,128)(2,1)} async-done(((bf16[512,512]{0,1:T(8,128)(2,1)}), bf16[512,512]{0,1:T(8,128)(2,1)}) %all-reduce.5.cloned.1.call-update) | async-done | bytes 524304 | tf_op jit(solution)/shard_map/psum | solution.py:111
  777.1 2.2 copy.21
  779.3 31.5 %reduce-scatter.15.cloned.1.call-done = bf16[64,16]{1,0:T(8,128)(2,1)} async-done(((bf16[512,16]{1,0:T(8,128)(2,1)}), bf16[64,16]{1,0:T(8,128)(2,1)}) %reduce-scatter.15.cloned.1.call-update) | async-done | bytes 2064
  812.2 33.1 %reduce-scatter.13.cloned.1.call-done = bf16[128,16]{1,0:T(8,128)(2,1)} async-done(((bf16[1024,16]{1,0:T(8,128)(2,1)}), bf16[128,16]{1,0:T(8,128)(2,1)}) %reduce-scatter.13.cloned.1.call-update) | async-done | bytes 4112
  846.7 244.4 %all-reduce.7.cloned.1.call-done = (f32[31,512]{1,0:T(8,128)}, f32[8,512]{1,0:T(8,128)}) async-done(((f32[31,512]{1,0:T(8,128)}, f32[8,512]{1,0:T(8,128)}), (f32[31,512]{1,0:T(8,128)}, f32[8,512]{1,0:T(8,128)})) %all-reduce.7.cloned.1.call-update) | async-done | bytes 79888 | tf_op jit(solution)/shard_map/psum | solution.py:109
  1091.2 1.5 copy.45
  (239 shorter events, 29.7 us)
Async XLA Ops:
  7.2 487.9 %reduce-scatter.11.cloned.1.call-start = ((), (), s32[]{:S(2)}) async-start(), calls=%async_computation.5 | async-start | bytes 540672 | tf_op jit(solution)/shard_map/reduce_scatter | solution.py:97
  12.4 6.7 copy-start.11
  14.0 6.1 collective-permute-start
  17.4 5.6 collective-permute-start.1
  18.8 13.9 %copy-start.22 = (f32[1,512]{1,0:T(1,128)}, f32[1,512]{1,0:T(1,128)S(1)}, u32[]{:S(2)}) copy-start(f32[1,512]{1,0:T(1,128)S(1)} %get-tuple-element.89) | copy-start | bytes 6148
  18.8 13.9 %copy-start.24 = (f32[1,512]{1,0:T(1,128)}, f32[1,512]{1,0:T(1,128)S(1)}, u32[]{:S(2)}) copy-start(f32[1,512]{1,0:T(1,128)S(1)} %get-tuple-element.90) | copy-start | bytes 6148
  18.8 13.9 %copy-start.26 = (f32[1,512]{1,0:T(1,128)}, f32[1,512]{1,0:T(1,128)S(1)}, u32[]{:S(2)}) copy-start(f32[1,512]{1,0:T(1,128)S(1)} %get-tuple-element.91) | copy-start | bytes 6148
  20.1 12.6 %copy-start.6 = (bf16[1,704,512]{2,1,0:T(8,128)(2,1)S(1)}, bf16[1,704,512]{2,1,0:T(8,128)(2,1)}, u32[]{:S(2)}) copy-start(bf16[1,704,512]{2,1,0:T(8,128)(2,1)} %param.9) | copy-start | bytes 2162692
  20.1 12.6 %copy-start.90 = (bf16[512,512]{1,0:T(8,128)(2,1)S(1)}, bf16[512,512]{1,0:T(8,128)(2,1)}, u32[]{:S(2)}) copy-start(bf16[512,512]{1,0:T(8,128)(2,1)} %param.13) | copy-start | bytes 1572868
  34.7 221.1 %copy-start.10 = (bf16[256,512]{1,0:T(8,128)(2,1)S(1)}, bf16[256,512]{1,0:T(8,128)(2,1)}, u32[]{:S(2)}) copy-start(bf16[256,512]{1,0:T(8,128)(2,1)} %param.16) | copy-start | bytes 786436
  250.0 11.7 %copy-start.12 = (f32[1,8,512]{2,1,0:T(8,128)S(1)}, f32[1,8,512]{2,1,0:T(8,128)}, u32[]{:S(2)}) copy-start(f32[1,8,512]{2,1,0:T(8,128)} %get-tuple-element.60) | copy-start | bytes 49156
  271.2 7.9 collective-permute-start.2
  272.5 6.6 copy-start.15
  272.5 6.6 copy-start.19
  272.5 6.6 copy-start.21
  272.5 6.6 copy-start.23
  272.6 6.6 copy-start.25
  272.6 6.6 copy-start.27
  272.6 6.6 copy-start.29
  272.6 6.6 copy-start.31
  272.6 6.6 copy-start.33
  272.6 6.6 copy-start.35
  272.6 6.6 copy-start.37
  272.8 6.3 collective-permute-start.3
  279.0 433.6 %reduce-scatter.9.cloned.1.call-start = ((), (), s32[]{:S(2)}) async-start(), calls=%async_computation.4 | async-start | bytes 1081344 | tf_op jit(solution)/shard_map/reduce_scatter | solution.py:94
  279.1 26.0 %copy-start.4 = (f32[1,704,1024]{2,1,0:T(8,128)S(1)}, f32[1,704,1024]{2,1,0:T(8,128)}, u32[]{:S(2)}) copy-start(f32[1,704,1024]{2,1,0:T(8,128)} %copy-done.3) | copy-start | bytes 8650756
  308.4 468.7 %all-reduce.5.cloned.1.call-start = ((), (), s32[]{:S(2)}) async-start(), calls=%async_computation.6 | async-start | bytes 1048576 | tf_op jit(solution)/shard_map/psum | solution.py:111
  309.5 501.3 %reduce-scatter.15.cloned.1.call-start = ((), (), s32[]{:S(2)}) async-start(), calls=%async_computation.8 | async-start | bytes 147456
  496.6 348.7 %reduce-scatter.13.cloned.1.call-start = ((), (), s32[]{:S(2)}) async-start(), calls=%async_computation.7 | async-start | bytes 294912
  498.9 219.4 %copy-start.84 = (f32[256]{0:T(256)S(1)}, f32[256]{0:T(256)}, u32[]{:S(2)}) copy-start(f32[256]{0:T(256)} %copy-done.83) | copy-start | bytes 3076
  498.9 219.4 %copy-start.87 = (f32[1,256]{1,0:T(1,128)S(1)}, f32[1,256]{1,0:T(1,128)}, u32[]{:S(2)}) copy-start(f32[1,256]{1,0:T(1,128)} %param.17) | copy-start | bytes 3076
  714.3 376.9 %all-reduce.7.cloned.1.call-start = ((), (), s32[]{:S(2)}) async-start(), calls=%async_computation.9 | async-start | bytes 163840 | tf_op jit(solution)/shard_map/psum | solution.py:109
  (70 other events, 296.1 us)
Sparse Core Ops, SparseCore 0:
  279.2 215.8 reduce-scatter.10
  500.0 212.6 reduce-scatter.8
  715.1 61.9 all-reduce.4
  779.5 31.3 reduce-scatter.14
  813.3 31.9 reduce-scatter.12
  851.3 239.8 all-reduce.6
where the time goes:
time: 1110 us; the launch traced here: 1100 us
  waiting for transfers between devices  752 us (68%)
  blocking collectives  224 us (20%)
  other arithmetic  55.3 us (5%)
  between operations  20.1 us (2%)
  matrix products  20 us (2%)
  local copies, waits for them, and re-layouts  19.4 us (2%)
    psum x1, waiting for transfers between devices, shards(): grad_kernel, grad_query = lax.psum((kernel_here, query_here), ('ep', 'seq'))  244 us
    reduce_scatter x1, waiting for transfers between devices, shards(): lax.psum_scatter(in_here.astype(jnp.bfloat16), 'seq', scatter_dimension=0...  214 us
    reduce_scatter x1, waiting for transfers between devices, shards(): lax.psum_scatter(out_here.astype(jnp.bfloat16), 'seq', scatter_dimension=...  180 us
    psum x1, blocking collectives, shards(): total, vec = lax.psum((jnp.sum(expo, axis=1), vec_here), 'seq')  138 us
    pmax x1, blocking collectives, shards(): top = lax.pmax(jnp.max(masked, axis=1), 'seq')  76.1 us
    unnamed x8, waiting for transfers between devices  64.6 us
    psum x1, waiting for transfers between devices, shards(): lax.psum(value_here.astype(jnp.bfloat16), 'ep').astype(jnp.float32)  46.4 us
    concatenate x2, other arithmetic, shards(): jnp.concatenate([dglu * sig, dglu * mixed[..., :width] * sig * (1.0 - sig...  26.3 us
  transfers between devices with their start and end apart: 10, of which 7 were waited for; matrix products, arithmetic and copies ran while one was open for 5% of the time, Pallas kernels for 0%

commit v1 on v0

v1 whole, which is shorter than its diff:
```python
import jax
import jax.numpy as jnp
from jax import lax
from jax.sharding import PartitionSpec as P


def pair(value):
    high = lax.reduce_precision(value, exponent_bits=8, mantissa_bits=7)
    return high.astype(jnp.bfloat16), (value - high).astype(jnp.bfloat16)


def to_all(value, axis):
    count = lax.axis_size(axis)
    return lax.all_to_all(jnp.broadcast_to(value[None], (count, *value.shape)), axis, 0, 0)


def shards(frames, lengths, w_in, kernel, w_out, pool_query, w_value, text_emb, teacher):
    hi = lax.Precision.HIGHEST
    n_ep, n_seq = lax.axis_size("ep"), lax.axis_size("seq")
    x = frames[0]
    n_rows, width = x.shape
    n_taps = kernel.shape[0]
    rim = n_taps // 2
    halo, side = 2 * (rim + 1), rim + 1
    n_heads = pool_query.shape[0]
    head_dim = width // n_heads
    n_cands = text_emb.shape[0]
    root_width = jnp.sqrt(jnp.float32(width))

    forward = [(i, i + 1) for i in range(n_seq - 1)]
    backward = [(target, source) for source, target in forward]
    low = lax.ppermute(x[n_rows - halo :], "seq", forward)
    high = lax.ppermute(x[:halo], "seq", backward)
    ext = jnp.concatenate([low, x, high], axis=0)
    offset = lax.axis_index("seq") * n_rows - halo
    positions = offset + jnp.arange(n_rows + 2 * halo, dtype=jnp.int32)
    valid = ((positions >= 0) & (positions < lengths[0]))[:, None]

    xf = ext.astype(jnp.float32)
    mean_val = jnp.mean(xf, axis=-1, keepdims=True)
    var_val = jnp.mean((xf - mean_val) ** 2, axis=-1, keepdims=True)
    normed = ((xf - mean_val) * lax.rsqrt(var_val + 1e-05)).astype(jnp.bfloat16)
    mixed = jnp.dot(normed, w_in, preferred_element_type=jnp.float32)
    sig = jax.nn.sigmoid(mixed[:, width:])
    glu = jnp.where(valid, mixed[:, :width] * sig, 0.0).astype(jnp.bfloat16)

    wide = n_rows + 2 * side
    conv = jnp.zeros((wide, width), jnp.float32)
    first = side - rim
    for k in range(n_taps):
        conv = conv + kernel[k] * glu[first + k : first + k + wide].astype(jnp.float32)
    sconv = jax.nn.sigmoid(conv)
    act = (conv * sconv).astype(jnp.bfloat16)
    resid = xf[side : side + wide] + jnp.dot(act, w_out, preferred_element_type=jnp.float32)
    queries = pool_query.astype(jnp.float32)
    scores = jnp.einsum("sd,hd->sh", resid, queries, precision=hi) / root_width
    valid_w = valid[side : side + wide]
    masked = jnp.where(valid_w, scores, -1e30)
    mid = slice(side, side + n_rows)
    top_here = jnp.max(masked[mid], axis=0)
    expo = jnp.where(valid_w[mid], jnp.exp(masked[mid] - top_here), 0.0)
    vec_here = jnp.einsum("sh,sd->hd", expo, resid[mid], precision=hi)
    total_here = jnp.sum(expo, axis=0)
    stats = jnp.zeros((n_heads, 128), jnp.float32).at[:, 0].set(top_here).at[:, 1].set(total_here)
    every = to_all(jnp.concatenate([vec_here, stats], axis=1), "seq")
    tops, totals, vecs = every[:, :, width], every[:, :, width + 1], every[:, :, :width]
    top = jnp.max(tops, axis=0)
    scale = jnp.exp(tops - top)
    total = jnp.sum(scale * totals, axis=0)
    vbar = jnp.sum(scale[..., None] * vecs, axis=0) / total[:, None]

    wvals = w_value.astype(jnp.float32).reshape(width, n_heads, head_dim)
    pooled = jnp.einsum("hd,dhk->hk", vbar, wvals, precision=hi).reshape(width)
    rms = jnp.sqrt(jnp.mean(pooled * pooled) + 1e-06)
    emb = pooled / rms
    texts = text_emb.astype(jnp.float32)
    score = jnp.einsum("d,cd->c", emb, texts, precision=hi) / root_width
    diff = score - teacher[0]
    loss_here = jnp.sum(diff * diff) / n_cands
    dscore = 2.0 * diff / n_cands
    demb = jnp.einsum("c,cd->d", dscore, texts, precision=hi) / root_width
    dpooled = (demb - emb * jnp.mean(demb * emb)) / rms
    dp3 = dpooled.reshape(n_heads, head_dim)
    dvbar = jnp.einsum("dhk,hk->hd", wvals, dp3, precision=hi)

    episode = jnp.concatenate(
        [vbar, dpooled[None], jnp.broadcast_to(loss_here, (1, width))], axis=0
    )
    episodes = to_all(episode, "ep")
    loss = jnp.sum(episodes[:, n_heads + 1, 0])
    grad_value = jnp.einsum(
        "ehd,ehk->dhk",
        episodes[:, :n_heads],
        episodes[:, n_heads].reshape(n_ep, n_heads, head_dim),
        precision=hi,
    ).reshape(width, width)

    probs = jnp.where(valid_w, jnp.exp(masked - top), 0.0) / total
    proj = jnp.einsum("sd,hd->sh", resid, dvbar, precision=hi)
    centre = jnp.sum(dvbar * vbar, axis=-1)
    dscores = probs * (proj - centre)
    query_here = jnp.einsum("sh,sd->hd", dscores[mid], resid[mid], precision=hi) / root_width
    dresid = (
        jnp.einsum("sh,hd->sd", probs, dvbar, precision=hi)
        + jnp.einsum("sh,hd->sd", dscores, queries, precision=hi) / root_width
    ).astype(jnp.bfloat16)
    out_here = jnp.einsum("sd,sf->df", act[mid], dresid[mid], preferred_element_type=jnp.float32)
    dact = jnp.einsum("sf,df->sd", dresid, w_out, preferred_element_type=jnp.float32)
    dconv = (dact * sconv * (1.0 + conv * (1.0 - sconv))).astype(jnp.bfloat16)
    dconv_f = dconv[mid].astype(jnp.float32)
    dglu = jnp.zeros((n_rows, width), jnp.float32)
    taps = []
    for k in range(n_taps):
        start = side + rim - k
        dglu = dglu + kernel[k] * dconv[start : start + n_rows].astype(jnp.float32)
        start = halo + k - rim
        taps.append(jnp.sum(glu[start : start + n_rows].astype(jnp.float32) * dconv_f, axis=0))
    inner = slice(halo, halo + n_rows)
    dglu = jnp.where(valid[inner], dglu, 0.0)
    sig_in, gate_in = sig[inner], mixed[inner, :width]
    dmixed = jnp.concatenate(
        [dglu * sig_in, dglu * gate_in * sig_in * (1.0 - sig_in)], axis=-1
    ).astype(jnp.bfloat16)
    in_here = jnp.einsum("sd,sf->df", normed[inner], dmixed, preferred_element_type=jnp.float32)

    cols = width // n_ep
    small = jnp.concatenate([*[t[None] for t in taps], query_here], axis=0)
    small_rows = -(-small.shape[0] // 16) * 16
    small = jnp.pad(small, ((0, small_rows - small.shape[0]), (0, 0)))
    small = small.reshape(small_rows, width // 128, 128).transpose(1, 0, 2)
    small = small.reshape(n_ep, -1, 128)
    rows = width // n_seq
    part_in = in_here.astype(jnp.bfloat16).reshape(width, n_ep, 2 * cols).transpose(1, 0, 2)
    part_out = (
        out_here.astype(jnp.bfloat16)
        .reshape(n_seq, 2, rows // 2, n_ep, cols)
        .transpose(3, 0, 2, 1, 4)
        .reshape(n_ep, width // 2, 2 * cols)
    )
    first_sum = jnp.sum(
        lax.all_to_all(
            jnp.concatenate([part_in, part_out, *pair(small)], axis=1), "ep", 0, 0
        ).astype(jnp.float32),
        axis=0,
    )
    n_small = small.shape[1]
    rows_in, rows_out, small_high, small_low = jnp.split(
        first_sum, [width, width + width // 2, width + width // 2 + n_small], axis=0
    )
    small_pair = jnp.concatenate(pair(small_high + small_low), axis=0)
    second_sum = jnp.sum(
        lax.all_to_all(
            jnp.concatenate(
                [
                    rows_in.astype(jnp.bfloat16).reshape(n_seq, rows, 2 * cols),
                    rows_out.astype(jnp.bfloat16).reshape(n_seq, rows // 2, 2 * cols),
                    jnp.broadcast_to(small_pair[None], (n_seq, *small_pair.shape)),
                ],
                axis=1,
            ),
            "seq",
            0,
            0,
        ).astype(jnp.float32),
        axis=0,
    )
    grad_in, grad_out, small_high, small_low = jnp.split(
        second_sum, [rows, rows + rows // 2, rows + rows // 2 + n_small], axis=0
    )
    grad_out = jnp.concatenate([grad_out[:, :cols], grad_out[:, cols:]], axis=0)
    small = to_all(small_high + small_low, "ep").reshape(width // 128, small_rows, 128)
    small = small.transpose(1, 0, 2).reshape(small_rows, width)
    grad_kernel, grad_query = small[:n_taps], small[n_taps : n_taps + n_heads]
    return (loss, grad_in, grad_out, grad_kernel, grad_query, grad_value)


def solution(mesh):
    return jax.shard_map(
        shards,
        mesh=mesh,
        in_specs=(P("ep", "seq", None), P("ep"), P(), P(), P(), P(), P(), P(), P("ep", None)),
        out_specs=(P(), P("seq", "ep"), P("seq", "ep"), P(), P(), P()),
        check_vma=False,
    )
```

time: 1110 us -> 197 us (0.18)
  waiting for transfers between devices: 752 us -> 61.8 us
  blocking collectives: 224 us -> 0 us
  starting transfers between devices: 10.9 us -> 37.8 us
  between operations: 20.1 us -> 4.35 us
    reduce_scatter x2 -> x0, waiting for transfers between devices: 394 us -> none  [the longest x1 214 us: shards(): lax.psum_scatter(in_here.astype(jnp.bfloat16), 'seq', scatter_dimension=0...]
    psum x2 -> x0, waiting for transfers between devices: 291 us -> none  [the longest x1 244 us: shards(): grad_kernel, grad_query = lax.psum((kernel_here, query_here), ('ep', 'seq'))]
    psum x2 -> x0, blocking collectives: 148 us -> none  [the longest x1 138 us: shards(): total, vec = lax.psum((jnp.sum(expo, axis=1), vec_here), 'seq')]
    pmax x1 -> x0, blocking collectives: 76.1 us -> none  [shards(): top = lax.pmax(jnp.max(masked, axis=1), 'seq')]
    unnamed x8 -> x0, waiting for transfers between devices: 64.6 us -> none
    all_to_all x0 -> x5, waiting for transfers between devices: none -> 61.8 us  [the longest x3 26 us: to_all(): lax.all_to_all(jnp.broadcast_to(value[None], (count, *value.shape)), axis...]
    all_to_all x0 -> x5, starting transfers between devices: none -> 33.2 us  [the longest x3 23.2 us: to_all(): lax.all_to_all(jnp.broadcast_to(value[None], (count, *value.shape)), axis...]
    concatenate x2 -> x6, other arithmetic: 26.3 us -> 2.84 us  [the longest x1 1.3 us: shards(): jnp.concatenate([part_in, part_out, *pair(small)], axis=1)]
  transfers between devices with their start and end apart: 10 -> 7, of which waited for: 7 -> 5; matrix products, arithmetic and copies ran while one was open for 5% -> 6% of each run, Pallas kernels for 0% -> 0%
where the time goes in v1:
time: 197 us; the launch traced here: 193 us
  waiting for transfers between devices  61.8 us (31%)
  other arithmetic  44.3 us (22%)
  starting transfers between devices  37.8 us (19%)
  local copies, waits for them, and re-layouts  27.7 us (14%)
  matrix products  17.4 us (9%)
  between operations  4.35 us (2%)
    all_to_all x3, waiting for transfers between devices, to_all(): lax.all_to_all(jnp.broadcast_to(value[None], (count, *value.shape)), axis...  26 us
    all_to_all x3, starting transfers between devices, to_all(): lax.all_to_all(jnp.broadcast_to(value[None], (count, *value.shape)), axis...  23.2 us
    all_to_all x1, waiting for transfers between devices, shards(): lax.all_to_all(jnp.concatenate([part_in, part_out, *pair(small)], axis=1)...  20.2 us
    all_to_all x1, waiting for transfers between devices, shards(): lax.all_to_all(jnp.concatenate([rows_in.astype(jnp.bfloat16).reshape(n_se...  15.6 us
    another operation x7, other arithmetic  12.1 us
    unnamed x125, local copies, waits for them, and re-layouts  10.4 us
    convert_element_type x1, other arithmetic, shards(): act = (conv * sconv).astype(jnp.bfloat16)  7.14 us
    reduce_sum x3, other arithmetic, shards(): jnp.sum(glu[start:start + n_rows].astype(jnp.float32) * dconv_f, axis=0)  6.2 us
  transfers between devices with their start and end apart: 7, of which 5 were waited for; matrix products, arithmetic and copies ran while one was open for 6% of the time, Pallas kernels for 0%

profile of v1, /device:TPU:8, one launch (start us, length us, event | category | flops | bytes accessed | tf_op | source)
XLA Modules:
  0.0 193.4 jit_solution(4294940272377048896)
XLA Ops:
  1.6 3.4 %collective-permute-start = (bf16[32,512]{1,0:T(8,128)(2,1)S(1)}, bf16[32,512]{1,0:T(8,128)(2,1)S(1)}, u32[]{:S(2)}, u32[]{:S(2)}) collective-permute-start(bf16[32,512]{1,0:T(8,128)(2,1)S(1)} %get-tuple-element.107), channel_id=1, source_target_pairs={{0,1},{1,2},{2,3},{3,4},{4,5},{5,6},{6,7},{7,8},{8,9},{9,10},{10,1... | collective-permute-start | bytes 98312 | tf_op jit(solution)/shard_map/ppermute | solution.py:32
  14.7 1.9 fusion.2
  17.0 7.1 %multiply_convert_fusion.2 = (bf16[736,512]{1,0:T(8,128)(2,1)S(1)}, f32[736,512]{1,0:T(8,128)}) fusion(bf16[768,512]{1,0:T(8,128)(2,1)S(1)} %get-tuple-element.102, f32[512]{0:T(512)S(1)} %bitcast.190, f32[512]{0:T(512)S(1)} %bitcast.192, f32[512]{0:T(512)S(1)} %bitcast.196, f32[512]{0:T(512)S(1)} %bitcast.198, f32[512]{0:T(512)S(1)} %bitcast.200, ...), kind=kLoop, calls=%fused_computation.46 | loop fusion | flops 36552704 | bytes 25688064 | tf_op jit(solution)/shard_map/convert_element_type | solution.py:53
  30.6 13.7 %all-to-all-start = ((f32[32,8,640]{2,1,0:T(8,128)}), f32[32,8,640]{2,1,0:T(8,128)}, u32[]{:S(2)}, u32[]{:S(2)}) async-start(f32[32,8,640]{2,1,0:T(8,128)} %broadcast_in_dim.194), calls=%async_computation | async-start | bytes 1310720 | tf_op jit(solution)/shard_map/all_to_all | solution.py:14
  44.3 2.1 %copy.84 = bf16[512,512]{0,1:T(8,128)(2,1)} copy(bf16[512,512]{1,0:T(8,128)(2,1)} %param.19) | data formatting | bytes 1048576 | tf_op args[6]
  46.4 17.3 %all-to-all-done = f32[32,8,640]{2,1,0:T(8,128)} async-done(((f32[32,8,640]{2,1,0:T(8,128)}), f32[32,8,640]{2,1,0:T(8,128)}, u32[]{:S(2)}, u32[]{:S(2)}) %all-to-all-start) | async-done | bytes 655392 | tf_op jit(solution)/shard_map/all_to_all | solution.py:14
  63.7 2.4 %fusion.100 = (f32[32,8,1]{2,1,0:T(8,128)}, f32[8]{0:T(128)}, f32[32,8,1]{2,1,0:T(8,128)S(1)}) fusion(f32[32,8,640]{2,1,0:T(8,128)} %all-to-all-done), kind=kLoop, calls=%fused_computation.193 | loop fusion | flops 248 | bytes 4128 | tf_op jit(solution)/shard_map/slice | solution.py:66
  66.1 1.6 copy.99
  71.5 1.7 fusion.128
  74.3 1.6 fusion.105
  78.5 1.3 multiply_reduce_fusion.3
  82.4 1.3 fusion.108
  85.8 2.4 %fusion.76 = f32[736,512]{1,0:T(8,128)S(1)} fusion(f32[8,1,512]{0,2,1:T(8,128)} %copy.96, f32[736,8]{0,1:T(8,128)S(1)} %fusion.67, f32[8]{0:T(128)S(1)} %fusion.89, f32[8]{0:T(128)S(1)} %copy-done.58, pred[736]{0:T(1024)(128)(4,1)S(1)} %copy-done.55), kind=kOutput, calls=%fused_computation.129 | convolution fusion | flops 36193536 | bytes 1548064 | tf_op jit(solution)/shard_map/sh,hd->sd/dot_general | solution.py:104
  88.2 1.4 fusion.66
  93.9 1.8 fusion.34
  95.7 1.8 fusion.51
  97.6 2.6 %fusion.43 = (f32[512]{0:T(512)S(1)}, f32[512]{0:T(512)S(1)}, f32[512]{0:T(512)S(1)}, f32[512]{0:T(512)S(1)}, f32[512]{0:T(512)S(1)}, /*index=5*/f32[512]{0:T(51...) fusion(bf16[768,512]{1,0:T(8,128)(2,1)S(1)} %get-tuple-element., ...), kind=kLoop, calls=%fused_computation.88 | loop fusion | flops 14411264 | bytes 10119168 | tf_op jit(solution)/shard_map/reduce_sum | solution.py:117
  100.5 1.5 reshape.164
  102.2 3.3 %copy.87 = bf16[8,32,8,2,64]{4,3,2,1,0:T(2,128)(2,1)} copy(bf16[8,32,8,2,64]{4,0,2,3,1:T(8,128)(2,1)} %bitcast.161) | data formatting | bytes 1048576 | tf_op jit(solution)/shard_map/transpose | solution.py:137
  105.5 2.4 %reshape.165 = bf16[8,256,128]{2,1,0:T(8,128)(2,1)S(1)} reshape(bf16[8,32,8,2,64]{4,3,2,1,0:T(2,128)(2,1)} %copy.87) | data formatting | bytes 1048576 | tf_op jit(solution)/shard_map/reshape | solution.py:138
  108.1 7.5 %multiply_convert_fusion.3 = (bf16[704,512]{1,0:T(8,128)(2,1)S(1)}, f32[704,512]{1,0:T(8,128)S(1)}) fusion(f32[768,512]{1,0:T(8,128)} %get-tuple-element.101, bf16[736,512]{1,0:T(8,128)(2,1)S(1)} %multiply_convert_fusion.1, f32[512]{0:T(512)S(1)} %bitcast.191, f32[512]{0:T(512)S(1)} %bitcast.193, f32[512]{0:T(512)S(1)} %bitcast.197, f32[512]{0:T(512)S(1)} %bitcast.199, ...), kind=kLoop, calls=%fused_computation.104 | loop fusion | flops 34242560 | bytes 26016448 | tf_op jit(solution)/shard_map/convert.2
  115.6 2.0 %fusion.54 = bf16[704,512]{1,0:T(8,128)(2,1)S(1)} fusion(f32[704,512]{1,0:T(8,128)S(1)} %get-tuple-element.98, f32[768,1024]{1,0:T(8,128)} %copy-done.1, f32[768,512]{1,0:T(8,128)S(1)} %copy-done.2), kind=kLoop, calls=%fused_computation.100 | loop fusion | flops 1802240 | bytes 5046272 | tf_op jit(solution)/shard_map/convert.3
  118.8 1.3 pad_maximum_fusion
  120.1 5.0 %all-to-all-start.2 = ((bf16[8,816,128]{2,1,0:T(8,128)(2,1)}), bf16[8,816,128]{2,1,0:T(8,128)(2,1)S(1)}, u32[]{:S(2)}, u32[]{:S(2)}) async-start(bf16[8,816,128]{2,1,0:T(8,128)(2,1)} %pad_maximum_fusion), calls=%async_computation.2 | async-start | bytes 3342336 | tf_op jit(solution)/shard_map/all_to_all | solution.py:141
  126.1 20.2 %all-to-all-done.2 = bf16[8,816,128]{2,1,0:T(8,128)(2,1)S(1)} async-done(((bf16[8,816,128]{2,1,0:T(8,128)(2,1)}), bf16[8,816,128]{2,1,0:T(8,128)(2,1)S(1)}, u32[]{:S(2)}, u32[]{:S(2)}) %all-to-all-start.2) | async-done | bytes 1671200 | tf_op jit(solution)/shard_map/all_to_all | solution.py:141
  147.1 4.8 %all-to-all-start.1 = ((f32[8,10,512]{2,1,0:T(8,128)}), f32[8,10,512]{2,1,0:T(8,128)S(1)}, u32[]{:S(2)}, u32[]{:S(2)}) async-start(f32[8,10,512]{2,1,0:T(8,128)} %broadcast_in_dim.197), calls=%async_computation.1 | async-start | bytes 524288 | tf_op jit(solution)/shard_map/all_to_all | solution.py:14
  153.1 4.9 %all-to-all-done.1 = f32[8,10,512]{2,1,0:T(8,128)S(1)} async-done(((f32[8,10,512]{2,1,0:T(8,128)}), f32[8,10,512]{2,1,0:T(8,128)S(1)}, u32[]{:S(2)}, u32[]{:S(2)}) %all-to-all-start.1) | async-done | bytes 163872 | tf_op jit(solution)/shard_map/all_to_all | solution.py:14
  158.0 5.0 %all-to-all-start.3 = ((bf16[32,72,128]{2,1,0:T(8,128)(2,1)}), bf16[32,72,128]{2,1,0:T(8,128)(2,1)S(1)}, u32[]{:S(2)}, u32[]{:S(2)}) async-start(bf16[32,72,128]{2,1,0:T(8,128)(2,1)} %pad_maximum_fusion.2), calls=%async_computation.3 | async-start | bytes 1179648 | tf_op jit(solution)/shard_map/all_to_all | solution.py:152
  164.1 1.3 copy.92
  166.0 15.6 %all-to-all-done.3 = bf16[32,72,128]{2,1,0:T(8,128)(2,1)S(1)} async-done(((bf16[32,72,128]{2,1,0:T(8,128)(2,1)}), bf16[32,72,128]{2,1,0:T(8,128)(2,1)S(1)}, u32[]{:S(2)}, u32[]{:S(2)}) %all-to-all-start.3) | async-done | bytes 589856 | tf_op jit(solution)/shard_map/all_to_all | solution.py:152
  183.0 4.7 %all-to-all-start.4 = ((f32[8,24,128]{2,1,0:T(8,128)}), f32[8,24,128]{2,1,0:T(8,128)S(1)}, u32[]{:S(2)}, u32[]{:S(2)}) async-start(f32[8,24,128]{2,1,0:T(8,128)} %broadcast_in_dim.233), calls=%async_computation.4 | async-start | bytes 196608 | tf_op jit(solution)/shard_map/all_to_all | solution.py:14
  188.3 3.8 %all-to-all-done.4 = f32[8,24,128]{2,1,0:T(8,128)S(1)} async-done(((f32[8,24,128]{2,1,0:T(8,128)}), f32[8,24,128]{2,1,0:T(8,128)S(1)}, u32[]{:S(2)}, u32[]{:S(2)}) %all-to-all-start.4) | async-done | bytes 98336 | tf_op jit(solution)/shard_map/all_to_all | solution.py:14
  (205 shorter events, 40.4 us)
Async XLA Ops:
  0.6 13.0 %copy-start = (bf16[512,1024]{1,0:T(8,128)(2,1)S(1)}, bf16[512,1024]{1,0:T(8,128)(2,1)}, u32[]{:S(2)}) copy-start(bf16[512,1024]{1,0:T(8,128)(2,1)} %param.15) | copy-start | bytes 3145732
  0.6 11.4 %copy-start.3 = (bf16[1,704,512]{2,1,0:T(8,128)(2,1)S(1)}, bf16[1,704,512]{2,1,0:T(8,128)(2,1)}, u32[]{:S(2)}) copy-start(bf16[1,704,512]{2,1,0:T(8,128)(2,1)} %param.13) | copy-start | bytes 2162692
  1.6 9.2 %collective-permute-start = (bf16[32,512]{1,0:T(8,128)(2,1)S(1)}, bf16[32,512]{1,0:T(8,128)(2,1)S(1)}, u32[]{:S(2)}, u32[]{:S(2)}) collective-permute-start(bf16[32,512]{1,0:T(8,128)(2,1)S(1)} %get-tuple-element.107), channel_id=1, source_target_pairs={{0,1},{1,2},{2,3},{3,4},{4,5},{5,6},{6,7},{7,8},{8,9},{9,10},{10,1... | collective-permute-start | bytes 98312 | tf_op jit(solution)/shard_map/ppermute | solution.py:32
  5.0 5.8 %collective-permute-start.1 = (bf16[32,512]{1,0:T(8,128)(2,1)S(1)}, bf16[32,512]{1,0:T(8,128)(2,1)S(1)}, u32[]{:S(2)}, u32[]{:S(2)}) collective-permute-start(bf16[32,512]{1,0:T(8,128)(2,1)S(1)} %get-tuple-element.108), channel_id=1, source_target_pairs={{1,0},{2,1},{3,2},{4,3},{5,4},{6,5},{7,6},{8,7},{9,8},{10,9},{11,1... | collective-permute-start | bytes 98312 | tf_op jit(solution)/shard_map/ppermute | solution.py:33
  7.3 9.5 %copy-start.14 = (f32[1,512]{1,0:T(1,128)}, f32[1,512]{1,0:T(1,128)S(1)}, u32[]{:S(2)}) copy-start(f32[1,512]{1,0:T(1,128)S(1)} %get-tuple-element.146) | copy-start | bytes 6148
  8.5 8.3 %copy-start.16 = (f32[1,512]{1,0:T(1,128)}, f32[1,512]{1,0:T(1,128)S(1)}, u32[]{:S(2)}) copy-start(f32[1,512]{1,0:T(1,128)S(1)} %get-tuple-element.116) | copy-start | bytes 6148
  8.5 8.3 %copy-start.18 = (f32[1,512]{1,0:T(1,128)}, f32[1,512]{1,0:T(1,128)S(1)}, u32[]{:S(2)}) copy-start(f32[1,512]{1,0:T(1,128)S(1)} %get-tuple-element.117) | copy-start | bytes 6148
  8.5 8.3 %copy-start.20 = (f32[1,512]{1,0:T(1,128)}, f32[1,512]{1,0:T(1,128)S(1)}, u32[]{:S(2)}) copy-start(f32[1,512]{1,0:T(1,128)S(1)} %get-tuple-element.118) | copy-start | bytes 6148
  8.5 8.3 %copy-start.22 = (f32[1,512]{1,0:T(1,128)}, f32[1,512]{1,0:T(1,128)S(1)}, u32[]{:S(2)}) copy-start(f32[1,512]{1,0:T(1,128)S(1)} %get-tuple-element.119) | copy-start | bytes 6148
  8.5 8.3 %copy-start.24 = (f32[1,512]{1,0:T(1,128)}, f32[1,512]{1,0:T(1,128)S(1)}, u32[]{:S(2)}) copy-start(f32[1,512]{1,0:T(1,128)S(1)} %get-tuple-element.120) | copy-start | bytes 6148
  8.5 8.3 %copy-start.26 = (f32[1,512]{1,0:T(1,128)}, f32[1,512]{1,0:T(1,128)S(1)}, u32[]{:S(2)}) copy-start(f32[1,512]{1,0:T(1,128)S(1)} %get-tuple-element.121) | copy-start | bytes 6148
  8.5 8.3 %copy-start.28 = (f32[1,512]{1,0:T(1,128)}, f32[1,512]{1,0:T(1,128)S(1)}, u32[]{:S(2)}) copy-start(f32[1,512]{1,0:T(1,128)S(1)} %get-tuple-element.122) | copy-start | bytes 6148
  8.5 8.3 %copy-start.30 = (f32[1,512]{1,0:T(1,128)}, f32[1,512]{1,0:T(1,128)S(1)}, u32[]{:S(2)}) copy-start(f32[1,512]{1,0:T(1,128)S(1)} %get-tuple-element.123) | copy-start | bytes 6148
  8.5 8.3 %copy-start.32 = (f32[1,512]{1,0:T(1,128)}, f32[1,512]{1,0:T(1,128)S(1)}, u32[]{:S(2)}) copy-start(f32[1,512]{1,0:T(1,128)S(1)} %get-tuple-element.124) | copy-start | bytes 6148
  8.6 8.3 %copy-start.34 = (f32[1,512]{1,0:T(1,128)}, f32[1,512]{1,0:T(1,128)S(1)}, u32[]{:S(2)}) copy-start(f32[1,512]{1,0:T(1,128)S(1)} %get-tuple-element.125) | copy-start | bytes 6148
  8.6 8.3 %copy-start.36 = (f32[1,512]{1,0:T(1,128)}, f32[1,512]{1,0:T(1,128)S(1)}, u32[]{:S(2)}) copy-start(f32[1,512]{1,0:T(1,128)S(1)} %get-tuple-element.126) | copy-start | bytes 6148
  8.6 8.3 %copy-start.38 = (f32[1,512]{1,0:T(1,128)}, f32[1,512]{1,0:T(1,128)S(1)}, u32[]{:S(2)}) copy-start(f32[1,512]{1,0:T(1,128)S(1)} %get-tuple-element.127) | copy-start | bytes 6148
  8.6 8.3 %copy-start.40 = (f32[1,512]{1,0:T(1,128)}, f32[1,512]{1,0:T(1,128)S(1)}, u32[]{:S(2)}) copy-start(f32[1,512]{1,0:T(1,128)S(1)} %get-tuple-element.128) | copy-start | bytes 6148
  8.6 8.3 %copy-start.42 = (f32[1,512]{1,0:T(1,128)}, f32[1,512]{1,0:T(1,128)S(1)}, u32[]{:S(2)}) copy-start(f32[1,512]{1,0:T(1,128)S(1)} %get-tuple-element.129) | copy-start | bytes 6148
  8.6 8.3 %copy-start.44 = (f32[1,512]{1,0:T(1,128)}, f32[1,512]{1,0:T(1,128)S(1)}, u32[]{:S(2)}) copy-start(f32[1,512]{1,0:T(1,128)S(1)} %get-tuple-element.130) | copy-start | bytes 6148
  8.6 8.3 %copy-start.46 = (f32[1,512]{1,0:T(1,128)}, f32[1,512]{1,0:T(1,128)S(1)}, u32[]{:S(2)}) copy-start(f32[1,512]{1,0:T(1,128)S(1)} %get-tuple-element.131) | copy-start | bytes 6148
  8.6 8.3 %copy-start.48 = (f32[1,512]{1,0:T(1,128)}, f32[1,512]{1,0:T(1,128)S(1)}, u32[]{:S(2)}) copy-start(f32[1,512]{1,0:T(1,128)S(1)} %get-tuple-element.132) | copy-start | bytes 6148
  8.6 8.3 %copy-start.50 = (f32[1,512]{1,0:T(1,128)}, f32[1,512]{1,0:T(1,128)S(1)}, u32[]{:S(2)}) copy-start(f32[1,512]{1,0:T(1,128)S(1)} %get-tuple-element.133) | copy-start | bytes 6148
  9.4 16.6 %copy-start.54 = (pred[736]{0:T(1024)(128)(4,1)}, pred[736]{0:T(1024)(128)(4,1)S(1)}, u32[]{:S(2)}) copy-start(pred[736]{0:T(1024)(128)(4,1)S(1)} %slice.530) | copy-start | bytes 2212
  9.5 17.9 %copy-start.56 = (pred[704]{0:T(1024)(128)(4,1)}, pred[704]{0:T(1024)(128)(4,1)S(1)}, u32[]{:S(2)}) copy-start(pred[704]{0:T(1024)(128)(4,1)S(1)} %slice.529) | copy-start | bytes 2116
  30.6 33.1 %all-to-all-start = ((f32[32,8,640]{2,1,0:T(8,128)}), f32[32,8,640]{2,1,0:T(8,128)}, u32[]{:S(2)}, u32[]{:S(2)}) async-start(f32[32,8,640]{2,1,0:T(8,128)} %broadcast_in_dim.194), calls=%async_computation | async-start | bytes 1310720 | tf_op jit(solution)/shard_map/all_to_all | solution.py:14
  73.2 12.6 %copy-start.55 = (pred[736]{0:T(1024)(128)(4,1)S(1)}, pred[736]{0:T(1024)(128)(4,1)}, u32[]{:S(2)}) copy-start(pred[736]{0:T(1024)(128)(4,1)} %copy-done.54) | copy-start | bytes 2212
  73.2 12.6 %copy-start.58 = (f32[8]{0:T(128)S(1)}, f32[8]{0:T(128)}, u32[]{:S(2)}) copy-start(f32[8]{0:T(128)} %get-tuple-element.110) | copy-start | bytes 100
  120.1 26.2 %all-to-all-start.2 = ((bf16[8,816,128]{2,1,0:T(8,128)(2,1)}), bf16[8,816,128]{2,1,0:T(8,128)(2,1)S(1)}, u32[]{:S(2)}, u32[]{:S(2)}) async-start(bf16[8,816,128]{2,1,0:T(8,128)(2,1)} %pad_maximum_fusion), calls=%async_computation.2 | async-start | bytes 3342336 | tf_op jit(solution)/shard_map/all_to_all | solution.py:141
  147.1 10.9 %all-to-all-start.1 = ((f32[8,10,512]{2,1,0:T(8,128)}), f32[8,10,512]{2,1,0:T(8,128)S(1)}, u32[]{:S(2)}, u32[]{:S(2)}) async-start(f32[8,10,512]{2,1,0:T(8,128)} %broadcast_in_dim.197), calls=%async_computation.1 | async-start | bytes 524288 | tf_op jit(solution)/shard_map/all_to_all | solution.py:14
  158.0 23.6 %all-to-all-start.3 = ((bf16[32,72,128]{2,1,0:T(8,128)(2,1)}), bf16[32,72,128]{2,1,0:T(8,128)(2,1)S(1)}, u32[]{:S(2)}, u32[]{:S(2)}) async-start(bf16[32,72,128]{2,1,0:T(8,128)(2,1)} %pad_maximum_fusion.2), calls=%async_computation.3 | async-start | bytes 1179648 | tf_op jit(solution)/shard_map/all_to_all | solution.py:152
  183.0 9.1 %all-to-all-start.4 = ((f32[8,24,128]{2,1,0:T(8,128)}), f32[8,24,128]{2,1,0:T(8,128)S(1)}, u32[]{:S(2)}, u32[]{:S(2)}) async-start(f32[8,24,128]{2,1,0:T(8,128)} %broadcast_in_dim.233), calls=%async_computation.4 | async-start | bytes 196608 | tf_op jit(solution)/shard_map/all_to_all | solution.py:14
  (34 other events, 162.5 us)

commit v2 on v0

v2 whole, which is shorter than its diff:
```python
import functools

import jax
import jax.numpy as jnp
from jax import lax
from jax.experimental import pallas as pl
from jax.experimental.pallas import tpu as pltpu
from jax.sharding import PartitionSpec as P

F32, BF16 = jnp.float32, jnp.bfloat16
NN = (((1,), (0,)), ((), ()))
NT = (((1,), (1,)), ((), ()))
TN = (((0,), (0,)), ((), ()))
LANES = 128
STEP = 32
SIDE = 16


def dot(a, b, dims=NN):
    return lax.dot_general(a, b, dims, preferred_element_type=F32)


def split3(value):
    high = value.astype(BF16)
    rest = value - high.astype(F32)
    mid = rest.astype(BF16)
    return high, mid, (rest - mid.astype(F32)).astype(BF16)


def stacked(value):
    return jnp.concatenate(split3(value), axis=0)


def folded(value, count=3, rows=8):
    total = value[0:rows]
    for i in range(1, count):
        total = total + value[i * rows : (i + 1) * rows]
    return total


def lane_groups(shape, pieces):
    group = lax.broadcasted_iota(jnp.int32, shape, 1) // 8
    out = jnp.zeros(shape, F32)
    for g, piece in enumerate(pieces):
        out = jnp.where(group == g, piece.astype(F32), out)
    return out.astype(BF16)


def across(column):
    lane = lax.broadcasted_iota(jnp.int32, (8, LANES), 1)
    head = lax.broadcasted_iota(jnp.int32, (8, LANES), 0)
    return jnp.sum(jnp.where(lane % 8 == head, column, 0.0), axis=0, keepdims=True)


def down(row):
    lane = lax.broadcasted_iota(jnp.int32, (8, LANES), 1)
    head = lax.broadcasted_iota(jnp.int32, (8, LANES), 0)
    return jnp.sum(jnp.where(lane == head, row, 0.0), axis=1, keepdims=True)


def gated(x, w_in, width):
    xf = x.astype(F32)
    centred = xf - jnp.mean(xf, axis=-1, keepdims=True)
    var = jnp.mean(centred * centred, axis=-1, keepdims=True)
    normed = (centred * lax.rsqrt(var + 1e-05)).astype(BF16)
    mixed = dot(normed, w_in)
    return normed, mixed[:, :width], jax.nn.sigmoid(mixed[:, width:])


def row_mask(first, rows, length):
    at = first + lax.broadcasted_iota(jnp.int32, (rows, 1), 0)
    return (at >= 0) & (at < length)


def project_kernel(place, x_ref, w_in_ref, normed_ref, sig_ref, slope_ref, glu_ref):
    rows, width = x_ref.shape
    chunk = rows // 4
    for i in range(4):
        part = pl.ds(i * chunk, chunk)
        normed, gate, sig = gated(x_ref[part, :], w_in_ref[...], width)
        valid = row_mask(place[0] + i * chunk, chunk, place[1])
        normed_ref[part, :] = normed
        sig_ref[part, :] = sig.astype(BF16)
        both = gate * sig
        slope_ref[part, :] = (both * (1.0 - sig)).astype(BF16)
        glu_ref[part, :] = jnp.where(valid, both, 0.0).astype(BF16)


def shifted(block):
    rows = block.shape[0]
    return [block if s == 0 else pltpu.roll(block, rows - s, 0) for s in range(8)]


def forward_kernel(
    place, low_ref, high_ref, x_ref, own_glu_ref, w_in_ref, taps_ref, w_out_ref, query_ref,
    glu_ref, act_ref, slope_ref, resid_ref, sums_ref, glu_f,
):
    rows, width = x_ref.shape
    wide = rows + 2 * SIDE
    n_taps = taps_ref.shape[0]
    halo = jnp.concatenate([low_ref[...], high_ref[...]], axis=0)
    unused, gate, sig = gated(halo, w_in_ref[...], width)
    both = gate * sig
    valid_low = row_mask(place[0] - STEP, STEP, place[1])
    valid_high = row_mask(place[0] + rows, STEP, place[1])
    low = jnp.where(valid_low, both[:STEP], 0.0).astype(BF16)
    high = jnp.where(valid_high, both[STEP:], 0.0).astype(BF16)
    glu_ref[0:STEP, :] = low
    glu_ref[STEP : STEP + rows, :] = own_glu_ref[...]
    glu_ref[STEP + rows :, :] = high
    glu_f[0:STEP, :] = low.astype(F32)
    glu_f[STEP : STEP + rows, :] = own_glu_ref[...].astype(F32)
    glu_f[STEP + rows :, :] = high.astype(F32)

    @pl.loop(0, wide // STEP)
    def _(i):
        start = pl.multiple_of(i * STEP, STEP)
        for c in range(width // LANES):
            cols = slice(c * LANES, (c + 1) * LANES)
            views = shifted(glu_f[pl.ds(start, 2 * STEP), cols])
            acc = jnp.zeros((STEP, LANES), F32)
            for k in range(n_taps):
                q, s = divmod(k + 1, 8)
                acc = acc + taps_ref[k : k + 1, cols] * views[s][8 * q : 8 * q + STEP]
            s = jax.nn.sigmoid(acc)
            act_ref[pl.ds(start, STEP), cols] = (acc * s).astype(BF16)
            slope_ref[pl.ds(start, STEP), cols] = (s * (1.0 + acc * (1.0 - s))).astype(BF16)

    w_out = w_out_ref[...]
    resid_ref[0:SIDE, :] = low_ref[STEP - SIDE :, :].astype(F32) + dot(act_ref[0:SIDE, :], w_out)
    resid_ref[SIDE + rows :, :] = high_ref[0:SIDE, :].astype(F32) + dot(
        act_ref[SIDE + rows :, :], w_out
    )
    queries = jnp.concatenate([query_ref[...]] * (LANES // 8), axis=0)
    root = jnp.sqrt(jnp.float32(width))
    parts = 2
    chunk = rows // parts
    scores = []
    for i in range(parts):
        own = pl.ds(SIDE + i * chunk, chunk)
        resid = x_ref[pl.ds(i * chunk, chunk), :].astype(F32) + dot(act_ref[own, :], w_out)
        resid_ref[own, :] = resid
        score = sum(dot(piece, queries, NT) for piece in split3(resid)) / root
        valid = row_mask(place[0] + i * chunk, chunk, place[1])
        scores.append(jnp.where(valid, score, -1e30))
    top = functools.reduce(
        jnp.maximum, [jnp.max(score, axis=0, keepdims=True) for score in scores]
    )
    total = jnp.zeros((1, LANES), F32)
    vec = jnp.zeros((LANES, width), F32)
    for i in range(parts):
        valid = row_mask(place[0] + i * chunk, chunk, place[1])
        expo = jnp.where(valid, jnp.exp(scores[i] - top), 0.0)
        total = total + jnp.sum(expo, axis=0, keepdims=True)
        weights = lane_groups(expo.shape, split3(expo))
        for piece in split3(resid_ref[pl.ds(SIDE + i * chunk, chunk), :]):
            vec = vec + dot(weights, piece, TN)
    lane = lax.broadcasted_iota(jnp.int32, (8, LANES), 1)
    sums = jnp.concatenate(
        [folded(vec), jnp.where(lane == 0, down(top), down(total))], axis=1
    )

    @pl.loop(0, sums_ref.shape[0])
    def _(i):
        sums_ref[i] = sums


def backward_kernel(
    place, sums_ref, w_value_ref, text_ref, teacher_ref, query_ref, resid_ref, act_ref, slope_ref,
    glu_ref, normed_ref, sig_ref, gate_slope_ref, w_out_ref, taps_ref,
    episode_ref, mine_ref, other_ref,
    dconv_f, glu_f, dresid_s, dmixed_s, in_s, tap_s, small_s,
):
    rows, width = normed_ref.shape
    wide = rows + 2 * SIDE
    n_taps = taps_ref.shape[0]
    n_cands = text_ref.shape[0]
    head_dim = width // 8
    root = jnp.sqrt(jnp.float32(width))

    stats = sums_ref[:, :, width:]
    tops, totals = stats[:, :, 0:1], stats[:, :, 1:2]
    top = jnp.max(tops, axis=0)
    scale = jnp.exp(tops - top[None])
    total = jnp.sum(scale * totals, axis=0)
    vbar = jnp.sum(scale * sums_ref[:, :, :width], axis=0) / total
    at = lax.broadcasted_iota(jnp.int32, (8, width), 1) // head_dim
    own_head = at == lax.broadcasted_iota(jnp.int32, (8, width), 0)
    w_value = w_value_ref[...]
    texts = text_ref[...]
    full = folded(dot(stacked(vbar), w_value))
    pooled = jnp.sum(jnp.where(own_head, full, 0.0), axis=0, keepdims=True)
    pooled = jnp.broadcast_to(pooled, (8, width))
    rms = jnp.sqrt(jnp.mean(pooled * pooled, axis=-1, keepdims=True) + 1e-06)
    emb = pooled / rms
    diff = folded(dot(stacked(emb), texts, NT)) / root - teacher_ref[...]
    loss = jnp.sum(diff * diff, axis=-1, keepdims=True) / n_cands
    demb = folded(dot(stacked(2.0 * diff / n_cands), texts)) / root
    dpooled = (demb - emb * jnp.mean(demb * emb, axis=-1, keepdims=True)) / rms
    dvbar = folded(dot(stacked(jnp.where(own_head, dpooled, 0.0)), w_value, NT))
    centre = jnp.sum(dvbar * vbar, axis=-1, keepdims=True)
    row = lax.broadcasted_iota(jnp.int32, (8, width), 0)
    episode_ref[0:8, :] = vbar
    episode_ref[8:16, :] = jnp.where(row == 0, dpooled, jnp.where(row == 1, loss, 0.0))

    top_l, total_l, centre_l = across(top), across(total), across(centre)
    query = query_ref[...]
    queries = jnp.concatenate([query] * (LANES // 8), axis=0)
    d_high, d_mid, d_low = split3(dvbar)
    many = lambda piece: jnp.concatenate([piece] * (LANES // 8), axis=0)
    dv_high, dv_mid, dv_low = many(d_high), many(d_mid), many(d_low)
    mixing = jnp.concatenate(
        [d_high, d_mid, d_high, d_mid, query, query, query, jnp.zeros((LANES - 56, width), BF16)],
        axis=0,
    )
    w_out = w_out_ref[...]
    parts = 2
    chunk = wide // parts
    grad_query = jnp.zeros((LANES, width), F32)
    for i in range(parts):
        here = pl.ds(i * chunk, chunk)
        r_high, r_mid, r_low = split3(resid_ref[here, :])
        score = (dot(r_high, queries, NT) + dot(r_mid, queries, NT) + dot(r_low, queries, NT)) / root
        valid = row_mask(place[0] - SIDE + i * chunk, chunk, place[1])
        probs = jnp.where(valid, jnp.exp(score - top_l), 0.0) / total_l
        proj = dot(r_high, dv_high, NT) + (dot(r_high, dv_mid, NT) + dot(r_mid, dv_high, NT))
        proj = proj + (
            dot(r_high, dv_low, NT) + dot(r_mid, dv_mid, NT) + dot(r_low, dv_high, NT)
        )
        dscores = probs * (proj - centre_l) / root
        p_high, p_mid, unused = split3(probs)
        s_pieces = split3(dscores)
        mixed = lane_groups(probs.shape, (p_high, p_high, p_mid, p_mid, *s_pieces))
        dresid = dot(mixed, mixing).astype(BF16)
        dresid_s[here, :] = dresid
        own = lax.broadcasted_iota(jnp.int32, (chunk, 1), 0) + i * chunk
        own = (own >= SIDE) & (own < SIDE + rows)
        weights = lane_groups(probs.shape, s_pieces)
        weights = jnp.where(own, weights.astype(F32), 0.0).astype(BF16)
        for piece in (r_high, r_mid, r_low):
            grad_query = grad_query + dot(weights, piece, TN)
        dact = dot(dresid, w_out, NT)
        dconv = (dact * slope_ref[here, :].astype(F32)).astype(BF16)
        dconv_f[here, :] = dconv.astype(F32)
    small_s[0:8, :] = folded(grad_query)

    glu_f[...] = glu_ref[...].astype(F32)
    tap_s[...] = jnp.zeros_like(tap_s)

    @pl.loop(0, rows // STEP)
    def _(i):
        start = pl.multiple_of(i * STEP, STEP)
        valid = row_mask(place[0] + start, STEP, place[1])
        for c in range(width // LANES):
            cols = slice(c * LANES, (c + 1) * LANES)
            views = shifted(dconv_f[pl.ds(start, 2 * STEP), cols])
            acc = jnp.zeros((STEP, LANES), F32)
            for k in range(n_taps):
                q, s = divmod(n_taps - k, 8)
                acc = acc + taps_ref[k : k + 1, cols] * views[s][8 * q : 8 * q + STEP]
            dglu = jnp.where(valid, acc, 0.0)
            here = pl.ds(start, STEP)
            dmixed_s[here, cols] = (dglu * sig_ref[here, cols].astype(F32)).astype(BF16)
            dmixed_s[here, slice(width + c * LANES, width + (c + 1) * LANES)] = (
                dglu * gate_slope_ref[here, cols].astype(F32)
            ).astype(BF16)
            own = views[0][SIDE : SIDE + STEP]
            views = shifted(glu_f[pl.ds(start + SIDE, 2 * STEP), cols])
            for k in range(n_taps):
                q, s = divmod(k + 1, 8)
                product = own * views[s][8 * q : 8 * q + STEP]
                tap_s[k, :, cols] += folded(product, STEP // 8)

    small_s[8 : 8 + n_taps, :] = jnp.sum(tap_s[...], axis=1)
    small_s[8 + n_taps :, :] = jnp.zeros((small_s.shape[0] - 8 - n_taps, width), F32)

    grad_out = dot(act_ref[SIDE : SIDE + rows, :], dresid_s[SIDE : SIDE + rows, :], TN)
    in_s[...] = dot(normed_ref[...], dmixed_s[...], TN).astype(BF16)
    core = place[2]
    halves = grad_out.reshape(width // 16, 2, 8, width)
    first, second = (halves[:, j].reshape(width // 2, width) for j in range(2))
    low_lane = lax.broadcasted_iota(jnp.int32, (width // 2, LANES), 1) < LANES // 2
    for y in range(width // LANES):
        a = first[:, y * LANES : (y + 1) * LANES]
        b = second[:, y * LANES : (y + 1) * LANES]
        even = jnp.where(low_lane, a, pltpu.roll(b, LANES // 2, 1))
        odd = jnp.where(low_lane, pltpu.roll(a, LANES // 2, 1), b)
        for ref, which, block in (
            (mine_ref, core, jnp.where(core == 0, even, odd)),
            (other_ref, 1 - core, jnp.where(core == 0, odd, even)),
        ):
            at = pl.multiple_of((2 * y + which) * LANES, LANES)
            ref[y, 0:width, :] = in_s[:, pl.ds(at, LANES)]
            ref[y, width : width + width // 2, :] = block.astype(BF16)
            half = small_s.shape[0] // 2
            share = small_s[pl.ds(pl.multiple_of(which * half, 8), half), y * LANES : (y + 1) * LANES]
            high = share.astype(BF16).astype(F32)
            ref[y, width + width // 2 :, :] = jnp.concatenate(
                [high, share - high], axis=0
            ).astype(BF16)


def pair(value, axis):
    high = lax.reduce_precision(value, exponent_bits=8, mantissa_bits=7)
    return jnp.concatenate([high, value - high], axis=axis).astype(BF16)


def call(kernel, outs, scratch, n_args, flops):
    vmem = pl.BlockSpec(memory_space=pltpu.VMEM)
    return pl.pallas_call(
        kernel,
        out_shape=outs,
        in_specs=[pl.BlockSpec(memory_space=pltpu.SMEM)] + [vmem] * n_args,
        out_specs=[vmem] * len(outs),
        scratch_shapes=scratch,
        compiler_params=pltpu.CompilerParams(vmem_limit_bytes=48 * 2**20),
        cost_estimate=pl.CostEstimate(flops=flops, bytes_accessed=8 * 2**20, transcendentals=2**20),
    )


def shards(frames, lengths, w_in, kernel, w_out, pool_query, w_value, text_emb, teacher):
    n_ep, n_seq = lax.axis_size("ep"), lax.axis_size("seq")
    x = frames[0]
    rows, width = x.shape
    n_taps, n_heads = kernel.shape[0], pool_query.shape[0]
    wide, whole = rows + 2 * SIDE, rows + 2 * STEP
    shape = jax.ShapeDtypeStruct

    forward = [(i, i + 1) for i in range(n_seq - 1)]
    backward = [(target, source) for source, target in forward]
    low = lax.ppermute(x[rows - STEP :], "seq", forward)
    high = lax.ppermute(x[:STEP], "seq", backward)
    core = lax.axis_index("ep") % 2
    place = jnp.stack([lax.axis_index("seq") * rows, lengths[0], core]).astype(jnp.int32)

    own = shape((rows, width), BF16)
    normed, sig, gate_slope, own_glu = call(project_kernel, [own] * 4, [], 2, 2 * rows * width * width * 2)(
        place, x, w_in
    )
    glu, act, slope, resid, sums = call(
        forward_kernel,
        [
            shape((whole, width), BF16),
            shape((wide, width), BF16),
            shape((wide, width), BF16),
            shape((wide, width), F32),
            shape((n_seq, n_heads, width + LANES), F32),
        ],
        [pltpu.VMEM((whole, width), F32)],
        8,
        2 * rows * width * width * 4,
    )(place, low, high, x, own_glu, w_in, kernel, w_out, pool_query)
    sums = lax.all_to_all(sums, "seq", 0, 0)

    small_rows = 48
    payload = shape((n_ep // 2, width + width // 2 + small_rows, LANES), BF16)
    episode, mine, other = call(
        backward_kernel,
        [shape((16, width), F32), payload, payload],
        [
            pltpu.VMEM((wide, width), F32),
            pltpu.VMEM((whole, width), F32),
            pltpu.VMEM((wide, width), BF16),
            pltpu.VMEM((rows, 2 * width), BF16),
            pltpu.VMEM((width, 2 * width), BF16),
            pltpu.VMEM((n_taps, 8, width), F32),
            pltpu.VMEM((small_rows, width), F32),
        ],
        14,
        2 * rows * width * width * 8,
    )(
        place, sums, w_value, text_emb, teacher, pool_query, resid, act, slope,
        glu, normed, sig, gate_slope, w_out, kernel,
    )

    half = small_rows // 2
    big = width + width // 2

    def packed(total):
        share = total[..., big : big + half, :] + total[..., big + half :, :]
        return total[..., :big, :].astype(BF16), pair(share, -2)

    got = lax.ppermute(other, "ep", [(i, i ^ 1) for i in range(n_ep)])
    total = mine.astype(F32) + got.astype(F32)
    groups = [[2 * y + c for y in range(n_ep // 2)] for c in range(2)]
    got = lax.all_to_all(
        jnp.concatenate(packed(total), axis=-2), "ep", 0, 0, axis_index_groups=groups
    )
    grads, share = packed(jnp.sum(got.astype(F32), axis=0))
    in_rows = width // n_seq
    out_rows = in_rows // 2
    got = lax.all_to_all(
        jnp.concatenate(
            [
                grads[:width].reshape(n_seq, in_rows, LANES),
                grads[width:].reshape(n_seq, out_rows, LANES),
                jnp.broadcast_to(share[None], (n_seq, *share.shape)),
            ],
            axis=1,
        ),
        "seq",
        0,
        0,
    )
    total = jnp.sum(got.astype(F32), axis=0)
    grad_in = total[:in_rows]
    grad_out = total[in_rows : in_rows + out_rows]
    grad_out = jnp.concatenate([grad_out[:, : LANES // 2], grad_out[:, LANES // 2 :]], axis=0)
    share = total[in_rows + out_rows :]
    share = share[:half] + share[half:]
    last = jnp.concatenate([share, episode.reshape(-1, LANES)], axis=0)
    last = lax.all_to_all(jnp.broadcast_to(last[None], (n_ep, *last.shape)), "ep", 0, 0)
    small = last[:, :half].reshape(width // LANES, small_rows, LANES)
    small = small.transpose(1, 0, 2).reshape(small_rows, width)
    grad_query, grad_kernel = small[:n_heads], small[n_heads : n_heads + n_taps]
    episodes = last[:, half:].reshape(n_ep, 16, width)
    loss = jnp.sum(episodes[:, n_heads + 1, 0])
    grad_value = jnp.einsum(
        "ehd,ehk->dhk",
        episodes[:, :n_heads],
        episodes[:, n_heads].reshape(n_ep, n_heads, width // n_heads),
        precision=lax.Precision.HIGHEST,
    ).reshape(width, width)
    return (loss, grad_in, grad_out, grad_kernel, grad_query, grad_value)


def solution(mesh):
    return jax.shard_map(
        shards,
        mesh=mesh,
        in_specs=(P("ep", "seq", None), P("ep"), P(), P(), P(), P(), P(), P(), P("ep", None)),
        out_specs=(P(), P("seq", "ep"), P("seq", "ep"), P(), P(), P()),
        check_vma=False,
    )
```

time: 1110 us -> 139 us (0.13)
  waiting for transfers between devices: 752 us -> 27.3 us
  blocking collectives: 224 us -> 49 us
  other arithmetic: 55.3 us -> 3.85 us
  Pallas kernels: 0 us -> 30.5 us
  matrix products: 20 us -> 1.01 us
  between operations: 20.1 us -> 1.56 us
  local copies, waits for them, and re-layouts: 19.4 us -> 7.6 us
    reduce_scatter x2 -> x0, waiting for transfers between devices: 394 us -> none  [the longest x1 214 us: shards(): lax.psum_scatter(in_here.astype(jnp.bfloat16), 'seq', scatter_dimension=0...]
    psum x2 -> x0, waiting for transfers between devices: 291 us -> none  [the longest x1 244 us: shards(): grad_kernel, grad_query = lax.psum((kernel_here, query_here), ('ep', 'seq'))]
    psum x2 -> x0, blocking collectives: 148 us -> none  [the longest x1 138 us: shards(): total, vec = lax.psum((jnp.sum(expo, axis=1), vec_here), 'seq')]
    pmax x1 -> x0, blocking collectives: 76.1 us -> none  [shards(): top = lax.pmax(jnp.max(masked, axis=1), 'seq')]
    unnamed x8 -> x0, waiting for transfers between devices: 64.6 us -> none
    all_to_all x0 -> x2, blocking collectives: none -> 49 us  [the longest x1 32.6 us: shards(): sums = lax.all_to_all(sums, 'seq', 0, 0)]
    pallas_call x0 -> x3, Pallas kernels: none -> 30.5 us  [the longest x1 18.1 us: shards(): call(backward_kernel, [shape((16, width), F32), payload, payload], [pltpu...]
    concatenate x2 -> x5, other arithmetic: 26.3 us -> 1.53 us  [the longest x1 0.86 us: shards(): jnp.concatenate([grads[:width].reshape(n_seq, in_rows, LANES), grads[widt...]
  transfers between devices with their start and end apart: 10 -> 5, of which waited for: 7 -> 3; matrix products, arithmetic and copies ran while one was open for 5% -> 1% of each run, Pallas kernels for 0% -> 1%
where the time goes in v2:
time: 139 us; the launch traced here: 136 us
  blocking collectives  49 us (35%)
  Pallas kernels  30.5 us (22%)
  waiting for transfers between devices  27.3 us (20%)
  starting transfers between devices  15.6 us (11%)
  local copies, waits for them, and re-layouts  7.6 us (5%)
  other arithmetic  3.85 us (3%)
  between operations  1.56 us (1%)
    all_to_all x1, blocking collectives, shards(): sums = lax.all_to_all(sums, 'seq', 0, 0)  32.6 us
    all_to_all x1, waiting for transfers between devices, shards(): lax.all_to_all(jnp.concatenate([grads[:width].reshape(n_seq, in_rows, LAN...  18.3 us
    pallas_call x1, Pallas kernels, shards(): call(backward_kernel, [shape((16, width), F32), payload, payload], [pltpu...  18.1 us
    all_to_all x1, blocking collectives, shards(): lax.all_to_all(jnp.concatenate(packed(total), axis=-2), 'ep', 0, 0, axis_...  16.4 us
    pallas_call x1, Pallas kernels, shards(): call(forward_kernel, [shape((whole, width), BF16), shape((wide, width), B...  10.3 us
    all_to_all x1, waiting for transfers between devices, shards(): lax.all_to_all(jnp.broadcast_to(last[None], (n_ep, *last.shape)), 'ep', 0...  6.49 us
    all_to_all x1, starting transfers between devices, shards(): lax.all_to_all(jnp.concatenate([grads[:width].reshape(n_seq, in_rows, LAN...  4.97 us
    all_to_all x1, starting transfers between devices, shards(): lax.all_to_all(jnp.broadcast_to(last[None], (n_ep, *last.shape)), 'ep', 0...  4.81 us
  transfers between devices with their start and end apart: 5, of which 3 were waited for; matrix products, arithmetic and copies ran while one was open for 1% of the time, Pallas kernels for 1%

profile of v2, /device:TPU:8, one launch (start us, length us, event | category | flops | bytes accessed | tf_op | source)
XLA Modules:
  0.0 136.4 jit_solution(15979288849243263242)
XLA Ops:
  0.7 0.8 slice_bitcast_fusion.1
  1.5 1.3 collective-permute-start.1
  2.8 4.5 %collective-permute-start = (bf16[32,512]{1,0:T(8,128)(2,1)S(1)}, bf16[32,512]{1,0:T(8,128)(2,1)S(1)}, u32[]{:S(2)}, u32[]{:S(2)}) collective-permute-start(bf16[32,512]{1,0:T(8,128)(2,1)S(1)} %get-tuple-element.57), channel_id=1, source_target_pairs={{0,1},{1,2},{2,3},{3,4},{4,5},{5,6},{6,7},{7,8},{8,9},{9,10},{10,1... | collective-permute-start | bytes 98312 | tf_op jit(solution)/shard_map/ppermute | solution.py:331
  8.0 0.1 pad_add_fusion.place
  8.0 1.1 copy-done
  9.2 1.2 copy-done.1
  10.4 2.0 %shard_map.136 = (bf16[704,512]{1,0:T(8,128)(2,1)S(1)}, bf16[704,512]{1,0:T(8,128)(2,1)S(1)}, bf16[704,512]{1,0:T(8,128)(2,1)S(1)}, bf16[704,512]{1,0:T(8,128)(2,1)S(1)}) custom-call(s32[3]{0:T(128)S(1)} %pad_add_fusion.place, bf16[704,512]{1,0:T(8,128)(2,1)S(1)} %bitcast.21, bf16[512,1024]{1,0:T(8,128)(2,1)S(1)} %copy-done.1), custom_call_target="tpu_custom_call" | custom-call | flops 738197504 | bytes 8388608 | tf_op jit(solution)/shard_map/pallas_call | solution.py:337
  12.5 10.3 %shard_map.137 = (bf16[768,512]{1,0:T(8,128)(2,1)S(1)}, bf16[736,512]{1,0:T(8,128)(2,1)S(1)}, bf16[736,512]{1,0:T(8,128)(2,1)S(1)}, f32[736,512]{1,0:T(8,128)}, f32[32,8,640]{2,1,0:T(8,128)S(1)}) custom-call(s32[3]{0:T(128)S(1)} %pad_add_fusion.place, bf16[32,512]{1,0:T(8,128)(2,1)S(1)} %collective-permute-done.low_ref, ...), custom_call_target="tpu_custom_call" | custom-call | flops 1476395008 | bytes 8388608 | tf_op jit(solution)/shard_map/pallas_call | solution.py:340
  22.8 32.6 %all_to_all.20.sums_ref = f32[32,8,640]{2,1,0:T(8,128)S(1)} all-to-all(f32[32,8,640]{2,1,0:T(8,128)S(1)} %get-tuple-element.19), channel_id=1, replica_groups=mesh['ep'=8,'seq'=32] {'seq'}, dimensions={0} | all-to-all | bytes 1310720 | tf_op jit(solution)/shard_map/all_to_all | solution.py:353
  55.5 18.1 %shard_map.138 = (f32[16,512]{1,0:T(8,128)S(1)}, bf16[4,816,128]{2,1,0:T(8,128)(2,1)}, bf16[4,816,128]{2,1,0:T(8,128)(2,1)}) custom-call(s32[3]{0:T(128)S(1)} %pad_add_fusion.place, f32[32,8,640]{2,1,0:T(8,128)S(1)} %all_to_all.20.sums_ref, bf16[512,512]{1,0:T(8,128)(2,1)S(1)} %copy-done.3, bf16[256,512]{1,0:T(8,128)(2,1)S(1)} %copy-done.4, ...), custom_call_target="tpu_custom_call" | custom-call | flops 2952790016 | bytes 8388608 | tf_op jit(solution)/shard_map/pallas_call | solution.py:357
  73.6 2.6 %collective-permute-done.2 = bf16[4,816,128]{2,1,0:T(8,128)(2,1)S(1)} collective-permute-done((bf16[4,816,128]{2,1,0:T(8,128)(2,1)}, bf16[4,816,128]{2,1,0:T(8,128)(2,1)S(1)}, u32[]{:S(2)}, u32[]{:S(2)}) %collective-permute-start.2) | collective-permute-done | bytes 835616 | tf_op jit(solution)/shard_map/ppermute | solution.py:383
  76.2 1.4 %convert_add_fusion = f32[4,816,128]{2,1,0:T(8,128)S(1)} fusion(bf16[4,816,128]{2,1,0:T(8,128)(2,1)S(1)} %collective-permute-done.2, bf16[4,816,128]{2,1,0:T(8,128)(2,1)} %get-tuple-element.27), kind=kLoop, calls=%fused_computation.1 | loop fusion | flops 1253376 | bytes 3342336 | tf_op jit(solution)/shard_map/add | solution.py:384
  77.6 0.1 slice.159
  77.7 0.1 pad_maximum_fusion
  77.7 16.4 %all_to_all.21 = bf16[4,816,128]{2,1,0:T(8,128)(2,1)S(1)} all-to-all(bf16[4,816,128]{2,1,0:T(8,128)(2,1)S(1)} %pad_maximum_fusion), channel_id=1, replica_groups={{0,64,128,192},{32,96,160,224},{1,65,129,193},{33,97,161,225},{2,66,130..., dimensions={0} | all-to-all | bytes 1671168 | tf_op jit(solution)/shard_map/all_to_all | solution.py:386
  94.1 0.1 convert_reduce_fusion
  94.4 0.9 pad_maximum_fusion.1
  95.2 5.0 %all-to-all-start.2 = ((bf16[32,72,128]{2,1,0:T(8,128)(2,1)}), bf16[32,72,128]{2,1,0:T(8,128)(2,1)S(1)}, u32[]{:S(2)}, u32[]{:S(2)}) async-start(bf16[32,72,128]{2,1,0:T(8,128)(2,1)} %pad_maximum_fusion.1), calls=%async_computation.2 | async-start | bytes 1179648 | tf_op jit(solution)/shard_map/all_to_all | solution.py:392
  100.2 18.3 %all-to-all-done.2 = bf16[32,72,128]{2,1,0:T(8,128)(2,1)S(1)} async-done(((bf16[32,72,128]{2,1,0:T(8,128)(2,1)}), bf16[32,72,128]{2,1,0:T(8,128)(2,1)S(1)}, u32[]{:S(2)}, u32[]{:S(2)}) %all-to-all-start.2) | async-done | bytes 589856 | tf_op jit(solution)/shard_map/all_to_all | solution.py:392
  118.5 0.1 convert_reduce_fusion.1
  118.6 0.6 slice.122
  119.2 0.8 broadcast_in_dim.5
  119.9 4.8 %all-to-all-start.3 = ((f32[8,88,128]{2,1,0:T(8,128)}), f32[8,88,128]{2,1,0:T(8,128)S(1)}, u32[]{:S(2)}, u32[]{:S(2)}) async-start(f32[8,88,128]{2,1,0:T(8,128)} %broadcast_in_dim.5), calls=%async_computation.3 | async-start | bytes 720896 | tf_op jit(solution)/shard_map/all_to_all | solution.py:412
  124.7 0.1 fusion.5
  124.8 0.6 pad_maximum_fusion.4
  125.4 6.5 %all-to-all-done.3 = f32[8,88,128]{2,1,0:T(8,128)S(1)} async-done(((f32[8,88,128]{2,1,0:T(8,128)}), f32[8,88,128]{2,1,0:T(8,128)S(1)}, u32[]{:S(2)}, u32[]{:S(2)}) %all-to-all-start.3) | async-done | bytes 360480 | tf_op jit(solution)/shard_map/all_to_all | solution.py:412
  131.9 0.6 slice_bitcast_fusion.3
  132.6 0.6 slice_reduce_fusion.1
  133.3 0.6 copy.30
  134.0 0.1 reshape_squeeze.3
  134.1 1.0 fusion
  135.1 1.3 copy.28
  (37 shorter events, 0.4 us)
Async XLA Ops:
  0.6 11.8 %copy-start.6 = (bf16[8,512]{1,0:T(8,128)(2,1)S(1)}, bf16[8,512]{1,0:T(8,128)(2,1)}, u32[]{:S(2)}) copy-start(bf16[8,512]{1,0:T(8,128)(2,1)} %query_ref.3) | copy-start | bytes 24580
  0.6 11.8 %copy-start.5 = (f32[31,512]{1,0:T(8,128)S(1)}, f32[31,512]{1,0:T(8,128)}, u32[]{:S(2)}) copy-start(f32[31,512]{1,0:T(8,128)} %taps_ref.3) | copy-start | bytes 190468
  1.5 10.9 %collective-permute-start.1 = (bf16[32,512]{1,0:T(8,128)(2,1)S(1)}, bf16[32,512]{1,0:T(8,128)(2,1)S(1)}, u32[]{:S(2)}, u32[]{:S(2)}) collective-permute-start(bf16[32,512]{1,0:T(8,128)(2,1)S(1)} %get-tuple-element.56), channel_id=1, source_target_pairs={{1,0},{2,1},{3,2},{4,3},{5,4},{6,5},{7,6},{8,7},{9,8},{10,9},{11,1... | collective-permute-start | bytes 98312 | tf_op jit(solution)/shard_map/ppermute | solution.py:332
  2.8 9.7 %collective-permute-start = (bf16[32,512]{1,0:T(8,128)(2,1)S(1)}, bf16[32,512]{1,0:T(8,128)(2,1)S(1)}, u32[]{:S(2)}, u32[]{:S(2)}) collective-permute-start(bf16[32,512]{1,0:T(8,128)(2,1)S(1)} %get-tuple-element.57), channel_id=1, source_target_pairs={{0,1},{1,2},{2,3},{3,4},{4,5},{5,6},{6,7},{7,8},{8,9},{9,10},{10,1... | collective-permute-start | bytes 98312 | tf_op jit(solution)/shard_map/ppermute | solution.py:331
  8.0 1.1 copy-start
  9.2 1.2 copy-start.1
  10.4 2.1 %copy-start.2 = (bf16[512,512]{1,0:T(8,128)(2,1)S(1)}, bf16[512,512]{1,0:T(8,128)(2,1)}, u32[]{:S(2)}) copy-start(bf16[512,512]{1,0:T(8,128)(2,1)} %w_out_ref.3) | copy-start | bytes 1572868
  12.4 43.0 %copy-start.3 = (bf16[512,512]{1,0:T(8,128)(2,1)S(1)}, bf16[512,512]{1,0:T(8,128)(2,1)}, u32[]{:S(2)}) copy-start(bf16[512,512]{1,0:T(8,128)(2,1)} %w_value_ref.1) | copy-start | bytes 1572868
  12.5 43.0 %copy-start.4 = (bf16[256,512]{1,0:T(8,128)(2,1)S(1)}, bf16[256,512]{1,0:T(8,128)(2,1)}, u32[]{:S(2)}) copy-start(bf16[256,512]{1,0:T(8,128)(2,1)} %text_ref.1) | copy-start | bytes 786436
  12.5 43.0 %copy-start.7 = (f32[1,256]{1,0:T(1,128)S(1)}, f32[1,256]{1,0:T(1,128)}, u32[]{:S(2)}) copy-start(f32[1,256]{1,0:T(1,128)} %teacher_ref.1) | copy-start | bytes 3076
  22.8 32.6 %copy-start.8 = (bf16[768,512]{1,0:T(8,128)(2,1)}, bf16[768,512]{1,0:T(8,128)(2,1)S(1)}, u32[]{:S(2)}) copy-start(bf16[768,512]{1,0:T(8,128)(2,1)S(1)} %get-tuple-element.23.glu_ref) | copy-start | bytes 2359300
  73.6 2.6 %collective-permute-start.2 = (bf16[4,816,128]{2,1,0:T(8,128)(2,1)}, bf16[4,816,128]{2,1,0:T(8,128)(2,1)S(1)}, u32[]{:S(2)}, u32[]{:S(2)}) collective-permute-start(bf16[4,816,128]{2,1,0:T(8,128)(2,1)} %get-tuple-element.28), channel_id=1, source_target_pairs={{0,32},{32,0},{64,96},{96,64},{128,160},{160,128},{192,224},{224,1... | collective-permute-start | bytes 2506760 | tf_op jit(solution)/shard_map/ppermute | solution.py:383
  95.2 23.2 %all-to-all-start.2 = ((bf16[32,72,128]{2,1,0:T(8,128)(2,1)}), bf16[32,72,128]{2,1,0:T(8,128)(2,1)S(1)}, u32[]{:S(2)}, u32[]{:S(2)}) async-start(bf16[32,72,128]{2,1,0:T(8,128)(2,1)} %pad_maximum_fusion.1), calls=%async_computation.2 | async-start | bytes 1179648 | tf_op jit(solution)/shard_map/all_to_all | solution.py:392
  119.9 12.0 %all-to-all-start.3 = ((f32[8,88,128]{2,1,0:T(8,128)}), f32[8,88,128]{2,1,0:T(8,128)S(1)}, u32[]{:S(2)}, u32[]{:S(2)}) async-start(f32[8,88,128]{2,1,0:T(8,128)} %broadcast_in_dim.5), calls=%async_computation.3 | async-start | bytes 720896 | tf_op jit(solution)/shard_map/all_to_all | solution.py:412

commit v3 on v2

--- a/solution.py
+++ b/solution.py
@@ -168,7 +168,7 @@
 def backward_kernel(
     place, sums_ref, w_value_ref, text_ref, teacher_ref, query_ref, resid_ref, act_ref, slope_ref,
     glu_ref, normed_ref, sig_ref, gate_slope_ref, w_out_ref, taps_ref,
-    episode_ref, mine_ref, other_ref,
+    mine_ref, other_ref,
     dconv_f, glu_f, dresid_s, dmixed_s, in_s, tap_s, small_s,
 ):
     rows, width = normed_ref.shape
@@ -200,8 +200,12 @@
     dvbar = folded(dot(stacked(jnp.where(own_head, dpooled, 0.0)), w_value, NT))
     centre = jnp.sum(dvbar * vbar, axis=-1, keepdims=True)
     row = lax.broadcasted_iota(jnp.int32, (8, width), 0)
-    episode_ref[0:8, :] = vbar
-    episode_ref[8:16, :] = jnp.where(row == 0, dpooled, jnp.where(row == 1, loss, 0.0))
+    loss_high = loss.astype(BF16).astype(F32)
+    rest = jnp.where(row == 4, loss_high, jnp.where(row == 5, loss - loss_high, 0.0))[:, :LANES]
+    blocks = [slice(c * LANES, (c + 1) * LANES) for c in range(width // LANES)]
+    for c, cols in enumerate(blocks):
+        rest = jnp.where(row[:, :LANES] == c, dpooled[:, cols], rest)
+    episode = jnp.concatenate([*[vbar[:, cols] for cols in blocks], rest], axis=0)
 
     top_l, total_l, centre_l = across(top), across(total), across(centre)
     query = query_ref[...]
@@ -242,7 +246,11 @@
         dact = dot(dresid, w_out, NT)
         dconv = (dact * slope_ref[here, :].astype(F32)).astype(BF16)
         dconv_f[here, :] = dconv.astype(F32)
-    small_s[0:8, :] = folded(grad_query)
+    query_sum = folded(grad_query)
+    high = query_sum.astype(BF16).astype(F32)
+    half = small_s.shape[0] // 2
+    small_s[0:8, :] = jnp.where(row < 4, high, pltpu.roll(query_sum - high, 4, 0))
+    small_s[half : half + 8, :] = jnp.where(row < 4, pltpu.roll(high, 4, 0), query_sum - high)
 
     glu_f[...] = glu_ref[...].astype(F32)
     tap_s[...] = jnp.zeros_like(tap_s)
@@ -271,8 +279,9 @@
                 product = own * views[s][8 * q : 8 * q + STEP]
                 tap_s[k, :, cols] += folded(product, STEP // 8)
 
-    small_s[8 : 8 + n_taps, :] = jnp.sum(tap_s[...], axis=1)
-    small_s[8 + n_taps :, :] = jnp.zeros((small_s.shape[0] - 8 - n_taps, width), F32)
+    tap_sum = jnp.sum(tap_s[...], axis=1)
+    small_s[8:half, :] = tap_sum[: half - 8]
+    small_s[half + 8 :, :] = tap_sum[half - 8 :]
 
     grad_out = dot(act_ref[SIDE : SIDE + rows, :], dresid_s[SIDE : SIDE + rows, :], TN)
     in_s[...] = dot(normed_ref[...], dmixed_s[...], TN).astype(BF16)
@@ -292,25 +301,105 @@
             at = pl.multiple_of((2 * y + which) * LANES, LANES)
             ref[y, 0:width, :] = in_s[:, pl.ds(at, LANES)]
             ref[y, width : width + width // 2, :] = block.astype(BF16)
-            half = small_s.shape[0] // 2
             share = small_s[pl.ds(pl.multiple_of(which * half, 8), half), y * LANES : (y + 1) * LANES]
-            high = share.astype(BF16).astype(F32)
-            ref[y, width + width // 2 :, :] = jnp.concatenate(
-                [high, share - high], axis=0
-            ).astype(BF16)
-
-
-def pair(value, axis):
-    high = lax.reduce_precision(value, exponent_bits=8, mantissa_bits=7)
-    return jnp.concatenate([high, value - high], axis=axis).astype(BF16)
-
-
-def call(kernel, outs, scratch, n_args, flops):
+            ref[y, width + width // 2 :, :] = jnp.concatenate([share, episode], axis=0).astype(BF16)
+
+
+def paired(rows):
+    row = lax.broadcasted_iota(jnp.int32, rows.shape, 0)
+    value = rows + pltpu.roll(rows, 4, 0)
+    high = value.astype(BF16).astype(F32)
+    return jnp.where(row < 4, high, value - high)
+
+
+def cores_kernel(big, half, mine_ref, got_ref, out_ref):
+    for y in range(mine_ref.shape[0]):
+        total = mine_ref[y, 0:big, :].astype(F32) + got_ref[y, 0:big, :].astype(F32)
+        out_ref[y, 0:big, :] = total.astype(BF16)
+        mine, got = mine_ref[y, big:, :].astype(F32), got_ref[y, big:, :].astype(F32)
+        share = mine[:half] + got[:half]
+        out_ref[y, big:, :] = jnp.concatenate(
+            [paired(share[:8]), share[8:], mine[half:], got[half:], jnp.zeros((8, LANES), F32)],
+            axis=0,
+        ).astype(BF16)
+
+
+def rows_kernel(big, half, got_ref, out_ref):
+    n_y, n_seq = got_ref.shape[0], out_ref.shape[0]
+    total = got_ref[0, 0:big, :].astype(F32)
+    share = got_ref[0, big:, :].astype(F32)[:half]
+    for y in range(1, n_y):
+        total = total + got_ref[y, 0:big, :].astype(F32)
+        share = share + got_ref[y, big:, :].astype(F32)[:half]
+    share = jnp.concatenate([paired(share[:8]), share[8:]], axis=0)
+    split = 2 * big // 3
+    out_ref[...] = jnp.concatenate(
+        [
+            total[:split].reshape(n_seq, split // n_seq, LANES),
+            total[split:].reshape(n_seq, (big - split) // n_seq, LANES),
+            jnp.broadcast_to(share[None], (n_seq, half, LANES)),
+        ],
+        axis=1,
+    ).astype(BF16)
+
+
+def value_kernel(big, half, got_ref, grad_ref, loss_ref):
+    width = grad_ref.shape[0]
+    head = lax.broadcasted_iota(jnp.int32, (8, width), 1) // (width // 8)
+    own_head = head == lax.broadcasted_iota(jnp.int32, (8, width), 0)
+    vectors, others = [], []
+    loss = jnp.zeros((1, LANES), F32)
+    n_blocks = width // LANES
+    size = 8 * (n_blocks + 1)
+    for y in range(got_ref.shape[0]):
+        rows = got_ref[y, big:, :].astype(F32)
+        for start in (half, half + size):
+            episode = rows[start : start + size]
+            rest = episode[8 * n_blocks :]
+            vectors.append(
+                jnp.concatenate([episode[8 * c : 8 * c + 8] for c in range(n_blocks)], axis=1)
+            )
+            dpooled = jnp.concatenate([rest[c : c + 1] for c in range(n_blocks)], axis=1)
+            others.append(jnp.where(own_head, dpooled, 0.0))
+            loss = loss + rest[4:5] + rest[5:6]
+    vectors, others = (jnp.concatenate(v, axis=0).astype(BF16) for v in (vectors, others))
+    grad_ref[...] = dot(vectors, others, TN)
+    loss_ref[...] = loss
+
+
+def owner_kernel(got_ref, grad_in_ref, grad_out_ref, out_ref):
+    total = got_ref[0].astype(F32)
+    for s in range(1, got_ref.shape[0]):
+        total = total + got_ref[s].astype(F32)
+    in_rows, cols = grad_in_ref.shape[0], grad_out_ref.shape[1]
+    out_rows = grad_out_ref.shape[0] // 2
+    grad_in_ref[...] = total[:in_rows]
+    pair_rows = total[in_rows : in_rows + out_rows]
+    grad_out_ref[0:out_rows, :] = pair_rows[:, :cols]
+    grad_out_ref[out_rows:, :] = pair_rows[:, cols:]
+    share = total[in_rows + out_rows :]
+    share = jnp.concatenate([share[:8] + pltpu.roll(share[:8], 4, 0), share[8:]], axis=0)
+    for e in range(out_ref.shape[0]):
+        out_ref[e] = share
+
+
+def last_kernel(got_ref, taps_ref, query_ref):
+    n_taps = taps_ref.shape[0]
+    for y in range(got_ref.shape[0] // 2):
+        cols = slice(y * LANES, (y + 1) * LANES)
+        first, second = got_ref[2 * y], got_ref[2 * y + 1]
+        row = lax.broadcasted_iota(jnp.int32, (8, LANES), 0)
+        query_ref[:, cols] = jnp.where(row < 4, first[:8], second[:8])
+        taps_ref[0:16, cols] = first[8:]
+        taps_ref[16:n_taps, cols] = second[8 : 8 + n_taps - 16]
+
+
+def call(kernel, outs, scratch, n_args, flops, placed=True):
     vmem = pl.BlockSpec(memory_space=pltpu.VMEM)
     return pl.pallas_call(
         kernel,
         out_shape=outs,
-        in_specs=[pl.BlockSpec(memory_space=pltpu.SMEM)] + [vmem] * n_args,
+        in_specs=[pl.BlockSpec(memory_space=pltpu.SMEM)] * placed + [vmem] * n_args,
         out_specs=[vmem] * len(outs),
         scratch_shapes=scratch,
         compiler_params=pltpu.CompilerParams(vmem_limit_bytes=48 * 2**20),
@@ -353,17 +442,21 @@
     sums = lax.all_to_all(sums, "seq", 0, 0)
 
     small_rows = 48
-    payload = shape((n_ep // 2, width + width // 2 + small_rows, LANES), BF16)
-    episode, mine, other = call(
+    half = small_rows // 2
+    big = width + width // 2
+    n_y = n_ep // 2
+    size = 8 * (width // LANES + 1)
+    payload = shape((n_y, big + half + size, LANES), BF16)
+    mine, other = call(
         backward_kernel,
-        [shape((16, width), F32), payload, payload],
+        [payload, payload],
         [
             pltpu.VMEM((wide, width), F32),
             pltpu.VMEM((whole, width), F32),
             pltpu.VMEM((wide, width), BF16),
             pltpu.VMEM((rows, 2 * width), BF16),
             pltpu.VMEM((width, 2 * width), BF16),
-            pltpu.VMEM((n_taps, 8, width), F32),
+            pltpu.VMEM((n_taps + 1, 8, width), F32),
             pltpu.VMEM((small_rows, width), F32),
         ],
         14,
@@ -373,54 +466,40 @@
         glu, normed, sig, gate_slope, w_out, kernel,
     )
 
-    half = small_rows // 2
-    big = width + width // 2
-
-    def packed(total):
-        share = total[..., big : big + half, :] + total[..., big + half :, :]
-        return total[..., :big, :].astype(BF16), pair(share, -2)
-
+    light = functools.partial(call, scratch=[], flops=2**20, placed=False)
     got = lax.ppermute(other, "ep", [(i, i ^ 1) for i in range(n_ep)])
-    total = mine.astype(F32) + got.astype(F32)
-    groups = [[2 * y + c for y in range(n_ep // 2)] for c in range(2)]
-    got = lax.all_to_all(
-        jnp.concatenate(packed(total), axis=-2), "ep", 0, 0, axis_index_groups=groups
-    )
-    grads, share = packed(jnp.sum(got.astype(F32), axis=0))
-    in_rows = width // n_seq
-    out_rows = in_rows // 2
-    got = lax.all_to_all(
-        jnp.concatenate(
-            [
-                grads[:width].reshape(n_seq, in_rows, LANES),
-                grads[width:].reshape(n_seq, out_rows, LANES),
-                jnp.broadcast_to(share[None], (n_seq, *share.shape)),
-            ],
-            axis=1,
-        ),
-        "seq",
-        0,
-        0,
-    )
-    total = jnp.sum(got.astype(F32), axis=0)
-    grad_in = total[:in_rows]
-    grad_out = total[in_rows : in_rows + out_rows]
-    grad_out = jnp.concatenate([grad_out[:, : LANES // 2], grad_out[:, LANES // 2 :]], axis=0)
-    share = total[in_rows + out_rows :]
-    share = share[:half] + share[half:]
-    last = jnp.concatenate([share, episode.reshape(-1, LANES)], axis=0)
-    last = lax.all_to_all(jnp.broadcast_to(last[None], (n_ep, *last.shape)), "ep", 0, 0)
-    small = last[:, :half].reshape(width // LANES, small_rows, LANES)
-    small = small.transpose(1, 0, 2).reshape(small_rows, width)
-    grad_query, grad_kernel = small[:n_heads], small[n_heads : n_heads + n_taps]
-    episodes = last[:, half:].reshape(n_ep, 16, width)
-    loss = jnp.sum(episodes[:, n_heads + 1, 0])
-    grad_value = jnp.einsum(
-        "ehd,ehk->dhk",
-        episodes[:, :n_heads],
-        episodes[:, n_heads].reshape(n_ep, n_heads, width // n_heads),
-        precision=lax.Precision.HIGHEST,
-    ).reshape(width, width)
+    (total,) = light(
+        functools.partial(cores_kernel, big, half),
+        [shape((n_y, big + half + 2 * size + 8, LANES), BF16)],
+        n_args=2,
+    )(mine, got)
+    groups = [[2 * y + c for y in range(n_y)] for c in range(2)]
+    got = lax.all_to_all(total, "ep", 0, 0, axis_index_groups=groups)
+    (total,) = light(
+        functools.partial(rows_kernel, big, half),
+        [shape((n_seq, big // n_seq + half, LANES), BF16)],
+        n_args=1,
+    )(got)
+    grad_value, loss = light(
+        functools.partial(value_kernel, big, half),
+        [shape((width, width), F32), shape((1, LANES), F32)],
+        n_args=1,
+    )(got)
+    loss = loss[0, 0]
+    got = lax.all_to_all(total, "seq", 0, 0)
+    grad_in, grad_out, share = light(
+        owner_kernel,
+        [
+            shape((width // n_seq, 2 * width // n_ep), F32),
+            shape((width // n_seq, width // n_ep), F32),
+            shape((n_ep, half, LANES), F32),
+        ],
+        n_args=1,
+    )(got)
+    got = lax.all_to_all(share, "ep", 0, 0)
+    grad_kernel, grad_query = light(
+        last_kernel, [shape((n_taps, width), F32), shape((n_heads, width), F32)], n_args=1
+    )(got)
     return (loss, grad_in, grad_out, grad_kernel, grad_query, grad_value)
 
 

time: 139 us -> 126 us (0.906)
  waiting for transfers between devices: 27.3 us -> 5.67 us
  blocking collectives: 49 us -> 68.6 us
  starting transfers between devices: 15.6 us -> 10.6 us
  other arithmetic: 3.85 us -> 0.08 us
  local copies, waits for them, and re-layouts: 7.6 us -> 4.34 us
  Pallas kernels: 30.5 us -> 33.5 us
    all_to_all x2 -> x1, waiting for transfers between devices: 24.7 us -> 3.07 us  [shards(): got = lax.all_to_all(share, 'ep', 0, 0)]
    all_to_all x1 -> x2, blocking collectives: 16.4 us -> 36 us  [the longest x1 18.9 us: shards(): got = lax.all_to_all(total, 'seq', 0, 0)]
    all_to_all x2 -> x1, starting transfers between devices: 9.78 us -> 4.73 us  [shards(): got = lax.all_to_all(share, 'ep', 0, 0)]
    pallas_call x1 -> x6, Pallas kernels: 18.1 us -> 21.1 us  [the longest x1 18.1 us: shards(): call(backward_kernel, [payload, payload], [pltpu.VMEM((wide, width), F32)...]
    concatenate x5 -> x0, other arithmetic: 1.53 us -> none  [the longest x1 0.86 us: shards(): jnp.concatenate([grads[:width].reshape(n_seq, in_rows, LANES), grads[widt...]
    slice x11 -> x0, local copies, waits for them, and re-layouts: 1.52 us -> none  [the longest x3 0.66 us: shards(): grad_query, grad_kernel = (small[:n_heads], small[n_heads:n_heads + n_taps])]
    unnamed x21 -> x20, local copies, waits for them, and re-layouts: 4.33 us -> 3.53 us
  transfers between devices with their start and end apart: 5 -> 4, of which waited for: 3 -> 2; matrix products, arithmetic and copies ran while one was open for 1% -> 0% of each run, Pallas kernels for 1% -> 3%
where the time goes in v3:
time: 126 us; the launch traced here: 124 us
  blocking collectives  68.6 us (54%)
  Pallas kernels  33.5 us (27%)
  starting transfers between devices  10.6 us (8%)
  waiting for transfers between devices  5.67 us (4%)
  local copies, waits for them, and re-layouts  4.34 us (3%)
  between operations  1.42 us (1%)
    all_to_all x1, blocking collectives, shards(): sums = lax.all_to_all(sums, 'seq', 0, 0)  32.6 us
    all_to_all x1, blocking collectives, shards(): got = lax.all_to_all(total, 'seq', 0, 0)  18.9 us
    pallas_call x1, Pallas kernels, shards(): call(backward_kernel, [payload, payload], [pltpu.VMEM((wide, width), F32)...  18.1 us
    all_to_all x1, blocking collectives, shards(): got = lax.all_to_all(total, 'ep', 0, 0, axis_index_groups=groups)  17.1 us
    pallas_call x1, Pallas kernels, shards(): call(forward_kernel, [shape((whole, width), BF16), shape((wide, width), B...  10.4 us
    all_to_all x1, starting transfers between devices, shards(): got = lax.all_to_all(share, 'ep', 0, 0)  4.73 us
    ppermute x1, starting transfers between devices, shards(): low = lax.ppermute(x[rows - STEP:], 'seq', forward)  4.55 us
    unnamed x20, local copies, waits for them, and re-layouts  3.53 us
  transfers between devices with their start and end apart: 4, of which 2 were waited for; matrix products, arithmetic and copies ran while one was open for 0% of the time, Pallas kernels for 3%

profile of v3, /device:TPU:8, one launch (start us, length us, event | category | flops | bytes accessed | tf_op | source)
XLA Modules:
  0.0 124.2 jit_solution(3168241274545119637)
XLA Ops:
  0.6 0.0 copy-start.7
  0.6 0.0 copy-start.6
  0.7 0.8 slice_bitcast_fusion
  1.5 1.3 %collective-permute-start.1 = (bf16[32,512]{1,0:T(8,128)(2,1)S(1)}, bf16[32,512]{1,0:T(8,128)(2,1)S(1)}, u32[]{:S(2)}, u32[]{:S(2)}) collective-permute-start(bf16[32,512]{1,0:T(8,128)(2,1)S(1)} %get-tuple-element.42), channel_id=1, source_target_pairs={{1,0},{2,1},{3,2},{4,3},{5,4},{6,5},{7,6},{8,7},{9,8},{10,9},{11,1... | collective-permute-start | bytes 98312 | tf_op jit(solution)/shard_map/ppermute | solution.py:421
  2.8 4.5 %collective-permute-start = (bf16[32,512]{1,0:T(8,128)(2,1)S(1)}, bf16[32,512]{1,0:T(8,128)(2,1)S(1)}, u32[]{:S(2)}, u32[]{:S(2)}) collective-permute-start(bf16[32,512]{1,0:T(8,128)(2,1)S(1)} %get-tuple-element.43), channel_id=1, source_target_pairs={{0,1},{1,2},{2,3},{3,4},{4,5},{5,6},{6,7},{7,8},{8,9},{9,10},{10,1... | collective-permute-start | bytes 98312 | tf_op jit(solution)/shard_map/ppermute | solution.py:420
  8.0 0.1 pad_add_fusion.place
  8.0 1.1 copy-done.1
  9.2 1.2 copy-done.2
  10.4 2.0 %shard_map.136 = (bf16[704,512]{1,0:T(8,128)(2,1)S(1)}, bf16[704,512]{1,0:T(8,128)(2,1)S(1)}, bf16[704,512]{1,0:T(8,128)(2,1)S(1)}, bf16[704,512]{1,0:T(8,128)(2,1)S(1)}) custom-call(s32[3]{0:T(128)S(1)} %pad_add_fusion.place, bf16[704,512]{1,0:T(8,128)(2,1)S(1)} %bitcast.9, bf16[512,1024]{1,0:T(8,128)(2,1)S(1)} %copy-done.2), custom_call_target="tpu_custom_call" | custom-call | flops 738197504 | bytes 8388608 | tf_op jit(solution)/shard_map/pallas_call | solution.py:426
  12.4 0.0 collective-permute-done.1.high_ref
  12.4 0.0 collective-permute-done.low_ref
  12.4 0.0 copy-done.7
  12.4 0.0 copy-done.6
  12.4 0.0 copy-done.3
  12.4 0.0 copy-start.4
  12.5 0.0 copy-start.5
  12.5 0.0 copy-start.8
  12.5 10.4 %shard_map.137 = (bf16[768,512]{1,0:T(8,128)(2,1)S(1)}, bf16[736,512]{1,0:T(8,128)(2,1)S(1)}, bf16[736,512]{1,0:T(8,128)(2,1)S(1)}, f32[736,512]{1,0:T(8,128)}, f32[32,8,640]{2,1,0:T(8,128)S(1)}) custom-call(s32[3]{0:T(128)S(1)} %pad_add_fusion.place, bf16[32,512]{1,0:T(8,128)(2,1)S(1)} %collective-permute-done.low_ref, ...), custom_call_target="tpu_custom_call" | custom-call | flops 1476395008 | bytes 8388608 | tf_op jit(solution)/shard_map/pallas_call | solution.py:429
  22.8 32.6 %all_to_all.20.sums_ref = f32[32,8,640]{2,1,0:T(8,128)S(1)} all-to-all(f32[32,8,640]{2,1,0:T(8,128)S(1)} %get-tuple-element.25), channel_id=1, replica_groups=mesh['ep'=8,'seq'=32] {'seq'}, dimensions={0} | all-to-all | bytes 1310720 | tf_op jit(solution)/shard_map/all_to_all | solution.py:442
  55.5 18.1 %shard_map.138 = (bf16[4,832,128]{2,1,0:T(8,128)(2,1)}, bf16[4,832,128]{2,1,0:T(8,128)(2,1)}) custom-call(s32[3]{0:T(128)S(1)} %pad_add_fusion.place, f32[32,8,640]{2,1,0:T(8,128)S(1)} %all_to_all.20.sums_ref, bf16[512,512]{1,0:T(8,128)(2,1)S(1)} %copy-done.4, bf16[256,512]{1,0:T(8,128)(2,1)S(1)} %copy-done.5, f32[1,256]{1,0:T(1,128)S(1)} %copy-done.8, ...), custom_call_target="tpu_custom_call" | custom-call | flops 2952790016 | bytes 8388608 | tf_op jit(solution)/shard_map/pallas_call | solution.py:450
  73.6 0.0 collective-permute-start.2
  73.6 2.6 %collective-permute-done.2.got_ref = bf16[4,832,128]{2,1,0:T(8,128)(2,1)S(1)} collective-permute-done((bf16[4,832,128]{2,1,0:T(8,128)(2,1)}, bf16[4,832,128]{2,1,0:T(8,128)(2,1)S(1)}, u32[]{:S(2)}, u32[]{:S(2)}) %collective-permute-start.2) | collective-permute-done | bytes 852000 | tf_op jit(solution)/shard_map/ppermute | solution.py:470
  76.2 1.2 copy-done
  77.4 0.2 shard_map.139
  77.6 17.1 %all_to_all.21.got_ref = bf16[4,880,128]{2,1,0:T(8,128)(2,1)S(1)} all-to-all(bf16[4,880,128]{2,1,0:T(8,128)(2,1)S(1)} %shard_map.139), channel_id=1, replica_groups={{0,64,128,192},{32,96,160,224},{1,65,129,193},{33,97,161,225},{2,66,130..., dimensions={0} | all-to-all | bytes 1802240 | tf_op jit(solution)/shard_map/all_to_all | solution.py:477
  94.7 0.1 shard_map.141
  94.8 18.9 %all_to_all.22.got_ref = bf16[32,48,128]{2,1,0:T(8,128)(2,1)S(1)} all-to-all(bf16[32,48,128]{2,1,0:T(8,128)(2,1)S(1)} %shard_map.141), channel_id=1, replica_groups=mesh['ep'=8,'seq'=32] {'seq'}, dimensions={0} | all-to-all | bytes 786432 | tf_op jit(solution)/shard_map/all_to_all | solution.py:489
  113.7 0.8 shard_map.142
  114.4 4.7 %all-to-all-start.3 = ((f32[8,24,128]{2,1,0:T(8,128)}), f32[8,24,128]{2,1,0:T(8,128)S(1)}, u32[]{:S(2)}, u32[]{:S(2)}) async-start(f32[8,24,128]{2,1,0:T(8,128)} %get-tuple-element.38), calls=%async_computation.3 | async-start | bytes 196608 | tf_op jit(solution)/shard_map/all_to_all | solution.py:499
  119.2 1.3 %shard_map.140 = (f32[512,512]{1,0:T(8,128)}, f32[1,128]{1,0:T(1,128)}) custom-call(bf16[4,880,128]{2,1,0:T(8,128)(2,1)S(1)} %all_to_all.21.got_ref), custom_call_target="tpu_custom_call" | custom-call | flops 1048576 | bytes 8388608 | tf_op jit(solution)/shard_map/pallas_call | solution.py:483
  120.4 3.1 %all-to-all-done.3.got_ref = f32[8,24,128]{2,1,0:T(8,128)S(1)} async-done(((f32[8,24,128]{2,1,0:T(8,128)}), f32[8,24,128]{2,1,0:T(8,128)S(1)}, u32[]{:S(2)}, u32[]{:S(2)}) %all-to-all-start.3) | async-done | bytes 98336 | tf_op jit(solution)/shard_map/all_to_all | solution.py:499
  123.5 0.6 shard_map.143
  (9 shorter events, 0.0 us)
Async XLA Ops:
  0.6 11.8 %copy-start.7 = (bf16[8,512]{1,0:T(8,128)(2,1)S(1)}, bf16[8,512]{1,0:T(8,128)(2,1)}, u32[]{:S(2)}) copy-start(bf16[8,512]{1,0:T(8,128)(2,1)} %query_ref.3) | copy-start | bytes 24580
  0.6 11.8 %copy-start.6 = (f32[31,512]{1,0:T(8,128)S(1)}, f32[31,512]{1,0:T(8,128)}, u32[]{:S(2)}) copy-start(f32[31,512]{1,0:T(8,128)} %taps_ref.3) | copy-start | bytes 190468
  1.5 10.9 %collective-permute-start.1 = (bf16[32,512]{1,0:T(8,128)(2,1)S(1)}, bf16[32,512]{1,0:T(8,128)(2,1)S(1)}, u32[]{:S(2)}, u32[]{:S(2)}) collective-permute-start(bf16[32,512]{1,0:T(8,128)(2,1)S(1)} %get-tuple-element.42), channel_id=1, source_target_pairs={{1,0},{2,1},{3,2},{4,3},{5,4},{6,5},{7,6},{8,7},{9,8},{10,9},{11,1... | collective-permute-start | bytes 98312 | tf_op jit(solution)/shard_map/ppermute | solution.py:421
  2.8 9.7 %collective-permute-start = (bf16[32,512]{1,0:T(8,128)(2,1)S(1)}, bf16[32,512]{1,0:T(8,128)(2,1)S(1)}, u32[]{:S(2)}, u32[]{:S(2)}) collective-permute-start(bf16[32,512]{1,0:T(8,128)(2,1)S(1)} %get-tuple-element.43), channel_id=1, source_target_pairs={{0,1},{1,2},{2,3},{3,4},{4,5},{5,6},{6,7},{7,8},{8,9},{9,10},{10,1... | collective-permute-start | bytes 98312 | tf_op jit(solution)/shard_map/ppermute | solution.py:420
  8.0 1.1 copy-start.1
  9.2 1.2 copy-start.2
  10.4 2.1 %copy-start.3 = (bf16[512,512]{1,0:T(8,128)(2,1)S(1)}, bf16[512,512]{1,0:T(8,128)(2,1)}, u32[]{:S(2)}) copy-start(bf16[512,512]{1,0:T(8,128)(2,1)} %w_out_ref.3) | copy-start | bytes 1572868
  12.4 43.0 %copy-start.4 = (bf16[512,512]{1,0:T(8,128)(2,1)S(1)}, bf16[512,512]{1,0:T(8,128)(2,1)}, u32[]{:S(2)}) copy-start(bf16[512,512]{1,0:T(8,128)(2,1)} %w_value_ref.1) | copy-start | bytes 1572868
  12.5 43.0 %copy-start.5 = (bf16[256,512]{1,0:T(8,128)(2,1)S(1)}, bf16[256,512]{1,0:T(8,128)(2,1)}, u32[]{:S(2)}) copy-start(bf16[256,512]{1,0:T(8,128)(2,1)} %text_ref.1) | copy-start | bytes 786436
  12.5 43.0 %copy-start.8 = (f32[1,256]{1,0:T(1,128)S(1)}, f32[1,256]{1,0:T(1,128)}, u32[]{:S(2)}) copy-start(f32[1,256]{1,0:T(1,128)} %teacher_ref.1) | copy-start | bytes 3076
  22.8 32.6 %copy-start.9 = (bf16[768,512]{1,0:T(8,128)(2,1)}, bf16[768,512]{1,0:T(8,128)(2,1)S(1)}, u32[]{:S(2)}) copy-start(bf16[768,512]{1,0:T(8,128)(2,1)S(1)} %get-tuple-element.29.glu_ref) | copy-start | bytes 2359300
  73.6 2.6 %collective-permute-start.2 = (bf16[4,832,128]{2,1,0:T(8,128)(2,1)}, bf16[4,832,128]{2,1,0:T(8,128)(2,1)S(1)}, u32[]{:S(2)}, u32[]{:S(2)}) collective-permute-start(bf16[4,832,128]{2,1,0:T(8,128)(2,1)} %get-tuple-element.34), channel_id=1, source_target_pairs={{0,32},{32,0},{64,96},{96,64},{128,160},{160,128},{192,224},{224,1... | collective-permute-start | bytes 2555912 | tf_op jit(solution)/shard_map/ppermute | solution.py:470
  76.2 1.2 copy-start
  114.4 9.1 %all-to-all-start.3 = ((f32[8,24,128]{2,1,0:T(8,128)}), f32[8,24,128]{2,1,0:T(8,128)S(1)}, u32[]{:S(2)}, u32[]{:S(2)}) async-start(f32[8,24,128]{2,1,0:T(8,128)} %get-tuple-element.38), calls=%async_computation.3 | async-start | bytes 196608 | tf_op jit(solution)/shard_map/all_to_all | solution.py:499

commit v4 on v3

--- a/solution.py
+++ b/solution.py
@@ -153,7 +153,7 @@
         expo = jnp.where(valid, jnp.exp(scores[i] - top), 0.0)
         total = total + jnp.sum(expo, axis=0, keepdims=True)
         weights = lane_groups(expo.shape, split3(expo))
-        for piece in split3(resid_ref[pl.ds(SIDE + i * chunk, chunk), :]):
+        for piece in split3(resid_ref[pl.ds(SIDE + i * chunk, chunk), :])[:2]:
             vec = vec + dot(weights, piece, TN)
     lane = lax.broadcasted_iota(jnp.int32, (8, LANES), 1)
     sums = jnp.concatenate(
@@ -209,10 +209,10 @@
 
     top_l, total_l, centre_l = across(top), across(total), across(centre)
     query = query_ref[...]
-    queries = jnp.concatenate([query] * (LANES // 8), axis=0)
     d_high, d_mid, d_low = split3(dvbar)
-    many = lambda piece: jnp.concatenate([piece] * (LANES // 8), axis=0)
-    dv_high, dv_mid, dv_low = many(d_high), many(d_mid), many(d_low)
+    many = lambda piece: [piece] * (LANES // 8)
+    both = jnp.concatenate(many(query) + many(d_high), axis=0)
+    queries, dv_mid = both[:LANES], jnp.concatenate(many(d_mid), axis=0)
     mixing = jnp.concatenate(
         [d_high, d_mid, d_high, d_mid, query, query, query, jnp.zeros((LANES - 56, width), BF16)],
         axis=0,
@@ -224,13 +224,11 @@
     for i in range(parts):
         here = pl.ds(i * chunk, chunk)
         r_high, r_mid, r_low = split3(resid_ref[here, :])
-        score = (dot(r_high, queries, NT) + dot(r_mid, queries, NT) + dot(r_low, queries, NT)) / root
+        products = dot(r_high, both, NT) + dot(r_mid, both, NT)
+        score = (products[:, :LANES] + dot(r_low, queries, NT)) / root
         valid = row_mask(place[0] - SIDE + i * chunk, chunk, place[1])
         probs = jnp.where(valid, jnp.exp(score - top_l), 0.0) / total_l
-        proj = dot(r_high, dv_high, NT) + (dot(r_high, dv_mid, NT) + dot(r_mid, dv_high, NT))
-        proj = proj + (
-            dot(r_high, dv_low, NT) + dot(r_mid, dv_mid, NT) + dot(r_low, dv_high, NT)
-        )
+        proj = products[:, LANES:] + dot(r_high, dv_mid, NT)
         dscores = probs * (proj - centre_l) / root
         p_high, p_mid, unused = split3(probs)
         s_pieces = split3(dscores)
@@ -241,7 +239,7 @@
         own = (own >= SIDE) & (own < SIDE + rows)
         weights = lane_groups(probs.shape, s_pieces)
         weights = jnp.where(own, weights.astype(F32), 0.0).astype(BF16)
-        for piece in (r_high, r_mid, r_low):
+        for piece in (r_high, r_mid):
             grad_query = grad_query + dot(weights, piece, TN)
         dact = dot(dresid, w_out, NT)
         dconv = (dact * slope_ref[here, :].astype(F32)).astype(BF16)
@@ -402,7 +400,7 @@
         in_specs=[pl.BlockSpec(memory_space=pltpu.SMEM)] * placed + [vmem] * n_args,
         out_specs=[vmem] * len(outs),
         scratch_shapes=scratch,
-        compiler_params=pltpu.CompilerParams(vmem_limit_bytes=48 * 2**20),
+        compiler_params=pltpu.CompilerParams(vmem_limit_bytes=24 * 2**20),
         cost_estimate=pl.CostEstimate(flops=flops, bytes_accessed=8 * 2**20, transcendentals=2**20),
     )
 
@@ -423,9 +421,9 @@
     place = jnp.stack([lax.axis_index("seq") * rows, lengths[0], core]).astype(jnp.int32)
 
     own = shape((rows, width), BF16)
-    normed, sig, gate_slope, own_glu = call(project_kernel, [own] * 4, [], 2, 2 * rows * width * width * 2)(
-        place, x, w_in
-    )
+    normed, sig, gate_slope, own_glu = call(
+        project_kernel, [own] * 4, [], 2, 2 * rows * width * width * 2
+    )(place, x, w_in)
     glu, act, slope, resid, sums = call(
         forward_kernel,
         [

time: 126 us -> 120 us (0.952)
  Pallas kernels: 33.5 us -> 28.5 us
    pallas_call x1, Pallas kernels: 18.1 us -> 14.8 us  [shards(): call(backward_kernel, [payload, payload], [pltpu.VMEM((wide, width), F32)...]
    pallas_call x1, Pallas kernels: 10.4 us -> 8.79 us  [shards(): call(forward_kernel, [shape((whole, width), BF16), shape((wide, width), B...]
    unnamed x20 -> x16, local copies, waits for them, and re-layouts: 3.53 us -> 2.37 us
where the time goes in v4:
time: 120 us; the launch traced here: 118 us
  blocking collectives  68.6 us (57%)
  Pallas kernels  28.5 us (24%)
  starting transfers between devices  10.7 us (9%)
  waiting for transfers between devices  5.45 us (5%)
  local copies, waits for them, and re-layouts  3.18 us (3%)
  between operations  1.43 us (1%)
    all_to_all x1, blocking collectives, shards(): sums = lax.all_to_all(sums, 'seq', 0, 0)  32.6 us
    all_to_all x1, blocking collectives, shards(): got = lax.all_to_all(total, 'seq', 0, 0)  18.9 us
    all_to_all x1, blocking collectives, shards(): got = lax.all_to_all(total, 'ep', 0, 0, axis_index_groups=groups)  17.1 us
    pallas_call x1, Pallas kernels, shards(): call(backward_kernel, [payload, payload], [pltpu.VMEM((wide, width), F32)...  14.8 us
    pallas_call x1, Pallas kernels, shards(): call(forward_kernel, [shape((whole, width), BF16), shape((wide, width), B...  8.79 us
    all_to_all x1, starting transfers between devices, shards(): got = lax.all_to_all(share, 'ep', 0, 0)  4.73 us
    ppermute x1, starting transfers between devices, shards(): low = lax.ppermute(x[rows - STEP:], 'seq', forward)  4.55 us
    all_to_all x1, waiting for transfers between devices, shards(): got = lax.all_to_all(share, 'ep', 0, 0)  3.07 us
  transfers between devices with their start and end apart: 4, of which 2 were waited for; matrix products, arithmetic and copies ran while one was open for 0% of the time, Pallas kernels for 3%

profile of v4, /device:TPU:8, one launch (start us, length us, event | category | flops | bytes accessed | tf_op | source)
XLA Modules:
  0.0 117.9 jit_solution(7577030267853586951)
XLA Ops:
  0.6 0.0 copy-start.6
  0.6 0.0 copy-start.5
  0.7 0.8 slice_bitcast_fusion
  1.5 1.3 %collective-permute-start.1 = (bf16[32,512]{1,0:T(8,128)(2,1)S(1)}, bf16[32,512]{1,0:T(8,128)(2,1)S(1)}, u32[]{:S(2)}, u32[]{:S(2)}) collective-permute-start(bf16[32,512]{1,0:T(8,128)(2,1)S(1)} %get-tuple-element.42), channel_id=1, source_target_pairs={{1,0},{2,1},{3,2},{4,3},{5,4},{6,5},{7,6},{8,7},{9,8},{10,9},{11,1... | collective-permute-start | bytes 98312 | tf_op jit(solution)/shard_map/ppermute | solution.py:419
  2.8 4.5 %collective-permute-start = (bf16[32,512]{1,0:T(8,128)(2,1)S(1)}, bf16[32,512]{1,0:T(8,128)(2,1)S(1)}, u32[]{:S(2)}, u32[]{:S(2)}) collective-permute-start(bf16[32,512]{1,0:T(8,128)(2,1)S(1)} %get-tuple-element.43), channel_id=1, source_target_pairs={{0,1},{1,2},{2,3},{3,4},{4,5},{5,6},{6,7},{7,8},{8,9},{9,10},{10,1... | collective-permute-start | bytes 98312 | tf_op jit(solution)/shard_map/ppermute | solution.py:418
  8.0 0.1 pad_add_fusion.place
  8.0 1.1 copy-done
  9.2 1.2 %copy-done.1 = bf16[512,1024]{1,0:T(8,128)(2,1)S(1)} copy-done((bf16[512,1024]{1,0:T(8,128)(2,1)S(1)}, bf16[512,1024]{1,0:T(8,128)(2,1)}, u32[]{:S(2)}) %copy-start.1) | copy-done | bytes 1048600
  10.4 2.0 %shard_map.136 = (bf16[704,512]{1,0:T(8,128)(2,1)S(1)}, bf16[704,512]{1,0:T(8,128)(2,1)S(1)}, bf16[704,512]{1,0:T(8,128)(2,1)S(1)}, bf16[704,512]{1,0:T(8,128)(2,1)S(1)}) custom-call(s32[3]{0:T(128)S(1)} %pad_add_fusion.place, bf16[704,512]{1,0:T(8,128)(2,1)S(1)} %bitcast.9, bf16[512,1024]{1,0:T(8,128)(2,1)S(1)} %copy-done.1), custom_call_target="tpu_custom_call" | custom-call | flops 738197504 | bytes 8388608 | tf_op jit(solution)/shard_map/pallas_call | solution.py:424
  12.4 0.0 collective-permute-done.1.high_ref
  12.4 0.0 collective-permute-done.low_ref
  12.4 0.0 copy-done.6
  12.4 0.0 copy-done.5
  12.4 0.0 copy-done.2
  12.4 0.0 copy-start.3
  12.5 0.0 copy-start.4
  12.5 0.0 copy-start.7
  12.5 8.8 %shard_map.137 = (bf16[768,512]{1,0:T(8,128)(2,1)S(1)}, bf16[736,512]{1,0:T(8,128)(2,1)S(1)}, bf16[736,512]{1,0:T(8,128)(2,1)S(1)}, f32[736,512]{1,0:T(8,128)S(1)}, f32[32,8,640]{2,1,0:T(8,128)S(1)}) custom-call(s32[3]{0:T(128)S(1)} %pad_add_fusion.place, bf16[32,512]{1,0:T(8,128)(2,1)S(1)} %collective-permute-done.low_ref, ...), custom_call_target="tpu_custom_call" | custom-call | flops 1476395008 | bytes 8388608 | tf_op jit(solution)/shard_map/pallas_call | solution.py:427
  21.3 32.6 %all_to_all.20.sums_ref = f32[32,8,640]{2,1,0:T(8,128)S(1)} all-to-all(f32[32,8,640]{2,1,0:T(8,128)S(1)} %get-tuple-element.25), channel_id=1, replica_groups=mesh['ep'=8,'seq'=32] {'seq'}, dimensions={0} | all-to-all | bytes 1310720 | tf_op jit(solution)/shard_map/all_to_all | solution.py:440
  53.9 0.0 copy-done.7
  53.9 14.8 %shard_map.138 = (bf16[4,832,128]{2,1,0:T(8,128)(2,1)S(1)}, bf16[4,832,128]{2,1,0:T(8,128)(2,1)S(1)}) custom-call(s32[3]{0:T(128)S(1)} %pad_add_fusion.place, f32[32,8,640]{2,1,0:T(8,128)S(1)} %all_to_all.20.sums_ref, bf16[512,512]{1,0:T(8,128)(2,1)S(1)} %copy-done.3, bf16[256,512]{1,0:T(8,128)(2,1)S(1)} %copy-done.4, f32[1,256]{1,0:T(1,128)S(1)} %copy-done.7, ...), custom_call_target="tpu_custom_call" | custom-call | flops 2952790016 | bytes 8388608 | tf_op jit(solution)/shard_map/pallas_call | solution.py:448
  68.7 0.1 collective-permute-start.2
  68.8 2.4 %collective-permute-done.2.got_ref = bf16[4,832,128]{2,1,0:T(8,128)(2,1)S(1)} collective-permute-done((bf16[4,832,128]{2,1,0:T(8,128)(2,1)S(1)}, bf16[4,832,128]{2,1,0:T(8,128)(2,1)S(1)}, u32[]{:S(2)}, u32[]{:S(2)}) %collective-permute-start.2) | collective-permute-done | bytes 852000 | tf_op jit(solution)/shard_map/ppermute | solution.py:468
  71.2 0.2 shard_map.139
  71.4 17.1 %all_to_all.21.got_ref = bf16[4,880,128]{2,1,0:T(8,128)(2,1)S(1)} all-to-all(bf16[4,880,128]{2,1,0:T(8,128)(2,1)S(1)} %shard_map.139), channel_id=1, replica_groups={{0,64,128,192},{32,96,160,224},{1,65,129,193},{33,97,161,225},{2,66,130..., dimensions={0} | all-to-all | bytes 1802240 | tf_op jit(solution)/shard_map/all_to_all | solution.py:475
  88.4 0.1 shard_map.141
  88.5 18.9 %all_to_all.22.got_ref = bf16[32,48,128]{2,1,0:T(8,128)(2,1)S(1)} all-to-all(bf16[32,48,128]{2,1,0:T(8,128)(2,1)S(1)} %shard_map.141), channel_id=1, replica_groups=mesh['ep'=8,'seq'=32] {'seq'}, dimensions={0} | all-to-all | bytes 786432 | tf_op jit(solution)/shard_map/all_to_all | solution.py:487
  107.4 0.8 shard_map.142
  108.2 4.7 %all-to-all-start.3 = ((f32[8,24,128]{2,1,0:T(8,128)}), f32[8,24,128]{2,1,0:T(8,128)S(1)}, u32[]{:S(2)}, u32[]{:S(2)}) async-start(f32[8,24,128]{2,1,0:T(8,128)} %get-tuple-element.38), calls=%async_computation.3 | async-start | bytes 196608 | tf_op jit(solution)/shard_map/all_to_all | solution.py:497
  112.9 1.3 %shard_map.140 = (f32[512,512]{1,0:T(8,128)}, f32[1,128]{1,0:T(1,128)}) custom-call(bf16[4,880,128]{2,1,0:T(8,128)(2,1)S(1)} %all_to_all.21.got_ref), custom_call_target="tpu_custom_call" | custom-call | flops 1048576 | bytes 8388608 | tf_op jit(solution)/shard_map/pallas_call | solution.py:481
  114.2 3.1 %all-to-all-done.3.got_ref = f32[8,24,128]{2,1,0:T(8,128)S(1)} async-done(((f32[8,24,128]{2,1,0:T(8,128)}), f32[8,24,128]{2,1,0:T(8,128)S(1)}, u32[]{:S(2)}, u32[]{:S(2)}) %all-to-all-start.3) | async-done | bytes 98336 | tf_op jit(solution)/shard_map/all_to_all | solution.py:497
  117.3 0.6 shard_map.143
  (5 shorter events, 0.0 us)
Async XLA Ops:
  0.6 11.8 %copy-start.6 = (bf16[8,512]{1,0:T(8,128)(2,1)S(1)}, bf16[8,512]{1,0:T(8,128)(2,1)}, u32[]{:S(2)}) copy-start(bf16[8,512]{1,0:T(8,128)(2,1)} %query_ref.3) | copy-start | bytes 24580
  0.6 11.8 %copy-start.5 = (f32[31,512]{1,0:T(8,128)S(1)}, f32[31,512]{1,0:T(8,128)}, u32[]{:S(2)}) copy-start(f32[31,512]{1,0:T(8,128)} %taps_ref.3) | copy-start | bytes 190468
  1.5 10.9 %collective-permute-start.1 = (bf16[32,512]{1,0:T(8,128)(2,1)S(1)}, bf16[32,512]{1,0:T(8,128)(2,1)S(1)}, u32[]{:S(2)}, u32[]{:S(2)}) collective-permute-start(bf16[32,512]{1,0:T(8,128)(2,1)S(1)} %get-tuple-element.42), channel_id=1, source_target_pairs={{1,0},{2,1},{3,2},{4,3},{5,4},{6,5},{7,6},{8,7},{9,8},{10,9},{11,1... | collective-permute-start | bytes 98312 | tf_op jit(solution)/shard_map/ppermute | solution.py:419
  2.8 9.7 %collective-permute-start = (bf16[32,512]{1,0:T(8,128)(2,1)S(1)}, bf16[32,512]{1,0:T(8,128)(2,1)S(1)}, u32[]{:S(2)}, u32[]{:S(2)}) collective-permute-start(bf16[32,512]{1,0:T(8,128)(2,1)S(1)} %get-tuple-element.43), channel_id=1, source_target_pairs={{0,1},{1,2},{2,3},{3,4},{4,5},{5,6},{6,7},{7,8},{8,9},{9,10},{10,1... | collective-permute-start | bytes 98312 | tf_op jit(solution)/shard_map/ppermute | solution.py:418
  8.0 1.1 copy-start
  9.2 1.2 %copy-start.1 = (bf16[512,1024]{1,0:T(8,128)(2,1)S(1)}, bf16[512,1024]{1,0:T(8,128)(2,1)}, u32[]{:S(2)}) copy-start(bf16[512,1024]{1,0:T(8,128)(2,1)} %w_in_ref.3) | copy-start | bytes 3145732
  10.4 2.1 %copy-start.2 = (bf16[512,512]{1,0:T(8,128)(2,1)S(1)}, bf16[512,512]{1,0:T(8,128)(2,1)}, u32[]{:S(2)}) copy-start(bf16[512,512]{1,0:T(8,128)(2,1)} %w_out_ref.3) | copy-start | bytes 1572868
  12.4 41.5 %copy-start.3 = (bf16[512,512]{1,0:T(8,128)(2,1)S(1)}, bf16[512,512]{1,0:T(8,128)(2,1)}, u32[]{:S(2)}) copy-start(bf16[512,512]{1,0:T(8,128)(2,1)} %w_value_ref.1) | copy-start | bytes 1572868
  12.5 41.5 %copy-start.4 = (bf16[256,512]{1,0:T(8,128)(2,1)S(1)}, bf16[256,512]{1,0:T(8,128)(2,1)}, u32[]{:S(2)}) copy-start(bf16[256,512]{1,0:T(8,128)(2,1)} %text_ref.1) | copy-start | bytes 786436
  12.5 41.5 %copy-start.7 = (f32[1,256]{1,0:T(1,128)S(1)}, f32[1,256]{1,0:T(1,128)}, u32[]{:S(2)}) copy-start(f32[1,256]{1,0:T(1,128)} %teacher_ref.1) | copy-start | bytes 3076
  68.7 2.5 %collective-permute-start.2 = (bf16[4,832,128]{2,1,0:T(8,128)(2,1)S(1)}, bf16[4,832,128]{2,1,0:T(8,128)(2,1)S(1)}, u32[]{:S(2)}, u32[]{:S(2)}) collective-permute-start(bf16[4,832,128]{2,1,0:T(8,128)(2,1)S(1)} %get-tuple-element.34), channel_id=1, source_target_pairs={{0,32},{32,0},{64,96},{96,64},{128,160},{160,128},{192,224},{224,1... | collective-permute-start | bytes 2555912 | tf_op jit(solution)/shard_map/ppermute | solution.py:468
  108.2 9.1 %all-to-all-start.3 = ((f32[8,24,128]{2,1,0:T(8,128)}), f32[8,24,128]{2,1,0:T(8,128)S(1)}, u32[]{:S(2)}, u32[]{:S(2)}) async-start(f32[8,24,128]{2,1,0:T(8,128)} %get-tuple-element.38), calls=%async_computation.3 | async-start | bytes 196608 | tf_op jit(solution)/shard_map/all_to_all | solution.py:497

commit v5 on v4

--- a/solution.py
+++ b/solution.py
@@ -165,15 +165,15 @@
         sums_ref[i] = sums
 
 
-def backward_kernel(
-    place, sums_ref, w_value_ref, text_ref, teacher_ref, query_ref, resid_ref, act_ref, slope_ref,
-    glu_ref, normed_ref, sig_ref, gate_slope_ref, w_out_ref, taps_ref,
-    mine_ref, other_ref,
-    dconv_f, glu_f, dresid_s, dmixed_s, in_s, tap_s, small_s,
+def middle_kernel(
+    place, sums_ref, w_value_ref, text_ref, teacher_ref, query_ref, resid_ref, slope_ref,
+    glu_ref, w_out_ref,
+    share_ref, episode_ref, dresid_ref, dconv_ref,
+    glu_f, tap_s,
 ):
-    rows, width = normed_ref.shape
-    wide = rows + 2 * SIDE
-    n_taps = taps_ref.shape[0]
+    wide, width = resid_ref.shape
+    rows = wide - 2 * SIDE
+    n_taps = tap_s.shape[0] - 1
     n_cands = text_ref.shape[0]
     head_dim = width // 8
     root = jnp.sqrt(jnp.float32(width))
@@ -205,7 +205,7 @@
     blocks = [slice(c * LANES, (c + 1) * LANES) for c in range(width // LANES)]
     for c, cols in enumerate(blocks):
         rest = jnp.where(row[:, :LANES] == c, dpooled[:, cols], rest)
-    episode = jnp.concatenate([*[vbar[:, cols] for cols in blocks], rest], axis=0)
+    episode_ref[...] = jnp.concatenate([*[vbar[:, cols] for cols in blocks], rest], axis=0)
 
     top_l, total_l, centre_l = across(top), across(total), across(centre)
     query = query_ref[...]
@@ -234,7 +234,7 @@
         s_pieces = split3(dscores)
         mixed = lane_groups(probs.shape, (p_high, p_high, p_mid, p_mid, *s_pieces))
         dresid = dot(mixed, mixing).astype(BF16)
-        dresid_s[here, :] = dresid
+        dresid_ref[here, :] = dresid
         own = lax.broadcasted_iota(jnp.int32, (chunk, 1), 0) + i * chunk
         own = (own >= SIDE) & (own < SIDE + rows)
         weights = lane_groups(probs.shape, s_pieces)
@@ -243,15 +243,41 @@
             grad_query = grad_query + dot(weights, piece, TN)
         dact = dot(dresid, w_out, NT)
         dconv = (dact * slope_ref[here, :].astype(F32)).astype(BF16)
-        dconv_f[here, :] = dconv.astype(F32)
+        dconv_ref[here, :] = dconv.astype(F32)
     query_sum = folded(grad_query)
-    high = query_sum.astype(BF16).astype(F32)
-    half = small_s.shape[0] // 2
-    small_s[0:8, :] = jnp.where(row < 4, high, pltpu.roll(query_sum - high, 4, 0))
-    small_s[half : half + 8, :] = jnp.where(row < 4, pltpu.roll(high, 4, 0), query_sum - high)
 
     glu_f[...] = glu_ref[...].astype(F32)
     tap_s[...] = jnp.zeros_like(tap_s)
+
+    @pl.loop(0, rows // STEP)
+    def _(i):
+        start = pl.multiple_of(i * STEP + SIDE, SIDE)
+        for c in range(width // LANES):
+            cols = slice(c * LANES, (c + 1) * LANES)
+            own = dconv_ref[pl.ds(start, STEP), cols]
+            views = shifted(glu_f[pl.ds(start, 2 * STEP), cols])
+            for k in range(n_taps):
+                q, s = divmod(k + 1, 8)
+                product = own * views[s][8 * q : 8 * q + STEP]
+                tap_s[k, :, cols] += folded(product, STEP // 8)
+
+    small = jnp.concatenate([query_sum, jnp.sum(tap_s[...], axis=1)], axis=0)
+    per = share_ref.shape[0] // len(blocks)
+    for c, cols in enumerate(blocks):
+        for j in range(per):
+            if 8 * j < small.shape[0]:
+                share_ref[c * per + j] = small[8 * j : 8 * j + 8, cols]
+            else:
+                share_ref[c * per + j] = jnp.zeros((8, LANES), F32)
+
+
+def backward_kernel(
+    place, dconv_ref, dresid_ref, act_ref, normed_ref, sig_ref, gate_slope_ref, taps_ref, episode_ref,
+    mine_ref, other_ref,
+    dmixed_s, in_s,
+):
+    rows, width = normed_ref.shape
+    n_taps = taps_ref.shape[0]
 
     @pl.loop(0, rows // STEP)
     def _(i):
@@ -259,7 +285,7 @@
         valid = row_mask(place[0] + start, STEP, place[1])
         for c in range(width // LANES):
             cols = slice(c * LANES, (c + 1) * LANES)
-            views = shifted(dconv_f[pl.ds(start, 2 * STEP), cols])
+            views = shifted(dconv_ref[pl.ds(start, 2 * STEP), cols])
             acc = jnp.zeros((STEP, LANES), F32)
             for k in range(n_taps):
                 q, s = divmod(n_taps - k, 8)
@@ -270,20 +296,13 @@
             dmixed_s[here, slice(width + c * LANES, width + (c + 1) * LANES)] = (
                 dglu * gate_slope_ref[here, cols].astype(F32)
             ).astype(BF16)
-            own = views[0][SIDE : SIDE + STEP]
-            views = shifted(glu_f[pl.ds(start + SIDE, 2 * STEP), cols])
-            for k in range(n_taps):
-                q, s = divmod(k + 1, 8)
-                product = own * views[s][8 * q : 8 * q + STEP]
-                tap_s[k, :, cols] += folded(product, STEP // 8)
-
-    tap_sum = jnp.sum(tap_s[...], axis=1)
-    small_s[8:half, :] = tap_sum[: half - 8]
-    small_s[half + 8 :, :] = tap_sum[half - 8 :]
-
-    grad_out = dot(act_ref[SIDE : SIDE + rows, :], dresid_s[SIDE : SIDE + rows, :], TN)
+
+    grad_out = dot(act_ref[SIDE : SIDE + rows, :], dresid_ref[SIDE : SIDE + rows, :], TN)
     in_s[...] = dot(normed_ref[...], dmixed_s[...], TN).astype(BF16)
     core = place[2]
+    big = width + width // 2
+    tail = mine_ref.shape[1] - big - episode_ref.shape[0]
+    episode = jnp.concatenate([episode_ref[...], jnp.zeros((tail, LANES), F32)], axis=0).astype(BF16)
     halves = grad_out.reshape(width // 16, 2, 8, width)
     first, second = (halves[:, j].reshape(width // 2, width) for j in range(2))
     low_lane = lax.broadcasted_iota(jnp.int32, (width // 2, LANES), 1) < LANES // 2
@@ -298,50 +317,44 @@
         ):
             at = pl.multiple_of((2 * y + which) * LANES, LANES)
             ref[y, 0:width, :] = in_s[:, pl.ds(at, LANES)]
-            ref[y, width : width + width // 2, :] = block.astype(BF16)
-            share = small_s[pl.ds(pl.multiple_of(which * half, 8), half), y * LANES : (y + 1) * LANES]
-            ref[y, width + width // 2 :, :] = jnp.concatenate([share, episode], axis=0).astype(BF16)
-
-
-def paired(rows):
-    row = lax.broadcasted_iota(jnp.int32, rows.shape, 0)
-    value = rows + pltpu.roll(rows, 4, 0)
+            ref[y, width:big, :] = block.astype(BF16)
+            ref[y, big:, :] = episode
+
+
+def paired(value):
     high = value.astype(BF16).astype(F32)
-    return jnp.where(row < 4, high, value - high)
-
-
-def cores_kernel(big, half, mine_ref, got_ref, out_ref):
+    return jnp.concatenate([high, value - high], axis=0)
+
+
+def cores_kernel(big, size, mine_ref, got_ref, share_ref, got_share_ref, out_ref):
+    share = paired(share_ref[...] + got_share_ref[...])
     for y in range(mine_ref.shape[0]):
         total = mine_ref[y, 0:big, :].astype(F32) + got_ref[y, 0:big, :].astype(F32)
         out_ref[y, 0:big, :] = total.astype(BF16)
         mine, got = mine_ref[y, big:, :].astype(F32), got_ref[y, big:, :].astype(F32)
-        share = mine[:half] + got[:half]
-        out_ref[y, big:, :] = jnp.concatenate(
-            [paired(share[:8]), share[8:], mine[half:], got[half:], jnp.zeros((8, LANES), F32)],
-            axis=0,
-        ).astype(BF16)
-
-
-def rows_kernel(big, half, got_ref, out_ref):
+        out_ref[y, big:, :] = jnp.concatenate([share, mine[:size], got[:size]], axis=0).astype(BF16)
+
+
+def rows_kernel(big, got_ref, out_ref):
     n_y, n_seq = got_ref.shape[0], out_ref.shape[0]
     total = got_ref[0, 0:big, :].astype(F32)
-    share = got_ref[0, big:, :].astype(F32)[:half]
+    share = got_ref[0, big:, :].astype(F32)[:16]
     for y in range(1, n_y):
         total = total + got_ref[y, 0:big, :].astype(F32)
-        share = share + got_ref[y, big:, :].astype(F32)[:half]
-    share = jnp.concatenate([paired(share[:8]), share[8:]], axis=0)
+        share = share + got_ref[y, big:, :].astype(F32)[:16]
+    share = paired(share[:8] + share[8:])
     split = 2 * big // 3
     out_ref[...] = jnp.concatenate(
         [
             total[:split].reshape(n_seq, split // n_seq, LANES),
             total[split:].reshape(n_seq, (big - split) // n_seq, LANES),
-            jnp.broadcast_to(share[None], (n_seq, half, LANES)),
+            jnp.broadcast_to(share[None], (n_seq, *share.shape)),
         ],
         axis=1,
     ).astype(BF16)
 
 
-def value_kernel(big, half, got_ref, grad_ref, loss_ref):
+def value_kernel(big, got_ref, grad_ref, loss_ref):
     width = grad_ref.shape[0]
     head = lax.broadcasted_iota(jnp.int32, (8, width), 1) // (width // 8)
     own_head = head == lax.broadcasted_iota(jnp.int32, (8, width), 0)
@@ -351,7 +364,7 @@
     size = 8 * (n_blocks + 1)
     for y in range(got_ref.shape[0]):
         rows = got_ref[y, big:, :].astype(F32)
-        for start in (half, half + size):
+        for start in (16, 16 + size):
             episode = rows[start : start + size]
             rest = episode[8 * n_blocks :]
             vectors.append(
@@ -365,31 +378,29 @@
     loss_ref[...] = loss
 
 
-def owner_kernel(got_ref, grad_in_ref, grad_out_ref, out_ref):
-    total = got_ref[0].astype(F32)
-    for s in range(1, got_ref.shape[0]):
-        total = total + got_ref[s].astype(F32)
+def owner_kernel(got_ref, grad_in_ref, grad_out_ref, taps_ref, query_ref):
+    n_seq = got_ref.shape[0]
     in_rows, cols = grad_in_ref.shape[0], grad_out_ref.shape[1]
     out_rows = grad_out_ref.shape[0] // 2
+    n_taps = taps_ref.shape[0]
+    per = n_seq // (taps_ref.shape[1] // LANES)
+    total = jnp.zeros((in_rows + out_rows, LANES), F32)
+    for s in range(n_seq):
+        block = got_ref[s].astype(F32)
+        total = total + block[: in_rows + out_rows]
+        share = block[in_rows + out_rows :]
+        share = share[:8] + share[8:]
+        c, j = divmod(s, per)
+        lanes = slice(c * LANES, (c + 1) * LANES)
+        if j == 0:
+            query_ref[:, lanes] = share
+        elif 8 * (j - 1) < n_taps:
+            last = min(8 * j, n_taps)
+            taps_ref[8 * (j - 1) : last, lanes] = share[: last - 8 * (j - 1)]
     grad_in_ref[...] = total[:in_rows]
-    pair_rows = total[in_rows : in_rows + out_rows]
+    pair_rows = total[in_rows:]
     grad_out_ref[0:out_rows, :] = pair_rows[:, :cols]
     grad_out_ref[out_rows:, :] = pair_rows[:, cols:]
-    share = total[in_rows + out_rows :]
-    share = jnp.concatenate([share[:8] + pltpu.roll(share[:8], 4, 0), share[8:]], axis=0)
-    for e in range(out_ref.shape[0]):
-        out_ref[e] = share
-
-
-def last_kernel(got_ref, taps_ref, query_ref):
-    n_taps = taps_ref.shape[0]
-    for y in range(got_ref.shape[0] // 2):
-        cols = slice(y * LANES, (y + 1) * LANES)
-        first, second = got_ref[2 * y], got_ref[2 * y + 1]
-        row = lax.broadcasted_iota(jnp.int32, (8, LANES), 0)
-        query_ref[:, cols] = jnp.where(row < 4, first[:8], second[:8])
-        taps_ref[0:16, cols] = first[8:]
-        taps_ref[16:n_taps, cols] = second[8 : 8 + n_taps - 16]
 
 
 def call(kernel, outs, scratch, n_args, flops, placed=True):
@@ -439,64 +450,67 @@
     )(place, low, high, x, own_glu, w_in, kernel, w_out, pool_query)
     sums = lax.all_to_all(sums, "seq", 0, 0)
 
-    small_rows = 48
-    half = small_rows // 2
     big = width + width // 2
     n_y = n_ep // 2
     size = 8 * (width // LANES + 1)
-    payload = shape((n_y, big + half + size, LANES), BF16)
+    share, episode, dresid, dconv = call(
+        middle_kernel,
+        [
+            shape((n_seq, 8, LANES), F32),
+            shape((size, LANES), F32),
+            shape((wide, width), BF16),
+            shape((wide, width), F32),
+        ],
+        [pltpu.VMEM((whole, width), F32), pltpu.VMEM((n_taps + 1, 8, width), F32)],
+        9,
+        2 * rows * width * width * 4,
+    )(place, sums, w_value, text_emb, teacher, pool_query, resid, slope, glu, w_out)
+
+    share = lax.all_to_all(share, "seq", 0, 0)
+
+    payload = shape((n_y, big + size + 8, LANES), BF16)
     mine, other = call(
         backward_kernel,
         [payload, payload],
-        [
-            pltpu.VMEM((wide, width), F32),
-            pltpu.VMEM((whole, width), F32),
-            pltpu.VMEM((wide, width), BF16),
-            pltpu.VMEM((rows, 2 * width), BF16),
-            pltpu.VMEM((width, 2 * width), BF16),
-            pltpu.VMEM((n_taps + 1, 8, width), F32),
-            pltpu.VMEM((small_rows, width), F32),
-        ],
-        14,
-        2 * rows * width * width * 8,
-    )(
-        place, sums, w_value, text_emb, teacher, pool_query, resid, act, slope,
-        glu, normed, sig, gate_slope, w_out, kernel,
-    )
+        [pltpu.VMEM((rows, 2 * width), BF16), pltpu.VMEM((width, 2 * width), BF16)],
+        8,
+        2 * rows * width * width * 40,
+    )(place, dconv, dresid, act, normed, sig, gate_slope, kernel, episode)
 
     light = functools.partial(call, scratch=[], flops=2**20, placed=False)
-    got = lax.ppermute(other, "ep", [(i, i ^ 1) for i in range(n_ep)])
+    other, share = lax.optimization_barrier((other, share))
+    swap = [(i, i ^ 1) for i in range(n_ep)]
+    got = lax.ppermute(other, "ep", swap)
+    share = jnp.sum(share, axis=0)
+    got_share = lax.ppermute(share, "ep", swap)
     (total,) = light(
-        functools.partial(cores_kernel, big, half),
-        [shape((n_y, big + half + 2 * size + 8, LANES), BF16)],
-        n_args=2,
-    )(mine, got)
+        functools.partial(cores_kernel, big, size),
+        [shape((n_y, big + 16 + 2 * size, LANES), BF16)],
+        n_args=4,
+    )(mine, got, share, got_share)
     groups = [[2 * y + c for y in range(n_y)] for c in range(2)]
     got = lax.all_to_all(total, "ep", 0, 0, axis_index_groups=groups)
     (total,) = light(
-        functools.partial(rows_kernel, big, half),
-        [shape((n_seq, big // n_seq + half, LANES), BF16)],
+        functools.partial(rows_kernel, big),
+        [shape((n_seq, big // n_seq + 16, LANES), BF16)],
         n_args=1,
     )(got)
     grad_value, loss = light(
-        functools.partial(value_kernel, big, half),
+        functools.partial(value_kernel, big),
         [shape((width, width), F32), shape((1, LANES), F32)],
         n_args=1,
     )(got)
     loss = loss[0, 0]
     got = lax.all_to_all(total, "seq", 0, 0)
-    grad_in, grad_out, share = light(
+    grad_in, grad_out, grad_kernel, grad_query = light(
         owner_kernel,
         [
             shape((width // n_seq, 2 * width // n_ep), F32),
             shape((width // n_seq, width // n_ep), F32),
-            shape((n_ep, half, LANES), F32),
+            shape((n_taps, width), F32),
+            shape((n_heads, width), F32),
         ],
         n_args=1,
-    )(got)
-    got = lax.all_to_all(share, "ep", 0, 0)
-    grad_kernel, grad_query = light(
-        last_kernel, [shape((n_taps, width), F32), shape((n_heads, width), F32)], n_args=1
     )(got)
     return (loss, grad_in, grad_out, grad_kernel, grad_query, grad_value)
 

time: 120 us -> 126 us (1.050); the launches traced: 118 us -> 125 us
  blocking collectives: 68.6 us -> 49.5 us
  starting transfers between devices: 10.7 us -> 21.2 us
  waiting for transfers between devices: 5.45 us -> 13.8 us
  local copies, waits for them, and re-layouts: 3.18 us -> 9.05 us
  Pallas kernels: 28.5 us -> 30.2 us
    all_to_all x1 -> x0, blocking collectives: 18.9 us -> none  [shards(): got = lax.all_to_all(total, 'seq', 0, 0)]
    all_to_all x1 -> x2, starting transfers between devices: 4.73 us -> 14.7 us  [the longest x1 9.78 us: shards(): got = lax.all_to_all(total, 'seq', 0, 0)]
    all_to_all x1 -> x2, waiting for transfers between devices: 3.07 us -> 12 us  [the longest x1 12 us: shards(): got = lax.all_to_all(total, 'seq', 0, 0)]
    unnamed x16 -> x32, local copies, waits for them, and re-layouts: 2.37 us -> 8.24 us
    pallas_call x5, Pallas kernels: 17 us -> 18.7 us  [the longest x1 9.12 us: shards(): call(middle_kernel, [shape((n_seq, 8, LANES), F32), shape((size, LANES),...]
  transfers between devices with their start and end apart: 4 -> 6, of which waited for: 2 -> 2; matrix products, arithmetic and copies ran while one was open for 0% -> 0% of each run, Pallas kernels for 3% -> 8%
where the time goes in v5:
time: 126 us; the launch traced here: 125 us
  blocking collectives  49.5 us (39%)
  Pallas kernels  30.2 us (24%)
  starting transfers between devices  21.2 us (17%)
  waiting for transfers between devices  13.8 us (11%)
  local copies, waits for them, and re-layouts  9.05 us (7%)
  between operations  1.52 us (1%)
    all_to_all x1, blocking collectives, shards(): sums = lax.all_to_all(sums, 'seq', 0, 0)  32.6 us
    all_to_all x1, blocking collectives, shards(): got = lax.all_to_all(total, 'ep', 0, 0, axis_index_groups=groups)  16.9 us
    all_to_all x1, waiting for transfers between devices, shards(): got = lax.all_to_all(total, 'seq', 0, 0)  12 us
    all_to_all x1, starting transfers between devices, shards(): got = lax.all_to_all(total, 'seq', 0, 0)  9.78 us
    pallas_call x1, Pallas kernels, shards(): call(middle_kernel, [shape((n_seq, 8, LANES), F32), shape((size, LANES),...  9.12 us
    pallas_call x1, Pallas kernels, shards(): call(forward_kernel, [shape((whole, width), BF16), shape((wide, width), B...  8.78 us
    unnamed x32, local copies, waits for them, and re-layouts  8.24 us
    pallas_call x1, Pallas kernels, shards(): call(backward_kernel, [payload, payload], [pltpu.VMEM((rows, 2 * width),...  7.23 us
  transfers between devices with their start and end apart: 6, of which 2 were waited for; matrix products, arithmetic and copies ran while one was open for 0% of the time, Pallas kernels for 8%

profile of v5, /device:TPU:8, one launch (start us, length us, event | category | flops | bytes accessed | tf_op | source)
XLA Modules:
  0.0 125.4 jit_solution(8351325755034692613)
XLA Ops:
  0.7 0.8 slice_bitcast_fusion
  1.5 1.3 %collective-permute-start.1 = (bf16[32,512]{1,0:T(8,128)(2,1)S(1)}, bf16[32,512]{1,0:T(8,128)(2,1)S(1)}, u32[]{:S(2)}, u32[]{:S(2)}) collective-permute-start(bf16[32,512]{1,0:T(8,128)(2,1)S(1)} %get-tuple-element.52), channel_id=1, source_target_pairs={{1,0},{2,1},{3,2},{4,3},{5,4},{6,5},{7,6},{8,7},{9,8},{10,9},{11,1... | collective-permute-start | bytes 98312 | tf_op jit(solution)/shard_map/ppermute | solution.py:430
  2.8 4.5 %collective-permute-start = (bf16[32,512]{1,0:T(8,128)(2,1)S(1)}, bf16[32,512]{1,0:T(8,128)(2,1)S(1)}, u32[]{:S(2)}, u32[]{:S(2)}) collective-permute-start(bf16[32,512]{1,0:T(8,128)(2,1)S(1)} %get-tuple-element.53), channel_id=1, source_target_pairs={{0,1},{1,2},{2,3},{3,4},{4,5},{5,6},{6,7},{7,8},{8,9},{9,10},{10,1... | collective-permute-start | bytes 98312 | tf_op jit(solution)/shard_map/ppermute | solution.py:429
  8.0 0.1 pad_add_fusion.place
  8.0 1.1 copy-done
  9.2 1.2 copy-done.1
  10.4 2.0 %shard_map.136 = (bf16[704,512]{1,0:T(8,128)(2,1)S(1)}, bf16[704,512]{1,0:T(8,128)(2,1)S(1)}, bf16[704,512]{1,0:T(8,128)(2,1)S(1)}, bf16[704,512]{1,0:T(8,128)(2,1)S(1)}) custom-call(s32[3]{0:T(128)S(1)} %pad_add_fusion.place, bf16[704,512]{1,0:T(8,128)(2,1)S(1)} %bitcast.9, bf16[512,1024]{1,0:T(8,128)(2,1)S(1)} %copy-done.1), custom_call_target="tpu_custom_call" | custom-call | flops 738197504 | bytes 8388608 | tf_op jit(solution)/shard_map/pallas_call | solution.py:435
  12.4 0.0 collective-permute-done.1.high_ref
  12.5 0.0 copy-start.3
  12.5 0.0 copy-start.4
  12.5 0.0 copy-start.7
  12.5 8.8 %shard_map.137 = (bf16[768,512]{1,0:T(8,128)(2,1)S(1)}, bf16[736,512]{1,0:T(8,128)(2,1)S(1)}, bf16[736,512]{1,0:T(8,128)(2,1)S(1)}, f32[736,512]{1,0:T(8,128)S(1)}, f32[32,8,640]{2,1,0:T(8,128)S(1)}) custom-call(s32[3]{0:T(128)S(1)} %pad_add_fusion.place, bf16[32,512]{1,0:T(8,128)(2,1)S(1)} %collective-permute-done.low_ref, ...), custom_call_target="tpu_custom_call" | custom-call | flops 1476395008 | bytes 8388608 | tf_op jit(solution)/shard_map/pallas_call | solution.py:438
  21.3 0.0 copy-start.14
  21.3 32.6 %all_to_all.20.sums_ref = f32[32,8,640]{2,1,0:T(8,128)S(1)} all-to-all(f32[32,8,640]{2,1,0:T(8,128)S(1)} %get-tuple-element.30), channel_id=1, replica_groups=mesh['ep'=8,'seq'=32] {'seq'}, dimensions={0} | all-to-all | bytes 1310720 | tf_op jit(solution)/shard_map/all_to_all | solution.py:451
  54.0 9.1 %shard_map.138 = (f32[32,8,128]{2,1,0:T(8,128)}, f32[40,128]{1,0:T(8,128)S(1)}, bf16[736,512]{1,0:T(8,128)(2,1)S(1)}, f32[736,512]{1,0:T(8,128)S(1)}) custom-call(s32[3]{0:T(128)S(1)} %pad_add_fusion.place, f32[32,8,640]{2,1,0:T(8,128)S(1)} %all_to_all.20.sums_ref, bf16[512,512]{1,0:T(8,128)(2,1)S(1)} %copy-done.3, bf16[256,512]{1,0:T(8,128)(2,1)S(1)} %copy-done.4, ...), custom_call_target="tpu_custom_call" | custom-call | flops 1476395008 | bytes 8388608 | tf_op jit(solution)/shard_map/pallas_call | solution.py:456
  63.1 1.1 copy-done.8
  64.2 5.0 %all-to-all-start.1 = ((f32[32,8,128]{2,1,0:T(8,128)}), f32[32,8,128]{2,1,0:T(8,128)S(1)}, u32[]{:S(2)}, u32[]{:S(2)}) async-start(f32[32,8,128]{2,1,0:T(8,128)} %get-tuple-element.43), calls=%async_computation.1 | async-start | bytes 262144 | tf_op jit(solution)/shard_map/all_to_all | solution.py:469
  69.2 1.4 %copy-done.9 = f32[736,512]{1,0:T(8,128)S(1)} copy-done((f32[736,512]{1,0:T(8,128)S(1)}, f32[736,512]{1,0:T(8,128)}, u32[]{:S(2)}) %copy-start.9) | copy-done | bytes 1507352
  70.6 1.1 copy-done.11
  71.7 1.1 copy-done.13
  72.8 1.1 copy-done.15
  74.0 7.2 %shard_map.139 = (bf16[4,816,128]{2,1,0:T(8,128)(2,1)S(1)}, bf16[4,816,128]{2,1,0:T(8,128)(2,1)S(1)}) custom-call(s32[3]{0:T(128)S(1)} %pad_add_fusion.place, f32[736,512]{1,0:T(8,128)S(1)} %copy-done.9, bf16[736,512]{1,0:T(8,128)(2,1)S(1)} %get-tuple-element.35.dresid_ref, bf16[736,512]{1,0:T(8,128)(2,1)S(1)} %copy-done.15, ...), custom_call_target="tpu_custom_call" | custom-call | flops 14763950080 | bytes 8388608 | tf_op jit(solution)/shard_map/pallas_call | solution.py:472
  81.2 0.1 collective-permute-start.2
  81.3 0.6 collective-permute-start.3
  81.9 1.7 %collective-permute-done.3.got_share_ref = f32[8,128]{1,0:T(8,128)S(1)} collective-permute-done((f32[8,128]{1,0:T(8,128)S(1)}, f32[8,128]{1,0:T(8,128)S(1)}, u32[]{:S(2)}, u32[]{:S(2)}) %collective-permute-start.3) | collective-permute-done | bytes 4128 | tf_op jit(solution)/shard_map/ppermute | solution.py:485
  83.7 0.2 shard_map.140
  83.8 16.9 %all_to_all.21.got_ref = bf16[4,864,128]{2,1,0:T(8,128)(2,1)S(1)} all-to-all(bf16[4,864,128]{2,1,0:T(8,128)(2,1)S(1)} %shard_map.140), channel_id=1, replica_groups={{0,64,128,192},{32,96,160,224},{1,65,129,193},{33,97,161,225},{2,66,130..., dimensions={0} | all-to-all | bytes 1769472 | tf_op jit(solution)/shard_map/all_to_all | solution.py:492
  100.7 0.8 shard_map.142
  101.6 9.8 %all-to-all-start.3 = ((bf16[32,40,128]{2,1,0:T(8,128)(2,1)}), bf16[32,40,128]{2,1,0:T(8,128)(2,1)S(1)}, u32[]{:S(2)}, u32[]{:S(2)}) async-start(bf16[32,40,128]{2,1,0:T(8,128)(2,1)} %shard_map.142), calls=%async_computation.3 | async-start | bytes 655360 | tf_op jit(solution)/shard_map/all_to_all | solution.py:504
  111.4 1.3 %shard_map.141 = (f32[512,512]{1,0:T(8,128)}, f32[1,128]{1,0:T(1,128)}) custom-call(bf16[4,864,128]{2,1,0:T(8,128)(2,1)S(1)} %all_to_all.21.got_ref), custom_call_target="tpu_custom_call" | custom-call | flops 1048576 | bytes 8388608 | tf_op jit(solution)/shard_map/pallas_call | solution.py:498
  112.7 12.0 %all-to-all-done.3.got_ref = bf16[32,40,128]{2,1,0:T(8,128)(2,1)S(1)} async-done(((bf16[32,40,128]{2,1,0:T(8,128)(2,1)}), bf16[32,40,128]{2,1,0:T(8,128)(2,1)S(1)}, u32[]{:S(2)}, u32[]{:S(2)}) %all-to-all-start.3) | async-done | bytes 327712 | tf_op jit(solution)/shard_map/all_to_all | solution.py:504
  124.7 0.7 shard_map.143
  (25 shorter events, 0.1 us)
Async XLA Ops:
  0.6 11.8 %copy-start.6 = (bf16[8,512]{1,0:T(8,128)(2,1)S(1)}, bf16[8,512]{1,0:T(8,128)(2,1)}, u32[]{:S(2)}) copy-start(bf16[8,512]{1,0:T(8,128)(2,1)} %query_ref.3) | copy-start | bytes 24580
  0.6 11.8 %copy-start.5 = (f32[31,512]{1,0:T(8,128)S(1)}, f32[31,512]{1,0:T(8,128)}, u32[]{:S(2)}) copy-start(f32[31,512]{1,0:T(8,128)} %taps_ref.3) | copy-start | bytes 190468
  1.5 10.9 %collective-permute-start.1 = (bf16[32,512]{1,0:T(8,128)(2,1)S(1)}, bf16[32,512]{1,0:T(8,128)(2,1)S(1)}, u32[]{:S(2)}, u32[]{:S(2)}) collective-permute-start(bf16[32,512]{1,0:T(8,128)(2,1)S(1)} %get-tuple-element.52), channel_id=1, source_target_pairs={{1,0},{2,1},{3,2},{4,3},{5,4},{6,5},{7,6},{8,7},{9,8},{10,9},{11,1... | collective-permute-start | bytes 98312 | tf_op jit(solution)/shard_map/ppermute | solution.py:430
  2.8 9.7 %collective-permute-start = (bf16[32,512]{1,0:T(8,128)(2,1)S(1)}, bf16[32,512]{1,0:T(8,128)(2,1)S(1)}, u32[]{:S(2)}, u32[]{:S(2)}) collective-permute-start(bf16[32,512]{1,0:T(8,128)(2,1)S(1)} %get-tuple-element.53), channel_id=1, source_target_pairs={{0,1},{1,2},{2,3},{3,4},{4,5},{5,6},{6,7},{7,8},{8,9},{9,10},{10,1... | collective-permute-start | bytes 98312 | tf_op jit(solution)/shard_map/ppermute | solution.py:429
  8.0 1.1 copy-start
  9.2 1.2 copy-start.1
  10.4 2.1 %copy-start.2 = (bf16[512,512]{1,0:T(8,128)(2,1)S(1)}, bf16[512,512]{1,0:T(8,128)(2,1)}, u32[]{:S(2)}) copy-start(bf16[512,512]{1,0:T(8,128)(2,1)} %w_out_ref.3) | copy-start | bytes 1572868
  12.4 8.9 %copy-start.10 = (bf16[704,512]{1,0:T(8,128)(2,1)}, bf16[704,512]{1,0:T(8,128)(2,1)S(1)}, u32[]{:S(2)}) copy-start(bf16[704,512]{1,0:T(8,128)(2,1)S(1)} %get-tuple-element.38.sig_ref) | copy-start | bytes 2162692
  12.4 8.9 %copy-start.12 = (bf16[704,512]{1,0:T(8,128)(2,1)}, bf16[704,512]{1,0:T(8,128)(2,1)S(1)}, u32[]{:S(2)}) copy-start(bf16[704,512]{1,0:T(8,128)(2,1)S(1)} %get-tuple-element.39.gate_slope_ref) | copy-start | bytes 2162692
  12.5 41.5 %copy-start.3 = (bf16[512,512]{1,0:T(8,128)(2,1)S(1)}, bf16[512,512]{1,0:T(8,128)(2,1)}, u32[]{:S(2)}) copy-start(bf16[512,512]{1,0:T(8,128)(2,1)} %w_value_ref.1) | copy-start | bytes 1572868
  12.5 41.5 %copy-start.4 = (bf16[256,512]{1,0:T(8,128)(2,1)S(1)}, bf16[256,512]{1,0:T(8,128)(2,1)}, u32[]{:S(2)}) copy-start(bf16[256,512]{1,0:T(8,128)(2,1)} %text_ref.1) | copy-start | bytes 786436
  12.5 41.5 %copy-start.7 = (f32[1,256]{1,0:T(1,128)S(1)}, f32[1,256]{1,0:T(1,128)}, u32[]{:S(2)}) copy-start(f32[1,256]{1,0:T(1,128)} %teacher_ref.1) | copy-start | bytes 3076
  21.3 32.7 %copy-start.14 = (bf16[736,512]{1,0:T(8,128)(2,1)}, bf16[736,512]{1,0:T(8,128)(2,1)S(1)}, u32[]{:S(2)}) copy-start(bf16[736,512]{1,0:T(8,128)(2,1)S(1)} %get-tuple-element.36.act_ref) | copy-start | bytes 2260996
  63.1 1.1 copy-start.8
  64.2 16.9 %all-to-all-start.1 = ((f32[32,8,128]{2,1,0:T(8,128)}), f32[32,8,128]{2,1,0:T(8,128)S(1)}, u32[]{:S(2)}, u32[]{:S(2)}) async-start(f32[32,8,128]{2,1,0:T(8,128)} %get-tuple-element.43), calls=%async_computation.1 | async-start | bytes 262144 | tf_op jit(solution)/shard_map/all_to_all | solution.py:469
  69.2 1.4 %copy-start.9 = (f32[736,512]{1,0:T(8,128)S(1)}, f32[736,512]{1,0:T(8,128)}, u32[]{:S(2)}) copy-start(f32[736,512]{1,0:T(8,128)} %copy-done.8) | copy-start | bytes 4521988
  70.6 1.1 copy-start.11
  71.7 1.1 copy-start.13
  72.8 1.1 copy-start.15
  81.2 2.5 %collective-permute-start.2 = (bf16[4,816,128]{2,1,0:T(8,128)(2,1)S(1)}, bf16[4,816,128]{2,1,0:T(8,128)(2,1)S(1)}, u32[]{:S(2)}, u32[]{:S(2)}) collective-permute-start(bf16[4,816,128]{2,1,0:T(8,128)(2,1)S(1)} %get-tuple-element.44), channel_id=1, source_target_pairs={{0,32},{32,0},{64,96},{96,64},{128,160},{160,128},{192,224},{224,1... | collective-permute-start | bytes 2506760 | tf_op jit(solution)/shard_map/ppermute | solution.py:483
  81.3 2.3 %collective-permute-start.3 = (f32[8,128]{1,0:T(8,128)S(1)}, f32[8,128]{1,0:T(8,128)S(1)}, u32[]{:S(2)}, u32[]{:S(2)}) collective-permute-start(f32[8,128]{1,0:T(8,128)S(1)} %reduce_sum.9.share_ref), channel_id=1, source_target_pairs={{0,32},{32,0},{64,96},{96,64},{128,160},{160,128},{192,224},{224,1... | collective-permute-start | bytes 12296 | tf_op jit(solution)/shard_map/ppermute | solution.py:485
  101.6 23.1 %all-to-all-start.3 = ((bf16[32,40,128]{2,1,0:T(8,128)(2,1)}), bf16[32,40,128]{2,1,0:T(8,128)(2,1)S(1)}, u32[]{:S(2)}, u32[]{:S(2)}) async-start(bf16[32,40,128]{2,1,0:T(8,128)(2,1)} %shard_map.142), calls=%async_computation.3 | async-start | bytes 655360 | tf_op jit(solution)/shard_map/all_to_all | solution.py:504

commit v6 on v4

--- a/solution.py
+++ b/solution.py
@@ -413,10 +413,13 @@
     wide, whole = rows + 2 * SIDE, rows + 2 * STEP
     shape = jax.ShapeDtypeStruct
 
-    forward = [(i, i + 1) for i in range(n_seq - 1)]
-    backward = [(target, source) for source, target in forward]
-    low = lax.ppermute(x[rows - STEP :], "seq", forward)
-    high = lax.ppermute(x[:STEP], "seq", backward)
+    odd = lax.axis_index("seq") % 2 == 1
+    near = [(i, i ^ 1) for i in range(n_seq)]
+    far = [(i, (i + 1) % n_seq if i % 2 else (i - 1) % n_seq) for i in range(n_seq)]
+    first, last = x[:STEP], x[rows - STEP :]
+    inner = lax.ppermute(jnp.where(odd, first, last), "seq", near)
+    outer = lax.ppermute(jnp.where(odd, last, first), "seq", far)
+    low, high = jnp.where(odd, inner, outer), jnp.where(odd, outer, inner)
     core = lax.axis_index("ep") % 2
     place = jnp.stack([lax.axis_index("seq") * rows, lengths[0], core]).astype(jnp.int32)
 

time: 120 us -> 115 us (0.958)
  blocking collectives: 68.6 us -> 60.8 us
  starting transfers between devices: 10.7 us -> 13 us
    all_to_all x1, blocking collectives: 32.6 us -> 24.9 us  [shards(): sums = lax.all_to_all(sums, 'seq', 0, 0)]
    ppermute x2, starting transfers between devices: 5.83 us -> 8.13 us  [the longest x1 8.13 us: shards(): outer = lax.ppermute(jnp.where(odd, last, first), 'seq', far)]
where the time goes in v6:
time: 115 us; the launch traced here: 112 us
  blocking collectives  60.8 us (53%)
  Pallas kernels  28.5 us (25%)
  starting transfers between devices  13 us (11%)
  waiting for transfers between devices  5.45 us (5%)
  local copies, waits for them, and re-layouts  2.37 us (2%)
  between operations  1.44 us (1%)
    all_to_all x1, blocking collectives, shards(): sums = lax.all_to_all(sums, 'seq', 0, 0)  24.9 us
    all_to_all x1, blocking collectives, shards(): got = lax.all_to_all(total, 'seq', 0, 0)  18.9 us
    all_to_all x1, blocking collectives, shards(): got = lax.all_to_all(total, 'ep', 0, 0, axis_index_groups=groups)  17.1 us
    pallas_call x1, Pallas kernels, shards(): call(backward_kernel, [payload, payload], [pltpu.VMEM((wide, width), F32)...  14.7 us
    pallas_call x1, Pallas kernels, shards(): call(forward_kernel, [shape((whole, width), BF16), shape((wide, width), B...  8.78 us
    ppermute x1, starting transfers between devices, shards(): outer = lax.ppermute(jnp.where(odd, last, first), 'seq', far)  8.13 us
    all_to_all x1, starting transfers between devices, shards(): got = lax.all_to_all(share, 'ep', 0, 0)  4.73 us
    all_to_all x1, waiting for transfers between devices, shards(): got = lax.all_to_all(share, 'ep', 0, 0)  3.07 us
  transfers between devices with their start and end apart: 4, of which 2 were waited for; matrix products, arithmetic and copies ran while one was open for 0% of the time, Pallas kernels for 3%

profile of v6, /device:TPU:8, one launch (start us, length us, event | category | flops | bytes accessed | tf_op | source)
XLA Modules:
  0.0 112.5 jit_solution(17109424638163922936)
XLA Ops:
  0.6 0.0 copy-start.5
  0.7 0.0 copy-start.6
  0.7 0.8 select_bitcast_fusion
  1.5 8.1 %collective-permute-start.1 = (bf16[32,512]{1,0:T(8,128)(2,1)S(1)}, bf16[32,512]{1,0:T(8,128)(2,1)S(1)}, u32[]{:S(2)}, u32[]{:S(2)}) collective-permute-start(bf16[32,512]{1,0:T(8,128)(2,1)S(1)} %get-tuple-element.42), channel_id=1, source_target_pairs={{0,31},{1,2},{2,1},{3,4},{4,3},{5,6},{6,5},{7,8},{8,7},{9,10},{10,... | collective-permute-start | bytes 98312 | tf_op jit(solution)/shard_map/ppermute | solution.py:421
  9.6 0.0 collective-permute-start
  10.3 0.1 pad_add_fusion.place
  10.3 1.1 copy-done
  11.5 1.2 %copy-done.1 = bf16[512,1024]{1,0:T(8,128)(2,1)S(1)} copy-done((bf16[512,1024]{1,0:T(8,128)(2,1)S(1)}, bf16[512,1024]{1,0:T(8,128)(2,1)}, u32[]{:S(2)}) %copy-start.1) | copy-done | bytes 1048600
  12.7 2.0 %shard_map.136 = (bf16[704,512]{1,0:T(8,128)(2,1)S(1)}, bf16[704,512]{1,0:T(8,128)(2,1)S(1)}, bf16[704,512]{1,0:T(8,128)(2,1)S(1)}, bf16[704,512]{1,0:T(8,128)(2,1)S(1)}) custom-call(s32[3]{0:T(128)S(1)} %pad_add_fusion.place, bf16[704,512]{1,0:T(8,128)(2,1)S(1)} %bitcast.9, bf16[512,1024]{1,0:T(8,128)(2,1)S(1)} %copy-done.1), custom_call_target="tpu_custom_call" | custom-call | flops 738197504 | bytes 8388608 | tf_op jit(solution)/shard_map/pallas_call | solution.py:427
  14.7 0.0 collective-permute-done.1
  14.7 0.0 collective-permute-done
  14.7 0.0 copy-done.5
  14.8 0.0 copy-done.6
  14.8 0.0 copy-done.2
  14.8 0.0 copy-start.3
  14.8 0.0 copy-start.4
  14.8 0.0 copy-start.7
  14.8 8.8 %shard_map.137 = (bf16[768,512]{1,0:T(8,128)(2,1)S(1)}, bf16[736,512]{1,0:T(8,128)(2,1)S(1)}, bf16[736,512]{1,0:T(8,128)(2,1)S(1)}, f32[736,512]{1,0:T(8,128)S(1)}, f32[32,8,640]{2,1,0:T(8,128)S(1)}) custom-call(s32[3]{0:T(128)S(1)} %pad_add_fusion.place, bf16[32,512]{1,0:T(8,128)(2,1)S(1)} %get-tuple-element.45.low_ref, ...), custom_call_target="tpu_custom_call" | custom-call | flops 1476395008 | bytes 8388608 | tf_op jit(solution)/shard_map/pallas_call | solution.py:430
  23.6 24.9 %all_to_all.20.sums_ref = f32[32,8,640]{2,1,0:T(8,128)S(1)} all-to-all(f32[32,8,640]{2,1,0:T(8,128)S(1)} %get-tuple-element.25), channel_id=1, replica_groups=mesh['ep'=8,'seq'=32] {'seq'}, dimensions={0} | all-to-all | bytes 1310720 | tf_op jit(solution)/shard_map/all_to_all | solution.py:443
  48.5 0.0 copy-done.3
  48.5 14.7 %shard_map.138 = (bf16[4,832,128]{2,1,0:T(8,128)(2,1)S(1)}, bf16[4,832,128]{2,1,0:T(8,128)(2,1)S(1)}) custom-call(s32[3]{0:T(128)S(1)} %pad_add_fusion.place, f32[32,8,640]{2,1,0:T(8,128)S(1)} %all_to_all.20.sums_ref, bf16[512,512]{1,0:T(8,128)(2,1)S(1)} %copy-done.3, bf16[256,512]{1,0:T(8,128)(2,1)S(1)} %copy-done.4, f32[1,256]{1,0:T(1,128)S(1)} %copy-done.7, ...), custom_call_target="tpu_custom_call" | custom-call | flops 2952790016 | bytes 8388608 | tf_op jit(solution)/shard_map/pallas_call | solution.py:451
  63.2 0.1 collective-permute-start.2
  63.3 2.4 %collective-permute-done.2.got_ref = bf16[4,832,128]{2,1,0:T(8,128)(2,1)S(1)} collective-permute-done((bf16[4,832,128]{2,1,0:T(8,128)(2,1)S(1)}, bf16[4,832,128]{2,1,0:T(8,128)(2,1)S(1)}, u32[]{:S(2)}, u32[]{:S(2)}) %collective-permute-start.2) | collective-permute-done | bytes 852000 | tf_op jit(solution)/shard_map/ppermute | solution.py:471
  65.7 0.2 shard_map.139
  65.9 17.1 %all_to_all.21.got_ref = bf16[4,880,128]{2,1,0:T(8,128)(2,1)S(1)} all-to-all(bf16[4,880,128]{2,1,0:T(8,128)(2,1)S(1)} %shard_map.139), channel_id=1, replica_groups={{0,64,128,192},{32,96,160,224},{1,65,129,193},{33,97,161,225},{2,66,130..., dimensions={0} | all-to-all | bytes 1802240 | tf_op jit(solution)/shard_map/all_to_all | solution.py:478
  83.0 0.1 shard_map.141
  83.1 18.9 %all_to_all.22.got_ref = bf16[32,48,128]{2,1,0:T(8,128)(2,1)S(1)} all-to-all(bf16[32,48,128]{2,1,0:T(8,128)(2,1)S(1)} %shard_map.141), channel_id=1, replica_groups=mesh['ep'=8,'seq'=32] {'seq'}, dimensions={0} | all-to-all | bytes 786432 | tf_op jit(solution)/shard_map/all_to_all | solution.py:490
  102.0 0.8 shard_map.142
  102.7 4.7 %all-to-all-start.3 = ((f32[8,24,128]{2,1,0:T(8,128)}), f32[8,24,128]{2,1,0:T(8,128)S(1)}, u32[]{:S(2)}, u32[]{:S(2)}) async-start(f32[8,24,128]{2,1,0:T(8,128)} %get-tuple-element.38), calls=%async_computation.3 | async-start | bytes 196608 | tf_op jit(solution)/shard_map/all_to_all | solution.py:500
  107.5 1.3 %shard_map.140 = (f32[512,512]{1,0:T(8,128)}, f32[1,128]{1,0:T(1,128)}) custom-call(bf16[4,880,128]{2,1,0:T(8,128)(2,1)S(1)} %all_to_all.21.got_ref), custom_call_target="tpu_custom_call" | custom-call | flops 1048576 | bytes 8388608 | tf_op jit(solution)/shard_map/pallas_call | solution.py:484
  108.8 3.1 %all-to-all-done.3.got_ref = f32[8,24,128]{2,1,0:T(8,128)S(1)} async-done(((f32[8,24,128]{2,1,0:T(8,128)}), f32[8,24,128]{2,1,0:T(8,128)S(1)}, u32[]{:S(2)}, u32[]{:S(2)}) %all-to-all-start.3) | async-done | bytes 98336 | tf_op jit(solution)/shard_map/all_to_all | solution.py:500
  111.8 0.6 shard_map.143
  (6 shorter events, 0.0 us)
Async XLA Ops:
  0.6 14.1 %copy-start.5 = (f32[31,512]{1,0:T(8,128)S(1)}, f32[31,512]{1,0:T(8,128)}, u32[]{:S(2)}) copy-start(f32[31,512]{1,0:T(8,128)} %taps_ref.3) | copy-start | bytes 190468
  0.7 14.1 %copy-start.6 = (bf16[8,512]{1,0:T(8,128)(2,1)S(1)}, bf16[8,512]{1,0:T(8,128)(2,1)}, u32[]{:S(2)}) copy-start(bf16[8,512]{1,0:T(8,128)(2,1)} %query_ref.3) | copy-start | bytes 24580
  1.5 13.2 %collective-permute-start.1 = (bf16[32,512]{1,0:T(8,128)(2,1)S(1)}, bf16[32,512]{1,0:T(8,128)(2,1)S(1)}, u32[]{:S(2)}, u32[]{:S(2)}) collective-permute-start(bf16[32,512]{1,0:T(8,128)(2,1)S(1)} %get-tuple-element.42), channel_id=1, source_target_pairs={{0,31},{1,2},{2,1},{3,4},{4,3},{5,6},{6,5},{7,8},{8,7},{9,10},{10,... | collective-permute-start | bytes 98312 | tf_op jit(solution)/shard_map/ppermute | solution.py:421
  9.6 5.1 %collective-permute-start = (bf16[32,512]{1,0:T(8,128)(2,1)S(1)}, bf16[32,512]{1,0:T(8,128)(2,1)S(1)}, u32[]{:S(2)}, u32[]{:S(2)}) collective-permute-start(bf16[32,512]{1,0:T(8,128)(2,1)S(1)} %get-tuple-element.43), channel_id=1, source_target_pairs={{0,1},{1,0},{2,3},{3,2},{4,5},{5,4},{6,7},{7,6},{8,9},{9,8},{10,11... | collective-permute-start | bytes 98312 | tf_op jit(solution)/shard_map/ppermute | solution.py:420
  10.3 1.1 copy-start
  11.5 1.2 %copy-start.1 = (bf16[512,1024]{1,0:T(8,128)(2,1)S(1)}, bf16[512,1024]{1,0:T(8,128)(2,1)}, u32[]{:S(2)}) copy-start(bf16[512,1024]{1,0:T(8,128)(2,1)} %w_in_ref.3) | copy-start | bytes 3145732
  12.7 2.1 %copy-start.2 = (bf16[512,512]{1,0:T(8,128)(2,1)S(1)}, bf16[512,512]{1,0:T(8,128)(2,1)}, u32[]{:S(2)}) copy-start(bf16[512,512]{1,0:T(8,128)(2,1)} %w_out_ref.3) | copy-start | bytes 1572868
  14.8 33.7 %copy-start.3 = (bf16[512,512]{1,0:T(8,128)(2,1)S(1)}, bf16[512,512]{1,0:T(8,128)(2,1)}, u32[]{:S(2)}) copy-start(bf16[512,512]{1,0:T(8,128)(2,1)} %w_value_ref.1) | copy-start | bytes 1572868
  14.8 33.7 %copy-start.4 = (bf16[256,512]{1,0:T(8,128)(2,1)S(1)}, bf16[256,512]{1,0:T(8,128)(2,1)}, u32[]{:S(2)}) copy-start(bf16[256,512]{1,0:T(8,128)(2,1)} %text_ref.1) | copy-start | bytes 786436
  14.8 33.7 %copy-start.7 = (f32[1,256]{1,0:T(1,128)S(1)}, f32[1,256]{1,0:T(1,128)}, u32[]{:S(2)}) copy-start(f32[1,256]{1,0:T(1,128)} %teacher_ref.1) | copy-start | bytes 3076
  63.2 2.5 %collective-permute-start.2 = (bf16[4,832,128]{2,1,0:T(8,128)(2,1)S(1)}, bf16[4,832,128]{2,1,0:T(8,128)(2,1)S(1)}, u32[]{:S(2)}, u32[]{:S(2)}) collective-permute-start(bf16[4,832,128]{2,1,0:T(8,128)(2,1)S(1)} %get-tuple-element.34), channel_id=1, source_target_pairs={{0,32},{32,0},{64,96},{96,64},{128,160},{160,128},{192,224},{224,1... | collective-permute-start | bytes 2555912 | tf_op jit(solution)/shard_map/ppermute | solution.py:471
  102.7 9.1 %all-to-all-start.3 = ((f32[8,24,128]{2,1,0:T(8,128)}), f32[8,24,128]{2,1,0:T(8,128)S(1)}, u32[]{:S(2)}, u32[]{:S(2)}) async-start(f32[8,24,128]{2,1,0:T(8,128)} %get-tuple-element.38), calls=%async_computation.3 | async-start | bytes 196608 | tf_op jit(solution)/shard_map/all_to_all | solution.py:500

commit v7 on v4

--- a/solution.py
+++ b/solution.py
@@ -70,6 +70,13 @@
 def row_mask(first, rows, length):
     at = first + lax.broadcasted_iota(jnp.int32, (rows, 1), 0)
     return (at >= 0) & (at < length)
+
+
+def ends_kernel(place, first_ref, last_ref, inner_ref, outer_ref):
+    odd = place[3] == 1
+    first, last = first_ref[...].astype(F32), last_ref[...].astype(F32)
+    inner_ref[...] = jnp.where(odd, first, last).astype(BF16)
+    outer_ref[...] = jnp.where(odd, last, first).astype(BF16)
 
 
 def project_kernel(place, x_ref, w_in_ref, normed_ref, sig_ref, slope_ref, glu_ref):
@@ -92,13 +99,17 @@
 
 
 def forward_kernel(
-    place, low_ref, high_ref, x_ref, own_glu_ref, w_in_ref, taps_ref, w_out_ref, query_ref,
+    place, inner_ref, outer_ref, x_ref, own_glu_ref, w_in_ref, taps_ref, w_out_ref, query_ref,
     glu_ref, act_ref, slope_ref, resid_ref, sums_ref, glu_f,
 ):
     rows, width = x_ref.shape
     wide = rows + 2 * SIDE
     n_taps = taps_ref.shape[0]
-    halo = jnp.concatenate([low_ref[...], high_ref[...]], axis=0)
+    odd = place[3] == 1
+    inner, outer = inner_ref[...].astype(F32), outer_ref[...].astype(F32)
+    halo = jnp.concatenate(
+        [jnp.where(odd, inner, outer), jnp.where(odd, outer, inner)], axis=0
+    )
     unused, gate, sig = gated(halo, w_in_ref[...], width)
     both = gate * sig
     valid_low = row_mask(place[0] - STEP, STEP, place[1])
@@ -127,8 +138,8 @@
             slope_ref[pl.ds(start, STEP), cols] = (s * (1.0 + acc * (1.0 - s))).astype(BF16)
 
     w_out = w_out_ref[...]
-    resid_ref[0:SIDE, :] = low_ref[STEP - SIDE :, :].astype(F32) + dot(act_ref[0:SIDE, :], w_out)
-    resid_ref[SIDE + rows :, :] = high_ref[0:SIDE, :].astype(F32) + dot(
+    resid_ref[0:SIDE, :] = halo[STEP - SIDE : STEP] + dot(act_ref[0:SIDE, :], w_out)
+    resid_ref[SIDE + rows :, :] = halo[STEP : STEP + SIDE] + dot(
         act_ref[SIDE + rows :, :], w_out
     )
     queries = jnp.concatenate([query_ref[...]] * (LANES // 8), axis=0)
@@ -413,12 +424,17 @@
     wide, whole = rows + 2 * SIDE, rows + 2 * STEP
     shape = jax.ShapeDtypeStruct
 
-    forward = [(i, i + 1) for i in range(n_seq - 1)]
-    backward = [(target, source) for source, target in forward]
-    low = lax.ppermute(x[rows - STEP :], "seq", forward)
-    high = lax.ppermute(x[:STEP], "seq", backward)
+    seq = lax.axis_index("seq")
+    odd = seq % 2
     core = lax.axis_index("ep") % 2
-    place = jnp.stack([lax.axis_index("seq") * rows, lengths[0], core]).astype(jnp.int32)
+    place = jnp.stack([seq * rows, lengths[0], core, odd]).astype(jnp.int32)
+    near = [(i, i ^ 1) for i in range(n_seq)]
+    far = [(i, (i + 1) % n_seq if i % 2 else (i - 1) % n_seq) for i in range(n_seq)]
+    inner, outer = call(ends_kernel, [shape((STEP, width), BF16)] * 2, [], 2, 2**16)(
+        place, x[:STEP], x[rows - STEP :]
+    )
+    inner = lax.ppermute(inner, "seq", near)
+    outer = lax.ppermute(outer, "seq", far)
 
     own = shape((rows, width), BF16)
     normed, sig, gate_slope, own_glu = call(
@@ -436,7 +452,7 @@
         [pltpu.VMEM((whole, width), F32)],
         8,
         2 * rows * width * width * 4,
-    )(place, low, high, x, own_glu, w_in, kernel, w_out, pool_query)
+    )(place, inner, outer, x, own_glu, w_in, kernel, w_out, pool_query)
     sums = lax.all_to_all(sums, "seq", 0, 0)
 
     small_rows = 48

time: 120 us -> 114 us (0.950)
  blocking collectives: 68.6 us -> 61.6 us
  starting transfers between devices: 10.7 us -> 13.8 us
  local copies, waits for them, and re-layouts: 3.18 us -> 0.83 us
    all_to_all x1, blocking collectives: 32.6 us -> 25.9 us  [shards(): sums = lax.all_to_all(sums, 'seq', 0, 0)]
    ppermute x2, starting transfers between devices: 5.83 us -> 8.97 us  [the longest x1 7.39 us: shards(): outer = lax.ppermute(outer, 'seq', far)]
    unnamed x16, local copies, waits for them, and re-layouts: 2.37 us -> 0.05 us
where the time goes in v7:
time: 114 us; the launch traced here: 112 us
  blocking collectives  61.6 us (54%)
  Pallas kernels  29.1 us (26%)
  starting transfers between devices  13.8 us (12%)
  waiting for transfers between devices  5.45 us (5%)
  between operations  1.57 us (1%)
    all_to_all x1, blocking collectives, shards(): sums = lax.all_to_all(sums, 'seq', 0, 0)  25.9 us
    all_to_all x1, blocking collectives, shards(): got = lax.all_to_all(total, 'seq', 0, 0)  18.6 us
    all_to_all x1, blocking collectives, shards(): got = lax.all_to_all(total, 'ep', 0, 0, axis_index_groups=groups)  17.1 us
    pallas_call x1, Pallas kernels, shards(): call(backward_kernel, [payload, payload], [pltpu.VMEM((wide, width), F32)...  14.8 us
    pallas_call x1, Pallas kernels, shards(): call(forward_kernel, [shape((whole, width), BF16), shape((wide, width), B...  8.79 us
    ppermute x1, starting transfers between devices, shards(): outer = lax.ppermute(outer, 'seq', far)  7.39 us
    all_to_all x1, starting transfers between devices, shards(): got = lax.all_to_all(share, 'ep', 0, 0)  4.73 us
    all_to_all x1, waiting for transfers between devices, shards(): got = lax.all_to_all(share, 'ep', 0, 0)  3.07 us
  transfers between devices with their start and end apart: 4, of which 2 were waited for; matrix products, arithmetic and copies ran while one was open for 0% of the time, Pallas kernels for 3%

profile of v7, /device:TPU:8, one launch (start us, length us, event | category | flops | bytes accessed | tf_op | source)
XLA Modules:
  0.0 112.4 jit_solution(9782918111829585553)
XLA Ops:
  0.6 0.0 copy-start
  0.6 0.0 copy-start.1
  1.4 0.8 slice_bitcast_fusion
  2.2 0.1 pad_add_fusion.place
  2.3 0.6 shard_map.136
  2.9 0.0 copy-start.2
  2.9 0.0 copy-start.5
  2.9 0.0 copy-start.6
  2.9 1.6 %collective-permute-start = (bf16[32,512]{1,0:T(8,128)(2,1)S(1)}, bf16[32,512]{1,0:T(8,128)(2,1)S(1)}, u32[]{:S(2)}, u32[]{:S(2)}) collective-permute-start(bf16[32,512]{1,0:T(8,128)(2,1)S(1)} %get-tuple-element.26), channel_id=1, source_target_pairs={{0,1},{1,0},{2,3},{3,2},{4,5},{5,4},{6,7},{7,6},{8,9},{9,8},{10,11... | collective-permute-start | bytes 98312 | tf_op jit(solution)/shard_map/ppermute | solution.py:436
  4.5 7.4 %collective-permute-start.1 = (bf16[32,512]{1,0:T(8,128)(2,1)S(1)}, bf16[32,512]{1,0:T(8,128)(2,1)S(1)}, u32[]{:S(2)}, u32[]{:S(2)}) collective-permute-start(bf16[32,512]{1,0:T(8,128)(2,1)S(1)} %get-tuple-element.27), channel_id=1, source_target_pairs={{0,31},{1,2},{2,1},{3,4},{4,3},{5,6},{6,5},{7,8},{8,7},{9,10},{10,... | collective-permute-start | bytes 98312 | tf_op jit(solution)/shard_map/ppermute | solution.py:437
  11.9 0.0 copy-done.1
  11.9 2.0 %shard_map.137 = (bf16[704,512]{1,0:T(8,128)(2,1)S(1)}, bf16[704,512]{1,0:T(8,128)(2,1)S(1)}, bf16[704,512]{1,0:T(8,128)(2,1)S(1)}, bf16[704,512]{1,0:T(8,128)(2,1)S(1)}) custom-call(s32[4]{0:T(128)S(1)} %pad_add_fusion.place, bf16[704,512]{1,0:T(8,128)(2,1)S(1)} %bitcast.10, bf16[512,1024]{1,0:T(8,128)(2,1)S(1)} %copy-done.1), custom_call_target="tpu_custom_call" | custom-call | flops 738197504 | bytes 8388608 | tf_op jit(solution)/shard_map/pallas_call | solution.py:440
  13.8 0.0 collective-permute-done.inner_ref
  13.8 0.0 collective-permute-done.1.outer_ref
  13.9 0.0 copy-start.3
  13.9 0.0 copy-start.4
  13.9 0.0 copy-start.7
  13.9 8.8 %shard_map.138 = (bf16[768,512]{1,0:T(8,128)(2,1)S(1)}, bf16[736,512]{1,0:T(8,128)(2,1)S(1)}, bf16[736,512]{1,0:T(8,128)(2,1)S(1)}, f32[736,512]{1,0:T(8,128)S(1)}, f32[32,8,640]{2,1,0:T(8,128)S(1)}) custom-call(s32[4]{0:T(128)S(1)} %pad_add_fusion.place, bf16[32,512]{1,0:T(8,128)(2,1)S(1)} %collective-permute-done.inner_ref, ...), custom_call_target="tpu_custom_call" | custom-call | flops 1476395008 | bytes 8388608 | tf_op jit(solution)/shard_map/pallas_call | solution.py:443
  22.7 25.9 %all_to_all.20.sums_ref = f32[32,8,640]{2,1,0:T(8,128)S(1)} all-to-all(f32[32,8,640]{2,1,0:T(8,128)S(1)} %get-tuple-element.29), channel_id=1, replica_groups=mesh['ep'=8,'seq'=32] {'seq'}, dimensions={0} | all-to-all | bytes 1310720 | tf_op jit(solution)/shard_map/all_to_all | solution.py:456
  48.6 0.0 copy-done.3
  48.6 14.8 %shard_map.139 = (bf16[4,832,128]{2,1,0:T(8,128)(2,1)S(1)}, bf16[4,832,128]{2,1,0:T(8,128)(2,1)S(1)}) custom-call(s32[4]{0:T(128)S(1)} %pad_add_fusion.place, f32[32,8,640]{2,1,0:T(8,128)S(1)} %all_to_all.20.sums_ref, bf16[512,512]{1,0:T(8,128)(2,1)S(1)} %copy-done.3, bf16[256,512]{1,0:T(8,128)(2,1)S(1)} %copy-done.4, f32[1,256]{1,0:T(1,128)S(1)} %copy-done.7, ...), custom_call_target="tpu_custom_call" | custom-call | flops 2952790016 | bytes 8388608 | tf_op jit(solution)/shard_map/pallas_call | solution.py:464
  63.4 0.1 collective-permute-start.2
  63.5 2.4 %collective-permute-done.2.got_ref = bf16[4,832,128]{2,1,0:T(8,128)(2,1)S(1)} collective-permute-done((bf16[4,832,128]{2,1,0:T(8,128)(2,1)S(1)}, bf16[4,832,128]{2,1,0:T(8,128)(2,1)S(1)}, u32[]{:S(2)}, u32[]{:S(2)}) %collective-permute-start.2) | collective-permute-done | bytes 852000 | tf_op jit(solution)/shard_map/ppermute | solution.py:484
  65.9 0.2 shard_map.140
  66.1 17.1 %all_to_all.21.got_ref = bf16[4,880,128]{2,1,0:T(8,128)(2,1)S(1)} all-to-all(bf16[4,880,128]{2,1,0:T(8,128)(2,1)S(1)} %shard_map.140), channel_id=1, replica_groups={{0,64,128,192},{32,96,160,224},{1,65,129,193},{33,97,161,225},{2,66,130..., dimensions={0} | all-to-all | bytes 1802240 | tf_op jit(solution)/shard_map/all_to_all | solution.py:491
  83.1 0.1 shard_map.142
  83.2 18.6 %all_to_all.22.got_ref = bf16[32,48,128]{2,1,0:T(8,128)(2,1)S(1)} all-to-all(bf16[32,48,128]{2,1,0:T(8,128)(2,1)S(1)} %shard_map.142), channel_id=1, replica_groups=mesh['ep'=8,'seq'=32] {'seq'}, dimensions={0} | all-to-all | bytes 786432 | tf_op jit(solution)/shard_map/all_to_all | solution.py:503
  101.8 0.8 shard_map.143
  102.6 4.7 %all-to-all-start.3 = ((f32[8,24,128]{2,1,0:T(8,128)}), f32[8,24,128]{2,1,0:T(8,128)S(1)}, u32[]{:S(2)}, u32[]{:S(2)}) async-start(f32[8,24,128]{2,1,0:T(8,128)} %get-tuple-element.42), calls=%async_computation.3 | async-start | bytes 196608 | tf_op jit(solution)/shard_map/all_to_all | solution.py:513
  107.3 1.3 %shard_map.141 = (f32[512,512]{1,0:T(8,128)}, f32[1,128]{1,0:T(1,128)}) custom-call(bf16[4,880,128]{2,1,0:T(8,128)(2,1)S(1)} %all_to_all.21.got_ref), custom_call_target="tpu_custom_call" | custom-call | flops 1048576 | bytes 8388608 | tf_op jit(solution)/shard_map/pallas_call | solution.py:497
  108.6 3.1 %all-to-all-done.3.got_ref = f32[8,24,128]{2,1,0:T(8,128)S(1)} async-done(((f32[8,24,128]{2,1,0:T(8,128)}), f32[8,24,128]{2,1,0:T(8,128)S(1)}, u32[]{:S(2)}, u32[]{:S(2)}) %all-to-all-start.3) | async-done | bytes 98336 | tf_op jit(solution)/shard_map/all_to_all | solution.py:513
  111.7 0.6 shard_map.144
  (6 shorter events, 0.0 us)
Async XLA Ops:
  0.6 11.2 %copy-start = (bf16[1,704,512]{2,1,0:T(8,128)(2,1)S(1)}, bf16[1,704,512]{2,1,0:T(8,128)(2,1)}, u32[]{:S(2)}) copy-start(bf16[1,704,512]{2,1,0:T(8,128)(2,1)} %param.9) | copy-start | bytes 2162692
  0.6 11.2 %copy-start.1 = (bf16[512,1024]{1,0:T(8,128)(2,1)S(1)}, bf16[512,1024]{1,0:T(8,128)(2,1)}, u32[]{:S(2)}) copy-start(bf16[512,1024]{1,0:T(8,128)(2,1)} %w_in_ref.3) | copy-start | bytes 3145732
  2.9 11.0 %copy-start.2 = (bf16[512,512]{1,0:T(8,128)(2,1)S(1)}, bf16[512,512]{1,0:T(8,128)(2,1)}, u32[]{:S(2)}) copy-start(bf16[512,512]{1,0:T(8,128)(2,1)} %w_out_ref.3) | copy-start | bytes 1572868
  2.9 11.0 %copy-start.5 = (f32[31,512]{1,0:T(8,128)S(1)}, f32[31,512]{1,0:T(8,128)}, u32[]{:S(2)}) copy-start(f32[31,512]{1,0:T(8,128)} %taps_ref.3) | copy-start | bytes 190468
  2.9 11.0 %copy-start.6 = (bf16[8,512]{1,0:T(8,128)(2,1)S(1)}, bf16[8,512]{1,0:T(8,128)(2,1)}, u32[]{:S(2)}) copy-start(bf16[8,512]{1,0:T(8,128)(2,1)} %query_ref.3) | copy-start | bytes 24580
  2.9 10.9 %collective-permute-start = (bf16[32,512]{1,0:T(8,128)(2,1)S(1)}, bf16[32,512]{1,0:T(8,128)(2,1)S(1)}, u32[]{:S(2)}, u32[]{:S(2)}) collective-permute-start(bf16[32,512]{1,0:T(8,128)(2,1)S(1)} %get-tuple-element.26), channel_id=1, source_target_pairs={{0,1},{1,0},{2,3},{3,2},{4,5},{5,4},{6,7},{7,6},{8,9},{9,8},{10,11... | collective-permute-start | bytes 98312 | tf_op jit(solution)/shard_map/ppermute | solution.py:436
  4.5 9.4 %collective-permute-start.1 = (bf16[32,512]{1,0:T(8,128)(2,1)S(1)}, bf16[32,512]{1,0:T(8,128)(2,1)S(1)}, u32[]{:S(2)}, u32[]{:S(2)}) collective-permute-start(bf16[32,512]{1,0:T(8,128)(2,1)S(1)} %get-tuple-element.27), channel_id=1, source_target_pairs={{0,31},{1,2},{2,1},{3,4},{4,3},{5,6},{6,5},{7,8},{8,7},{9,10},{10,... | collective-permute-start | bytes 98312 | tf_op jit(solution)/shard_map/ppermute | solution.py:437
  13.9 34.7 %copy-start.3 = (bf16[512,512]{1,0:T(8,128)(2,1)S(1)}, bf16[512,512]{1,0:T(8,128)(2,1)}, u32[]{:S(2)}) copy-start(bf16[512,512]{1,0:T(8,128)(2,1)} %w_value_ref.1) | copy-start | bytes 1572868
  13.9 34.7 %copy-start.4 = (bf16[256,512]{1,0:T(8,128)(2,1)S(1)}, bf16[256,512]{1,0:T(8,128)(2,1)}, u32[]{:S(2)}) copy-start(bf16[256,512]{1,0:T(8,128)(2,1)} %text_ref.1) | copy-start | bytes 786436
  13.9 34.7 %copy-start.7 = (f32[1,256]{1,0:T(1,128)S(1)}, f32[1,256]{1,0:T(1,128)}, u32[]{:S(2)}) copy-start(f32[1,256]{1,0:T(1,128)} %teacher_ref.1) | copy-start | bytes 3076
  63.4 2.5 %collective-permute-start.2 = (bf16[4,832,128]{2,1,0:T(8,128)(2,1)S(1)}, bf16[4,832,128]{2,1,0:T(8,128)(2,1)S(1)}, u32[]{:S(2)}, u32[]{:S(2)}) collective-permute-start(bf16[4,832,128]{2,1,0:T(8,128)(2,1)S(1)} %get-tuple-element.38), channel_id=1, source_target_pairs={{0,32},{32,0},{64,96},{96,64},{128,160},{160,128},{192,224},{224,1... | collective-permute-start | bytes 2555912 | tf_op jit(solution)/shard_map/ppermute | solution.py:484
  102.6 9.1 %all-to-all-start.3 = ((f32[8,24,128]{2,1,0:T(8,128)}), f32[8,24,128]{2,1,0:T(8,128)S(1)}, u32[]{:S(2)}, u32[]{:S(2)}) async-start(f32[8,24,128]{2,1,0:T(8,128)} %get-tuple-element.42), calls=%async_computation.3 | async-start | bytes 196608 | tf_op jit(solution)/shard_map/all_to_all | solution.py:513

commit v8 on v7

--- a/solution.py
+++ b/solution.py
@@ -79,7 +79,25 @@
     outer_ref[...] = jnp.where(odd, last, first).astype(BF16)
 
 
-def project_kernel(place, x_ref, w_in_ref, normed_ref, sig_ref, slope_ref, glu_ref):
+def shifted(block):
+    rows = block.shape[0]
+    return [block if s == 0 else pltpu.roll(block, rows - s, 0) for s in range(8)]
+
+
+def convolved(block, taps_ref, cols):
+    views = shifted(block)
+    acc = jnp.zeros((STEP, LANES), F32)
+    for k in range(taps_ref.shape[0]):
+        q, s = divmod(k + 1, 8)
+        acc = acc + taps_ref[k : k + 1, cols] * views[s][8 * q : 8 * q + STEP]
+    s = jax.nn.sigmoid(acc)
+    return (acc * s).astype(BF16), (s * (1.0 + acc * (1.0 - s))).astype(BF16)
+
+
+def project_kernel(
+    place, x_ref, w_in_ref, taps_ref,
+    normed_ref, sig_ref, gate_slope_ref, glu_ref, act_ref, slope_ref, glu_f,
+):
     rows, width = x_ref.shape
     chunk = rows // 4
     for i in range(4):
@@ -89,22 +107,28 @@
         normed_ref[part, :] = normed
         sig_ref[part, :] = sig.astype(BF16)
         both = gate * sig
-        slope_ref[part, :] = (both * (1.0 - sig)).astype(BF16)
-        glu_ref[part, :] = jnp.where(valid, both, 0.0).astype(BF16)
-
-
-def shifted(block):
-    rows = block.shape[0]
-    return [block if s == 0 else pltpu.roll(block, rows - s, 0) for s in range(8)]
+        gate_slope_ref[part, :] = (both * (1.0 - sig)).astype(BF16)
+        glu = jnp.where(valid, both, 0.0).astype(BF16)
+        glu_ref[part, :] = glu
+        glu_f[part, :] = glu.astype(F32)
+
+    @pl.loop(0, act_ref.shape[0] // STEP)
+    def _(i):
+        start = pl.multiple_of(i * STEP, STEP)
+        for c in range(width // LANES):
+            cols = slice(c * LANES, (c + 1) * LANES)
+            act, slope = convolved(glu_f[pl.ds(start, 2 * STEP), cols], taps_ref, cols)
+            act_ref[pl.ds(start, STEP), cols] = act
+            slope_ref[pl.ds(start, STEP), cols] = slope
 
 
 def forward_kernel(
     place, inner_ref, outer_ref, x_ref, own_glu_ref, w_in_ref, taps_ref, w_out_ref, query_ref,
+    own_act_ref, own_slope_ref,
     glu_ref, act_ref, slope_ref, resid_ref, sums_ref, glu_f,
 ):
     rows, width = x_ref.shape
     wide = rows + 2 * SIDE
-    n_taps = taps_ref.shape[0]
     odd = place[3] == 1
     inner, outer = inner_ref[...].astype(F32), outer_ref[...].astype(F32)
     halo = jnp.concatenate(
@@ -120,22 +144,17 @@
     glu_ref[STEP : STEP + rows, :] = own_glu_ref[...]
     glu_ref[STEP + rows :, :] = high
     glu_f[0:STEP, :] = low.astype(F32)
-    glu_f[STEP : STEP + rows, :] = own_glu_ref[...].astype(F32)
-    glu_f[STEP + rows :, :] = high.astype(F32)
-
-    @pl.loop(0, wide // STEP)
-    def _(i):
-        start = pl.multiple_of(i * STEP, STEP)
+    glu_f[STEP : 2 * STEP, :] = own_glu_ref[0:STEP, :].astype(F32)
+    glu_f[2 * STEP : 3 * STEP, :] = own_glu_ref[rows - STEP : rows, :].astype(F32)
+    glu_f[3 * STEP :, :] = high.astype(F32)
+    act_ref[STEP : wide - STEP, :] = own_act_ref[...]
+    slope_ref[STEP : wide - STEP, :] = own_slope_ref[...]
+    for source, target in ((0, 0), (2 * STEP, wide - STEP)):
         for c in range(width // LANES):
             cols = slice(c * LANES, (c + 1) * LANES)
-            views = shifted(glu_f[pl.ds(start, 2 * STEP), cols])
-            acc = jnp.zeros((STEP, LANES), F32)
-            for k in range(n_taps):
-                q, s = divmod(k + 1, 8)
-                acc = acc + taps_ref[k : k + 1, cols] * views[s][8 * q : 8 * q + STEP]
-            s = jax.nn.sigmoid(acc)
-            act_ref[pl.ds(start, STEP), cols] = (acc * s).astype(BF16)
-            slope_ref[pl.ds(start, STEP), cols] = (s * (1.0 + acc * (1.0 - s))).astype(BF16)
+            act, slope = convolved(glu_f[source : source + 2 * STEP, cols], taps_ref, cols)
+            act_ref[target : target + STEP, cols] = act
+            slope_ref[target : target + STEP, cols] = slope
 
     w_out = w_out_ref[...]
     resid_ref[0:SIDE, :] = halo[STEP - SIDE : STEP] + dot(act_ref[0:SIDE, :], w_out)
@@ -437,9 +456,14 @@
     outer = lax.ppermute(outer, "seq", far)
 
     own = shape((rows, width), BF16)
-    normed, sig, gate_slope, own_glu = call(
-        project_kernel, [own] * 4, [], 2, 2 * rows * width * width * 2
-    )(place, x, w_in)
+    mid = shape((rows - STEP, width), BF16)
+    normed, sig, gate_slope, own_glu, own_act, own_slope = call(
+        project_kernel,
+        [own] * 4 + [mid] * 2,
+        [pltpu.VMEM((rows, width), F32)],
+        3,
+        2 * rows * width * width * 4,
+    )(place, x, w_in, kernel)
     glu, act, slope, resid, sums = call(
         forward_kernel,
         [
@@ -449,10 +473,10 @@
             shape((wide, width), F32),
             shape((n_seq, n_heads, width + LANES), F32),
         ],
-        [pltpu.VMEM((whole, width), F32)],
-        8,
+        [pltpu.VMEM((4 * STEP, width), F32)],
+        10,
         2 * rows * width * width * 4,
-    )(place, inner, outer, x, own_glu, w_in, kernel, w_out, pool_query)
+    )(place, inner, outer, x, own_glu, w_in, kernel, w_out, pool_query, own_act, own_slope)
     sums = lax.all_to_all(sums, "seq", 0, 0)
 
     small_rows = 48

time: 114 us -> 113 us (level)
  blocking collectives: 61.6 us -> 60 us
    pallas_call x1, Pallas kernels: 8.79 us -> 3.95 us  [shards(): call(forward_kernel, [shape((whole, width), BF16), shape((wide, width), B...]
    pallas_call x1, Pallas kernels: 1.96 us -> 6.77 us  [shards(): call(project_kernel, [own] * 4 + [mid] * 2, [pltpu.VMEM((rows, width), F3...]
    all_to_all x1, blocking collectives: 25.9 us -> 24.1 us  [shards(): sums = lax.all_to_all(sums, 'seq', 0, 0)]
  transfers between devices with their start and end apart: 4 -> 4, of which waited for: 2 -> 2; matrix products, arithmetic and copies ran while one was open for 0% -> 0% of each run, Pallas kernels for 3% -> 7%
where the time goes in v8:
time: 113 us; the launch traced here: 111 us
  blocking collectives  60 us (53%)
  Pallas kernels  29 us (26%)
  starting transfers between devices  13.8 us (12%)
  waiting for transfers between devices  5.45 us (5%)
  between operations  1.56 us (1%)
    all_to_all x1, blocking collectives, shards(): sums = lax.all_to_all(sums, 'seq', 0, 0)  24.1 us
    all_to_all x1, blocking collectives, shards(): got = lax.all_to_all(total, 'seq', 0, 0)  18.9 us
    all_to_all x1, blocking collectives, shards(): got = lax.all_to_all(total, 'ep', 0, 0, axis_index_groups=groups)  17.1 us
    pallas_call x1, Pallas kernels, shards(): call(backward_kernel, [payload, payload], [pltpu.VMEM((wide, width), F32)...  14.7 us
    ppermute x1, starting transfers between devices, shards(): outer = lax.ppermute(outer, 'seq', far)  7.39 us
    pallas_call x1, Pallas kernels, shards(): call(project_kernel, [own] * 4 + [mid] * 2, [pltpu.VMEM((rows, width), F3...  6.77 us
    all_to_all x1, starting transfers between devices, shards(): got = lax.all_to_all(share, 'ep', 0, 0)  4.73 us
    pallas_call x1, Pallas kernels, shards(): call(forward_kernel, [shape((whole, width), BF16), shape((wide, width), B...  3.95 us
  transfers between devices with their start and end apart: 4, of which 2 were waited for; matrix products, arithmetic and copies ran while one was open for 0% of the time, Pallas kernels for 7%

profile of v8, /device:TPU:8, one launch (start us, length us, event | category | flops | bytes accessed | tf_op | source)
XLA Modules:
  0.0 110.8 jit_solution(3301099230960228060)
XLA Ops:
  0.6 0.0 copy-start
  1.4 0.8 slice_bitcast_fusion
  2.2 0.1 pad_add_fusion.place
  2.3 0.6 shard_map.136
  2.9 1.6 %collective-permute-start = (bf16[32,512]{1,0:T(8,128)(2,1)S(1)}, bf16[32,512]{1,0:T(8,128)(2,1)S(1)}, u32[]{:S(2)}, u32[]{:S(2)}) collective-permute-start(bf16[32,512]{1,0:T(8,128)(2,1)S(1)} %get-tuple-element.28), channel_id=1, source_target_pairs={{0,1},{1,0},{2,3},{3,2},{4,5},{5,4},{6,7},{7,6},{8,9},{9,8},{10,11... | collective-permute-start | bytes 98312 | tf_op jit(solution)/shard_map/ppermute | solution.py:455
  4.4 7.4 %collective-permute-start.1 = (bf16[32,512]{1,0:T(8,128)(2,1)S(1)}, bf16[32,512]{1,0:T(8,128)(2,1)S(1)}, u32[]{:S(2)}, u32[]{:S(2)}) collective-permute-start(bf16[32,512]{1,0:T(8,128)(2,1)S(1)} %get-tuple-element.29), channel_id=1, source_target_pairs={{0,31},{1,2},{2,1},{3,4},{4,3},{5,6},{6,5},{7,8},{8,7},{9,10},{10,... | collective-permute-start | bytes 98312 | tf_op jit(solution)/shard_map/ppermute | solution.py:456
  11.8 0.0 copy-done
  11.8 0.0 copy-done.1
  11.9 0.0 copy-start.6
  11.9 6.8 %shard_map.137 = (bf16[704,512]{1,0:T(8,128)(2,1)S(1)}, bf16[704,512]{1,0:T(8,128)(2,1)S(1)}, bf16[704,512]{1,0:T(8,128)(2,1)S(1)}, bf16[704,512]{1,0:T(8,128)(2...) custom-call(s32[4]{0:T(128)S(1)} %pad_add_fusion.place, bf16[704,512]{1,0:T(8,128)(2,1)S(1)} %bitcast.10, ...), custom_call_target="tpu_custom_call" | custom-call | flops 1476395008 | bytes 8388608 | tf_op jit(solution)/shard_map/pallas_call | solution.py:460
  18.6 0.0 collective-permute-done.inner_ref
  18.7 0.0 collective-permute-done.1.outer_ref
  18.7 0.0 copy-done.2
  18.7 0.0 copy-done.6
  18.7 0.0 copy-start.3
  18.7 0.0 copy-start.4
  18.7 0.0 copy-start.7
  18.7 3.9 %shard_map.138 = (bf16[768,512]{1,0:T(8,128)(2,1)S(1)}, bf16[736,512]{1,0:T(8,128)(2,1)S(1)}, bf16[736,512]{1,0:T(8,128)(2,1)S(1)}, f32[736,512]{1,0:T(8,128)S(1)}, f32[32,8,640]{2,1,0:T(8,128)S(1)}) custom-call(s32[4]{0:T(128)S(1)} %pad_add_fusion.place, bf16[32,512]{1,0:T(8,128)(2,1)S(1)} %collective-permute-done.inner_ref, ...), custom_call_target="tpu_custom_call" | custom-call | flops 1476395008 | bytes 8388608 | tf_op jit(solution)/shard_map/pallas_call | solution.py:467
  22.7 24.1 %all_to_all.20.sums_ref = f32[32,8,640]{2,1,0:T(8,128)S(1)} all-to-all(f32[32,8,640]{2,1,0:T(8,128)S(1)} %get-tuple-element.33), channel_id=1, replica_groups=mesh['ep'=8,'seq'=32] {'seq'}, dimensions={0} | all-to-all | bytes 1310720 | tf_op jit(solution)/shard_map/all_to_all | solution.py:480
  46.8 0.0 copy-done.7
  46.8 14.7 %shard_map.139 = (bf16[4,832,128]{2,1,0:T(8,128)(2,1)S(1)}, bf16[4,832,128]{2,1,0:T(8,128)(2,1)S(1)}) custom-call(s32[4]{0:T(128)S(1)} %pad_add_fusion.place, f32[32,8,640]{2,1,0:T(8,128)S(1)} %all_to_all.20.sums_ref, bf16[512,512]{1,0:T(8,128)(2,1)S(1)} %copy-done.3, bf16[256,512]{1,0:T(8,128)(2,1)S(1)} %copy-done.4, f32[1,256]{1,0:T(1,128)S(1)} %copy-done.7, ...), custom_call_target="tpu_custom_call" | custom-call | flops 2952790016 | bytes 8388608 | tf_op jit(solution)/shard_map/pallas_call | solution.py:488
  61.5 0.1 collective-permute-start.2
  61.6 2.4 %collective-permute-done.2.got_ref = bf16[4,832,128]{2,1,0:T(8,128)(2,1)S(1)} collective-permute-done((bf16[4,832,128]{2,1,0:T(8,128)(2,1)S(1)}, bf16[4,832,128]{2,1,0:T(8,128)(2,1)S(1)}, u32[]{:S(2)}, u32[]{:S(2)}) %collective-permute-start.2) | collective-permute-done | bytes 852000 | tf_op jit(solution)/shard_map/ppermute | solution.py:508
  64.0 0.2 shard_map.140
  64.2 17.1 %all_to_all.21.got_ref = bf16[4,880,128]{2,1,0:T(8,128)(2,1)S(1)} all-to-all(bf16[4,880,128]{2,1,0:T(8,128)(2,1)S(1)} %shard_map.140), channel_id=1, replica_groups={{0,64,128,192},{32,96,160,224},{1,65,129,193},{33,97,161,225},{2,66,130..., dimensions={0} | all-to-all | bytes 1802240 | tf_op jit(solution)/shard_map/all_to_all | solution.py:515
  81.2 0.1 shard_map.142
  81.4 18.9 %all_to_all.22.got_ref = bf16[32,48,128]{2,1,0:T(8,128)(2,1)S(1)} all-to-all(bf16[32,48,128]{2,1,0:T(8,128)(2,1)S(1)} %shard_map.142), channel_id=1, replica_groups=mesh['ep'=8,'seq'=32] {'seq'}, dimensions={0} | all-to-all | bytes 786432 | tf_op jit(solution)/shard_map/all_to_all | solution.py:527
  100.2 0.8 shard_map.143
  101.0 4.7 %all-to-all-start.3 = ((f32[8,24,128]{2,1,0:T(8,128)}), f32[8,24,128]{2,1,0:T(8,128)S(1)}, u32[]{:S(2)}, u32[]{:S(2)}) async-start(f32[8,24,128]{2,1,0:T(8,128)} %get-tuple-element.46), calls=%async_computation.3 | async-start | bytes 196608 | tf_op jit(solution)/shard_map/all_to_all | solution.py:537
  105.7 1.3 %shard_map.141 = (f32[512,512]{1,0:T(8,128)}, f32[1,128]{1,0:T(1,128)}) custom-call(bf16[4,880,128]{2,1,0:T(8,128)(2,1)S(1)} %all_to_all.21.got_ref), custom_call_target="tpu_custom_call" | custom-call | flops 1048576 | bytes 8388608 | tf_op jit(solution)/shard_map/pallas_call | solution.py:521
  107.0 3.1 %all-to-all-done.3.got_ref = f32[8,24,128]{2,1,0:T(8,128)S(1)} async-done(((f32[8,24,128]{2,1,0:T(8,128)}), f32[8,24,128]{2,1,0:T(8,128)S(1)}, u32[]{:S(2)}, u32[]{:S(2)}) %all-to-all-start.3) | async-done | bytes 98336 | tf_op jit(solution)/shard_map/all_to_all | solution.py:537
  110.1 0.6 shard_map.144
  (6 shorter events, 0.0 us)
Async XLA Ops:
  0.6 11.2 %copy-start = (bf16[1,704,512]{2,1,0:T(8,128)(2,1)S(1)}, bf16[1,704,512]{2,1,0:T(8,128)(2,1)}, u32[]{:S(2)}) copy-start(bf16[1,704,512]{2,1,0:T(8,128)(2,1)} %param.9) | copy-start | bytes 2162692
  0.6 11.2 %copy-start.5 = (f32[31,512]{1,0:T(8,128)S(1)}, f32[31,512]{1,0:T(8,128)}, u32[]{:S(2)}) copy-start(f32[31,512]{1,0:T(8,128)} %taps_ref.5) | copy-start | bytes 190468
  0.7 11.2 %copy-start.1 = (bf16[512,1024]{1,0:T(8,128)(2,1)S(1)}, bf16[512,1024]{1,0:T(8,128)(2,1)}, u32[]{:S(2)}) copy-start(bf16[512,1024]{1,0:T(8,128)(2,1)} %w_in_ref.3) | copy-start | bytes 3145732
  2.9 15.8 %collective-permute-start = (bf16[32,512]{1,0:T(8,128)(2,1)S(1)}, bf16[32,512]{1,0:T(8,128)(2,1)S(1)}, u32[]{:S(2)}, u32[]{:S(2)}) collective-permute-start(bf16[32,512]{1,0:T(8,128)(2,1)S(1)} %get-tuple-element.28), channel_id=1, source_target_pairs={{0,1},{1,0},{2,3},{3,2},{4,5},{5,4},{6,7},{7,6},{8,9},{9,8},{10,11... | collective-permute-start | bytes 98312 | tf_op jit(solution)/shard_map/ppermute | solution.py:455
  4.4 14.2 %collective-permute-start.1 = (bf16[32,512]{1,0:T(8,128)(2,1)S(1)}, bf16[32,512]{1,0:T(8,128)(2,1)S(1)}, u32[]{:S(2)}, u32[]{:S(2)}) collective-permute-start(bf16[32,512]{1,0:T(8,128)(2,1)S(1)} %get-tuple-element.29), channel_id=1, source_target_pairs={{0,31},{1,2},{2,1},{3,4},{4,3},{5,6},{6,5},{7,8},{8,7},{9,10},{10,... | collective-permute-start | bytes 98312 | tf_op jit(solution)/shard_map/ppermute | solution.py:456
  11.8 6.8 %copy-start.2 = (bf16[512,512]{1,0:T(8,128)(2,1)S(1)}, bf16[512,512]{1,0:T(8,128)(2,1)}, u32[]{:S(2)}) copy-start(bf16[512,512]{1,0:T(8,128)(2,1)} %w_out_ref.3) | copy-start | bytes 1572868
  11.9 6.8 %copy-start.6 = (bf16[8,512]{1,0:T(8,128)(2,1)S(1)}, bf16[8,512]{1,0:T(8,128)(2,1)}, u32[]{:S(2)}) copy-start(bf16[8,512]{1,0:T(8,128)(2,1)} %query_ref.3) | copy-start | bytes 24580
  18.7 28.1 %copy-start.3 = (bf16[512,512]{1,0:T(8,128)(2,1)S(1)}, bf16[512,512]{1,0:T(8,128)(2,1)}, u32[]{:S(2)}) copy-start(bf16[512,512]{1,0:T(8,128)(2,1)} %w_value_ref.1) | copy-start | bytes 1572868
  18.7 28.1 %copy-start.4 = (bf16[256,512]{1,0:T(8,128)(2,1)S(1)}, bf16[256,512]{1,0:T(8,128)(2,1)}, u32[]{:S(2)}) copy-start(bf16[256,512]{1,0:T(8,128)(2,1)} %text_ref.1) | copy-start | bytes 786436
  18.7 28.0 %copy-start.7 = (f32[1,256]{1,0:T(1,128)S(1)}, f32[1,256]{1,0:T(1,128)}, u32[]{:S(2)}) copy-start(f32[1,256]{1,0:T(1,128)} %teacher_ref.1) | copy-start | bytes 3076
  61.5 2.5 %collective-permute-start.2 = (bf16[4,832,128]{2,1,0:T(8,128)(2,1)S(1)}, bf16[4,832,128]{2,1,0:T(8,128)(2,1)S(1)}, u32[]{:S(2)}, u32[]{:S(2)}) collective-permute-start(bf16[4,832,128]{2,1,0:T(8,128)(2,1)S(1)} %get-tuple-element.42), channel_id=1, source_target_pairs={{0,32},{32,0},{64,96},{96,64},{128,160},{160,128},{192,224},{224,1... | collective-permute-start | bytes 2555912 | tf_op jit(solution)/shard_map/ppermute | solution.py:508
  101.0 9.1 %all-to-all-start.3 = ((f32[8,24,128]{2,1,0:T(8,128)}), f32[8,24,128]{2,1,0:T(8,128)S(1)}, u32[]{:S(2)}, u32[]{:S(2)}) async-start(f32[8,24,128]{2,1,0:T(8,128)} %get-tuple-element.46), calls=%async_computation.3 | async-start | bytes 196608 | tf_op jit(solution)/shard_map/all_to_all | solution.py:537

commit v9 on v8

--- a/solution.py
+++ b/solution.py
@@ -125,7 +125,7 @@
 def forward_kernel(
     place, inner_ref, outer_ref, x_ref, own_glu_ref, w_in_ref, taps_ref, w_out_ref, query_ref,
     own_act_ref, own_slope_ref,
-    glu_ref, act_ref, slope_ref, resid_ref, sums_ref, glu_f,
+    glu_ref, act_ref, slope_ref, resid_ref, score_ref, sums_ref, glu_f,
 ):
     rows, width = x_ref.shape
     wide = rows + 2 * SIDE
@@ -163,6 +163,12 @@
     )
     queries = jnp.concatenate([query_ref[...]] * (LANES // 8), axis=0)
     root = jnp.sqrt(jnp.float32(width))
+
+    def scored(resid):
+        return sum(dot(piece, queries, NT) for piece in split3(resid)) / root
+
+    score_ref[0:SIDE, :] = scored(resid_ref[0:SIDE, :])
+    score_ref[SIDE + rows :, :] = scored(resid_ref[SIDE + rows :, :])
     parts = 2
     chunk = rows // parts
     scores = []
@@ -170,7 +176,8 @@
         own = pl.ds(SIDE + i * chunk, chunk)
         resid = x_ref[pl.ds(i * chunk, chunk), :].astype(F32) + dot(act_ref[own, :], w_out)
         resid_ref[own, :] = resid
-        score = sum(dot(piece, queries, NT) for piece in split3(resid)) / root
+        score = scored(resid)
+        score_ref[own, :] = score
         valid = row_mask(place[0] + i * chunk, chunk, place[1])
         scores.append(jnp.where(valid, score, -1e30))
     top = functools.reduce(
@@ -196,7 +203,7 @@
 
 
 def backward_kernel(
-    place, sums_ref, w_value_ref, text_ref, teacher_ref, query_ref, resid_ref, act_ref, slope_ref,
+    place, sums_ref, w_value_ref, text_ref, teacher_ref, query_ref, resid_ref, score_ref, act_ref, slope_ref,
     glu_ref, normed_ref, sig_ref, gate_slope_ref, w_out_ref, taps_ref,
     mine_ref, other_ref,
     dconv_f, glu_f, dresid_s, dmixed_s, in_s, tap_s, small_s,
@@ -241,8 +248,7 @@
     query = query_ref[...]
     d_high, d_mid, d_low = split3(dvbar)
     many = lambda piece: [piece] * (LANES // 8)
-    both = jnp.concatenate(many(query) + many(d_high), axis=0)
-    queries, dv_mid = both[:LANES], jnp.concatenate(many(d_mid), axis=0)
+    pieces = jnp.concatenate(many(d_high) + many(d_mid), axis=0)
     mixing = jnp.concatenate(
         [d_high, d_mid, d_high, d_mid, query, query, query, jnp.zeros((LANES - 56, width), BF16)],
         axis=0,
@@ -253,12 +259,11 @@
     grad_query = jnp.zeros((LANES, width), F32)
     for i in range(parts):
         here = pl.ds(i * chunk, chunk)
-        r_high, r_mid, r_low = split3(resid_ref[here, :])
-        products = dot(r_high, both, NT) + dot(r_mid, both, NT)
-        score = (products[:, :LANES] + dot(r_low, queries, NT)) / root
+        r_high, r_mid = split3(resid_ref[here, :])[:2]
         valid = row_mask(place[0] - SIDE + i * chunk, chunk, place[1])
-        probs = jnp.where(valid, jnp.exp(score - top_l), 0.0) / total_l
-        proj = products[:, LANES:] + dot(r_high, dv_mid, NT)
+        probs = jnp.where(valid, jnp.exp(score_ref[here, :] - top_l), 0.0) / total_l
+        products = dot(r_high, pieces, NT)
+        proj = products[:, :LANES] + (products[:, LANES:] + dot(r_mid, pieces[:LANES], NT))
         dscores = probs * (proj - centre_l) / root
         p_high, p_mid, unused = split3(probs)
         s_pieces = split3(dscores)
@@ -464,13 +469,14 @@
         3,
         2 * rows * width * width * 4,
     )(place, x, w_in, kernel)
-    glu, act, slope, resid, sums = call(
+    glu, act, slope, resid, score, sums = call(
         forward_kernel,
         [
             shape((whole, width), BF16),
             shape((wide, width), BF16),
             shape((wide, width), BF16),
             shape((wide, width), F32),
+            shape((wide, LANES), F32),
             shape((n_seq, n_heads, width + LANES), F32),
         ],
         [pltpu.VMEM((4 * STEP, width), F32)],
@@ -497,10 +503,10 @@
             pltpu.VMEM((n_taps + 1, 8, width), F32),
             pltpu.VMEM((small_rows, width), F32),
         ],
-        14,
+        15,
         2 * rows * width * width * 8,
     )(
-        place, sums, w_value, text_emb, teacher, pool_query, resid, act, slope,
+        place, sums, w_value, text_emb, teacher, pool_query, resid, score, act, slope,
         glu, normed, sig, gate_slope, w_out, kernel,
     )
 

time: 113 us -> 113 us (level)
  no operation moved by 1% of the time
where the time goes in v9:
time: 113 us; the launch traced here: 110 us
  blocking collectives  60 us (53%)
  Pallas kernels  28.8 us (25%)
  starting transfers between devices  13.8 us (12%)
  waiting for transfers between devices  5.45 us (5%)
  between operations  1.56 us (1%)
    all_to_all x1, blocking collectives, shards(): sums = lax.all_to_all(sums, 'seq', 0, 0)  24.1 us
    all_to_all x1, blocking collectives, shards(): got = lax.all_to_all(total, 'seq', 0, 0)  18.9 us
    all_to_all x1, blocking collectives, shards(): got = lax.all_to_all(total, 'ep', 0, 0, axis_index_groups=groups)  17.1 us
    pallas_call x1, Pallas kernels, shards(): call(backward_kernel, [payload, payload], [pltpu.VMEM((wide, width), F32)...  14.2 us
    ppermute x1, starting transfers between devices, shards(): outer = lax.ppermute(outer, 'seq', far)  7.39 us
    pallas_call x1, Pallas kernels, shards(): call(project_kernel, [own] * 4 + [mid] * 2, [pltpu.VMEM((rows, width), F3...  6.77 us
    all_to_all x1, starting transfers between devices, shards(): got = lax.all_to_all(share, 'ep', 0, 0)  4.73 us
    pallas_call x1, Pallas kernels, shards(): call(forward_kernel, [shape((whole, width), BF16), shape((wide, width), B...  4.23 us
  transfers between devices with their start and end apart: 4, of which 2 were waited for; matrix products, arithmetic and copies ran while one was open for 0% of the time, Pallas kernels for 7%

profile of v9, /device:TPU:8, one launch (start us, length us, event | category | flops | bytes accessed | tf_op | source)
XLA Modules:
  0.0 110.5 jit_solution(15476006977747692679)
XLA Ops:
  0.6 0.0 copy-start
  0.6 0.0 copy-start.5
  1.4 0.8 slice_bitcast_fusion
  2.2 0.1 pad_add_fusion.place
  2.3 0.6 shard_map.136
  2.9 1.6 %collective-permute-start = (bf16[32,512]{1,0:T(8,128)(2,1)S(1)}, bf16[32,512]{1,0:T(8,128)(2,1)S(1)}, u32[]{:S(2)}, u32[]{:S(2)}) collective-permute-start(bf16[32,512]{1,0:T(8,128)(2,1)S(1)} %get-tuple-element.29), channel_id=1, source_target_pairs={{0,1},{1,0},{2,3},{3,2},{4,5},{5,4},{6,7},{7,6},{8,9},{9,8},{10,11... | collective-permute-start | bytes 98312 | tf_op jit(solution)/shard_map/ppermute | solution.py:460
  4.4 7.4 %collective-permute-start.1 = (bf16[32,512]{1,0:T(8,128)(2,1)S(1)}, bf16[32,512]{1,0:T(8,128)(2,1)S(1)}, u32[]{:S(2)}, u32[]{:S(2)}) collective-permute-start(bf16[32,512]{1,0:T(8,128)(2,1)S(1)} %get-tuple-element.30), channel_id=1, source_target_pairs={{0,31},{1,2},{2,1},{3,4},{4,3},{5,6},{6,5},{7,8},{8,7},{9,10},{10,... | collective-permute-start | bytes 98312 | tf_op jit(solution)/shard_map/ppermute | solution.py:461
  11.8 0.0 copy-done
  11.8 0.0 copy-done.1
  11.9 0.0 copy-start.6
  11.9 6.8 %shard_map.137 = (bf16[704,512]{1,0:T(8,128)(2,1)S(1)}, bf16[704,512]{1,0:T(8,128)(2,1)S(1)}, bf16[704,512]{1,0:T(8,128)(2,1)S(1)}, bf16[704,512]{1,0:T(8,128)(2...) custom-call(s32[4]{0:T(128)S(1)} %pad_add_fusion.place, bf16[704,512]{1,0:T(8,128)(2,1)S(1)} %bitcast.10, ...), custom_call_target="tpu_custom_call" | custom-call | flops 1476395008 | bytes 8388608 | tf_op jit(solution)/shard_map/pallas_call | solution.py:465
  18.6 0.0 collective-permute-done.inner_ref
  18.7 0.0 collective-permute-done.1.outer_ref
  18.7 0.0 copy-done.2
  18.7 0.0 copy-done.6
  18.7 0.0 copy-start.3
  18.7 0.0 copy-start.4
  18.7 0.0 copy-start.7
  18.7 4.2 %shard_map.138 = (bf16[768,512]{1,0:T(8,128)(2,1)S(1)}, bf16[736,512]{1,0:T(8,128)(2,1)S(1)}, bf16[736,512]{1,0:T(8,128)(2,1)S(1)}, f32[736,512]{1,0:T(8,128)S(1...) custom-call(s32[4]{0:T(128)S(1)} %pad_add_fusion.place, bf16[32,512]{1,0:T(8,128)(2,1)S(1)} %collective-permute-done.inner_ref, ...), custom_call_target="tpu_custom_call" | custom-call | flops 1476395008 | bytes 8388608 | tf_op jit(solution)/shard_map/pallas_call | solution.py:472
  23.0 24.1 %all_to_all.20.sums_ref = f32[32,8,640]{2,1,0:T(8,128)S(1)} all-to-all(f32[32,8,640]{2,1,0:T(8,128)S(1)} %get-tuple-element.34), channel_id=1, replica_groups=mesh['ep'=8,'seq'=32] {'seq'}, dimensions={0} | all-to-all | bytes 1310720 | tf_op jit(solution)/shard_map/all_to_all | solution.py:486
  47.0 14.2 %shard_map.139 = (bf16[4,832,128]{2,1,0:T(8,128)(2,1)S(1)}, bf16[4,832,128]{2,1,0:T(8,128)(2,1)S(1)}) custom-call(s32[4]{0:T(128)S(1)} %pad_add_fusion.place, f32[32,8,640]{2,1,0:T(8,128)S(1)} %all_to_all.20.sums_ref, bf16[512,512]{1,0:T(8,128)(2,1)S(1)} %copy-done.3, bf16[256,512]{1,0:T(8,128)(2,1)S(1)} %copy-done.4, f32[1,256]{1,0:T(1,128)S(1)} %copy-done.7, ...), custom_call_target="tpu_custom_call" | custom-call | flops 2952790016 | bytes 8388608 | tf_op jit(solution)/shard_map/pallas_call | solution.py:494
  61.3 0.1 collective-permute-start.2
  61.4 2.4 %collective-permute-done.2.got_ref = bf16[4,832,128]{2,1,0:T(8,128)(2,1)S(1)} collective-permute-done((bf16[4,832,128]{2,1,0:T(8,128)(2,1)S(1)}, bf16[4,832,128]{2,1,0:T(8,128)(2,1)S(1)}, u32[]{:S(2)}, u32[]{:S(2)}) %collective-permute-start.2) | collective-permute-done | bytes 852000 | tf_op jit(solution)/shard_map/ppermute | solution.py:514
  63.7 0.2 shard_map.140
  63.9 17.1 %all_to_all.21.got_ref = bf16[4,880,128]{2,1,0:T(8,128)(2,1)S(1)} all-to-all(bf16[4,880,128]{2,1,0:T(8,128)(2,1)S(1)} %shard_map.140), channel_id=1, replica_groups={{0,64,128,192},{32,96,160,224},{1,65,129,193},{33,97,161,225},{2,66,130..., dimensions={0} | all-to-all | bytes 1802240 | tf_op jit(solution)/shard_map/all_to_all | solution.py:521
  81.0 0.1 shard_map.142
  81.1 18.9 %all_to_all.22.got_ref = bf16[32,48,128]{2,1,0:T(8,128)(2,1)S(1)} all-to-all(bf16[32,48,128]{2,1,0:T(8,128)(2,1)S(1)} %shard_map.142), channel_id=1, replica_groups=mesh['ep'=8,'seq'=32] {'seq'}, dimensions={0} | all-to-all | bytes 786432 | tf_op jit(solution)/shard_map/all_to_all | solution.py:533
  100.0 0.8 shard_map.143
  100.8 4.7 %all-to-all-start.3 = ((f32[8,24,128]{2,1,0:T(8,128)}), f32[8,24,128]{2,1,0:T(8,128)S(1)}, u32[]{:S(2)}, u32[]{:S(2)}) async-start(f32[8,24,128]{2,1,0:T(8,128)} %get-tuple-element.48), calls=%async_computation.3 | async-start | bytes 196608 | tf_op jit(solution)/shard_map/all_to_all | solution.py:543
  105.5 1.3 %shard_map.141 = (f32[512,512]{1,0:T(8,128)}, f32[1,128]{1,0:T(1,128)}) custom-call(bf16[4,880,128]{2,1,0:T(8,128)(2,1)S(1)} %all_to_all.21.got_ref), custom_call_target="tpu_custom_call" | custom-call | flops 1048576 | bytes 8388608 | tf_op jit(solution)/shard_map/pallas_call | solution.py:527
  106.8 3.1 %all-to-all-done.3.got_ref = f32[8,24,128]{2,1,0:T(8,128)S(1)} async-done(((f32[8,24,128]{2,1,0:T(8,128)}), f32[8,24,128]{2,1,0:T(8,128)S(1)}, u32[]{:S(2)}, u32[]{:S(2)}) %all-to-all-start.3) | async-done | bytes 98336 | tf_op jit(solution)/shard_map/all_to_all | solution.py:543
  109.9 0.6 shard_map.144
  (6 shorter events, 0.0 us)
Async XLA Ops:
  0.6 11.2 %copy-start = (bf16[1,704,512]{2,1,0:T(8,128)(2,1)S(1)}, bf16[1,704,512]{2,1,0:T(8,128)(2,1)}, u32[]{:S(2)}) copy-start(bf16[1,704,512]{2,1,0:T(8,128)(2,1)} %param.9) | copy-start | bytes 2162692
  0.6 11.2 %copy-start.5 = (f32[31,512]{1,0:T(8,128)S(1)}, f32[31,512]{1,0:T(8,128)}, u32[]{:S(2)}) copy-start(f32[31,512]{1,0:T(8,128)} %taps_ref.5) | copy-start | bytes 190468
  0.7 11.2 %copy-start.1 = (bf16[512,1024]{1,0:T(8,128)(2,1)S(1)}, bf16[512,1024]{1,0:T(8,128)(2,1)}, u32[]{:S(2)}) copy-start(bf16[512,1024]{1,0:T(8,128)(2,1)} %w_in_ref.3) | copy-start | bytes 3145732
  2.9 15.8 %collective-permute-start = (bf16[32,512]{1,0:T(8,128)(2,1)S(1)}, bf16[32,512]{1,0:T(8,128)(2,1)S(1)}, u32[]{:S(2)}, u32[]{:S(2)}) collective-permute-start(bf16[32,512]{1,0:T(8,128)(2,1)S(1)} %get-tuple-element.29), channel_id=1, source_target_pairs={{0,1},{1,0},{2,3},{3,2},{4,5},{5,4},{6,7},{7,6},{8,9},{9,8},{10,11... | collective-permute-start | bytes 98312 | tf_op jit(solution)/shard_map/ppermute | solution.py:460
  4.4 14.2 %collective-permute-start.1 = (bf16[32,512]{1,0:T(8,128)(2,1)S(1)}, bf16[32,512]{1,0:T(8,128)(2,1)S(1)}, u32[]{:S(2)}, u32[]{:S(2)}) collective-permute-start(bf16[32,512]{1,0:T(8,128)(2,1)S(1)} %get-tuple-element.30), channel_id=1, source_target_pairs={{0,31},{1,2},{2,1},{3,4},{4,3},{5,6},{6,5},{7,8},{8,7},{9,10},{10,... | collective-permute-start | bytes 98312 | tf_op jit(solution)/shard_map/ppermute | solution.py:461
  11.8 6.8 %copy-start.2 = (bf16[512,512]{1,0:T(8,128)(2,1)S(1)}, bf16[512,512]{1,0:T(8,128)(2,1)}, u32[]{:S(2)}) copy-start(bf16[512,512]{1,0:T(8,128)(2,1)} %w_out_ref.3) | copy-start | bytes 1572868
  11.9 6.8 %copy-start.6 = (bf16[8,512]{1,0:T(8,128)(2,1)S(1)}, bf16[8,512]{1,0:T(8,128)(2,1)}, u32[]{:S(2)}) copy-start(bf16[8,512]{1,0:T(8,128)(2,1)} %query_ref.3) | copy-start | bytes 24580
  18.7 28.4 %copy-start.3 = (bf16[512,512]{1,0:T(8,128)(2,1)S(1)}, bf16[512,512]{1,0:T(8,128)(2,1)}, u32[]{:S(2)}) copy-start(bf16[512,512]{1,0:T(8,128)(2,1)} %w_value_ref.1) | copy-start | bytes 1572868
  18.7 28.3 %copy-start.4 = (bf16[256,512]{1,0:T(8,128)(2,1)S(1)}, bf16[256,512]{1,0:T(8,128)(2,1)}, u32[]{:S(2)}) copy-start(bf16[256,512]{1,0:T(8,128)(2,1)} %text_ref.1) | copy-start | bytes 786436
  18.7 28.3 %copy-start.7 = (f32[1,256]{1,0:T(1,128)S(1)}, f32[1,256]{1,0:T(1,128)}, u32[]{:S(2)}) copy-start(f32[1,256]{1,0:T(1,128)} %teacher_ref.1) | copy-start | bytes 3076
  61.3 2.5 %collective-permute-start.2 = (bf16[4,832,128]{2,1,0:T(8,128)(2,1)S(1)}, bf16[4,832,128]{2,1,0:T(8,128)(2,1)S(1)}, u32[]{:S(2)}, u32[]{:S(2)}) collective-permute-start(bf16[4,832,128]{2,1,0:T(8,128)(2,1)S(1)} %get-tuple-element.44), channel_id=1, source_target_pairs={{0,32},{32,0},{64,96},{96,64},{128,160},{160,128},{192,224},{224,1... | collective-permute-start | bytes 2555912 | tf_op jit(solution)/shard_map/ppermute | solution.py:514
  100.8 9.1 %all-to-all-start.3 = ((f32[8,24,128]{2,1,0:T(8,128)}), f32[8,24,128]{2,1,0:T(8,128)S(1)}, u32[]{:S(2)}, u32[]{:S(2)}) async-start(f32[8,24,128]{2,1,0:T(8,128)} %get-tuple-element.48), calls=%async_computation.3 | async-start | bytes 196608 | tf_op jit(solution)/shard_map/all_to_all | solution.py:543

commit v10 on v9

--- a/solution.py
+++ b/solution.py
@@ -167,8 +167,9 @@
     def scored(resid):
         return sum(dot(piece, queries, NT) for piece in split3(resid)) / root
 
-    score_ref[0:SIDE, :] = scored(resid_ref[0:SIDE, :])
-    score_ref[SIDE + rows :, :] = scored(resid_ref[SIDE + rows :, :])
+    sides = scored(jnp.concatenate([resid_ref[0:SIDE, :], resid_ref[SIDE + rows :, :]], axis=0))
+    score_ref[0:SIDE, :] = sides[:SIDE]
+    score_ref[SIDE + rows :, :] = sides[SIDE:]
     parts = 2
     chunk = rows // parts
     scores = []

time: 113 us -> 112 us (level)
  no operation moved by 1% of the time
where the time goes in v10:
time: 112 us; the launch traced here: 110 us
  blocking collectives  60 us (54%)
  Pallas kernels  28.6 us (26%)
  starting transfers between devices  13.8 us (12%)
  waiting for transfers between devices  5.45 us (5%)
  between operations  1.56 us (1%)
    all_to_all x1, blocking collectives, shards(): sums = lax.all_to_all(sums, 'seq', 0, 0)  24.1 us
    all_to_all x1, blocking collectives, shards(): got = lax.all_to_all(total, 'seq', 0, 0)  18.9 us
    all_to_all x1, blocking collectives, shards(): got = lax.all_to_all(total, 'ep', 0, 0, axis_index_groups=groups)  17.1 us
    pallas_call x1, Pallas kernels, shards(): call(backward_kernel, [payload, payload], [pltpu.VMEM((wide, width), F32)...  14.2 us
    ppermute x1, starting transfers between devices, shards(): outer = lax.ppermute(outer, 'seq', far)  7.39 us
    pallas_call x1, Pallas kernels, shards(): call(project_kernel, [own] * 4 + [mid] * 2, [pltpu.VMEM((rows, width), F3...  6.77 us
    all_to_all x1, starting transfers between devices, shards(): got = lax.all_to_all(share, 'ep', 0, 0)  4.73 us
    pallas_call x1, Pallas kernels, shards(): call(forward_kernel, [shape((whole, width), BF16), shape((wide, width), B...  4.05 us
  transfers between devices with their start and end apart: 4, of which 2 were waited for; matrix products, arithmetic and copies ran while one was open for 0% of the time, Pallas kernels for 7%

profile of v10, /device:TPU:8, one launch (start us, length us, event | category | flops | bytes accessed | tf_op | source)
XLA Modules:
  0.0 110.3 jit_solution(15209104014791034554)
XLA Ops:
  0.6 0.0 copy-start
  1.4 0.8 slice_bitcast_fusion
  2.2 0.1 pad_add_fusion.place
  2.3 0.6 shard_map.136
  2.9 1.6 %collective-permute-start = (bf16[32,512]{1,0:T(8,128)(2,1)S(1)}, bf16[32,512]{1,0:T(8,128)(2,1)S(1)}, u32[]{:S(2)}, u32[]{:S(2)}) collective-permute-start(bf16[32,512]{1,0:T(8,128)(2,1)S(1)} %get-tuple-element.29), channel_id=1, source_target_pairs={{0,1},{1,0},{2,3},{3,2},{4,5},{5,4},{6,7},{7,6},{8,9},{9,8},{10,11... | collective-permute-start | bytes 98312 | tf_op jit(solution)/shard_map/ppermute | solution.py:461
  4.4 7.4 %collective-permute-start.1 = (bf16[32,512]{1,0:T(8,128)(2,1)S(1)}, bf16[32,512]{1,0:T(8,128)(2,1)S(1)}, u32[]{:S(2)}, u32[]{:S(2)}) collective-permute-start(bf16[32,512]{1,0:T(8,128)(2,1)S(1)} %get-tuple-element.30), channel_id=1, source_target_pairs={{0,31},{1,2},{2,1},{3,4},{4,3},{5,6},{6,5},{7,8},{8,7},{9,10},{10,... | collective-permute-start | bytes 98312 | tf_op jit(solution)/shard_map/ppermute | solution.py:462
  11.8 0.0 copy-done
  11.8 0.0 copy-done.1
  11.9 0.0 copy-start.6
  11.9 6.8 %shard_map.137 = (bf16[704,512]{1,0:T(8,128)(2,1)S(1)}, bf16[704,512]{1,0:T(8,128)(2,1)S(1)}, bf16[704,512]{1,0:T(8,128)(2,1)S(1)}, bf16[704,512]{1,0:T(8,128)(2...) custom-call(s32[4]{0:T(128)S(1)} %pad_add_fusion.place, bf16[704,512]{1,0:T(8,128)(2,1)S(1)} %bitcast.10, ...), custom_call_target="tpu_custom_call" | custom-call | flops 1476395008 | bytes 8388608 | tf_op jit(solution)/shard_map/pallas_call | solution.py:466
  18.6 0.0 collective-permute-done.inner_ref
  18.7 0.0 collective-permute-done.1.outer_ref
  18.7 0.0 copy-done.2
  18.7 0.0 copy-done.6
  18.7 0.0 copy-start.3
  18.7 0.0 copy-start.4
  18.7 0.0 copy-start.7
  18.7 4.1 %shard_map.138 = (bf16[768,512]{1,0:T(8,128)(2,1)S(1)}, bf16[736,512]{1,0:T(8,128)(2,1)S(1)}, bf16[736,512]{1,0:T(8,128)(2,1)S(1)}, f32[736,512]{1,0:T(8,128)S(1...) custom-call(s32[4]{0:T(128)S(1)} %pad_add_fusion.place, bf16[32,512]{1,0:T(8,128)(2,1)S(1)} %collective-permute-done.inner_ref, ...), custom_call_target="tpu_custom_call" | custom-call | flops 1476395008 | bytes 8388608 | tf_op jit(solution)/shard_map/pallas_call | solution.py:473
  22.8 24.1 %all_to_all.20.sums_ref = f32[32,8,640]{2,1,0:T(8,128)S(1)} all-to-all(f32[32,8,640]{2,1,0:T(8,128)S(1)} %get-tuple-element.34), channel_id=1, replica_groups=mesh['ep'=8,'seq'=32] {'seq'}, dimensions={0} | all-to-all | bytes 1310720 | tf_op jit(solution)/shard_map/all_to_all | solution.py:487
  46.9 0.0 copy-done.3
  46.9 14.2 %shard_map.139 = (bf16[4,832,128]{2,1,0:T(8,128)(2,1)S(1)}, bf16[4,832,128]{2,1,0:T(8,128)(2,1)S(1)}) custom-call(s32[4]{0:T(128)S(1)} %pad_add_fusion.place, f32[32,8,640]{2,1,0:T(8,128)S(1)} %all_to_all.20.sums_ref, bf16[512,512]{1,0:T(8,128)(2,1)S(1)} %copy-done.3, bf16[256,512]{1,0:T(8,128)(2,1)S(1)} %copy-done.4, f32[1,256]{1,0:T(1,128)S(1)} %copy-done.7, ...), custom_call_target="tpu_custom_call" | custom-call | flops 2952790016 | bytes 8388608 | tf_op jit(solution)/shard_map/pallas_call | solution.py:495
  61.1 0.1 collective-permute-start.2
  61.2 2.4 %collective-permute-done.2.got_ref = bf16[4,832,128]{2,1,0:T(8,128)(2,1)S(1)} collective-permute-done((bf16[4,832,128]{2,1,0:T(8,128)(2,1)S(1)}, bf16[4,832,128]{2,1,0:T(8,128)(2,1)S(1)}, u32[]{:S(2)}, u32[]{:S(2)}) %collective-permute-start.2) | collective-permute-done | bytes 852000 | tf_op jit(solution)/shard_map/ppermute | solution.py:515
  63.5 0.2 shard_map.140
  63.7 17.1 %all_to_all.21.got_ref = bf16[4,880,128]{2,1,0:T(8,128)(2,1)S(1)} all-to-all(bf16[4,880,128]{2,1,0:T(8,128)(2,1)S(1)} %shard_map.140), channel_id=1, replica_groups={{0,64,128,192},{32,96,160,224},{1,65,129,193},{33,97,161,225},{2,66,130..., dimensions={0} | all-to-all | bytes 1802240 | tf_op jit(solution)/shard_map/all_to_all | solution.py:522
  80.8 0.1 shard_map.142
  80.9 18.9 %all_to_all.22.got_ref = bf16[32,48,128]{2,1,0:T(8,128)(2,1)S(1)} all-to-all(bf16[32,48,128]{2,1,0:T(8,128)(2,1)S(1)} %shard_map.142), channel_id=1, replica_groups=mesh['ep'=8,'seq'=32] {'seq'}, dimensions={0} | all-to-all | bytes 786432 | tf_op jit(solution)/shard_map/all_to_all | solution.py:534
  99.8 0.8 shard_map.143
  100.6 4.7 %all-to-all-start.3 = ((f32[8,24,128]{2,1,0:T(8,128)}), f32[8,24,128]{2,1,0:T(8,128)S(1)}, u32[]{:S(2)}, u32[]{:S(2)}) async-start(f32[8,24,128]{2,1,0:T(8,128)} %get-tuple-element.48), calls=%async_computation.3 | async-start | bytes 196608 | tf_op jit(solution)/shard_map/all_to_all | solution.py:544
  105.3 1.3 %shard_map.141 = (f32[512,512]{1,0:T(8,128)}, f32[1,128]{1,0:T(1,128)}) custom-call(bf16[4,880,128]{2,1,0:T(8,128)(2,1)S(1)} %all_to_all.21.got_ref), custom_call_target="tpu_custom_call" | custom-call | flops 1048576 | bytes 8388608 | tf_op jit(solution)/shard_map/pallas_call | solution.py:528
  106.6 3.1 %all-to-all-done.3.got_ref = f32[8,24,128]{2,1,0:T(8,128)S(1)} async-done(((f32[8,24,128]{2,1,0:T(8,128)}), f32[8,24,128]{2,1,0:T(8,128)S(1)}, u32[]{:S(2)}, u32[]{:S(2)}) %all-to-all-start.3) | async-done | bytes 98336 | tf_op jit(solution)/shard_map/all_to_all | solution.py:544
  109.7 0.6 shard_map.144
  (6 shorter events, 0.0 us)
Async XLA Ops:
  0.6 11.2 %copy-start = (bf16[1,704,512]{2,1,0:T(8,128)(2,1)S(1)}, bf16[1,704,512]{2,1,0:T(8,128)(2,1)}, u32[]{:S(2)}) copy-start(bf16[1,704,512]{2,1,0:T(8,128)(2,1)} %param.9) | copy-start | bytes 2162692
  0.6 11.2 %copy-start.5 = (f32[31,512]{1,0:T(8,128)S(1)}, f32[31,512]{1,0:T(8,128)}, u32[]{:S(2)}) copy-start(f32[31,512]{1,0:T(8,128)} %taps_ref.5) | copy-start | bytes 190468
  0.7 11.2 %copy-start.1 = (bf16[512,1024]{1,0:T(8,128)(2,1)S(1)}, bf16[512,1024]{1,0:T(8,128)(2,1)}, u32[]{:S(2)}) copy-start(bf16[512,1024]{1,0:T(8,128)(2,1)} %w_in_ref.3) | copy-start | bytes 3145732
  2.9 15.8 %collective-permute-start = (bf16[32,512]{1,0:T(8,128)(2,1)S(1)}, bf16[32,512]{1,0:T(8,128)(2,1)S(1)}, u32[]{:S(2)}, u32[]{:S(2)}) collective-permute-start(bf16[32,512]{1,0:T(8,128)(2,1)S(1)} %get-tuple-element.29), channel_id=1, source_target_pairs={{0,1},{1,0},{2,3},{3,2},{4,5},{5,4},{6,7},{7,6},{8,9},{9,8},{10,11... | collective-permute-start | bytes 98312 | tf_op jit(solution)/shard_map/ppermute | solution.py:461
  4.4 14.2 %collective-permute-start.1 = (bf16[32,512]{1,0:T(8,128)(2,1)S(1)}, bf16[32,512]{1,0:T(8,128)(2,1)S(1)}, u32[]{:S(2)}, u32[]{:S(2)}) collective-permute-start(bf16[32,512]{1,0:T(8,128)(2,1)S(1)} %get-tuple-element.30), channel_id=1, source_target_pairs={{0,31},{1,2},{2,1},{3,4},{4,3},{5,6},{6,5},{7,8},{8,7},{9,10},{10,... | collective-permute-start | bytes 98312 | tf_op jit(solution)/shard_map/ppermute | solution.py:462
  11.8 6.8 %copy-start.2 = (bf16[512,512]{1,0:T(8,128)(2,1)S(1)}, bf16[512,512]{1,0:T(8,128)(2,1)}, u32[]{:S(2)}) copy-start(bf16[512,512]{1,0:T(8,128)(2,1)} %w_out_ref.3) | copy-start | bytes 1572868
  11.9 6.8 %copy-start.6 = (bf16[8,512]{1,0:T(8,128)(2,1)S(1)}, bf16[8,512]{1,0:T(8,128)(2,1)}, u32[]{:S(2)}) copy-start(bf16[8,512]{1,0:T(8,128)(2,1)} %query_ref.3) | copy-start | bytes 24580
  18.7 28.2 %copy-start.3 = (bf16[512,512]{1,0:T(8,128)(2,1)S(1)}, bf16[512,512]{1,0:T(8,128)(2,1)}, u32[]{:S(2)}) copy-start(bf16[512,512]{1,0:T(8,128)(2,1)} %w_value_ref.1) | copy-start | bytes 1572868
  18.7 28.2 %copy-start.4 = (bf16[256,512]{1,0:T(8,128)(2,1)S(1)}, bf16[256,512]{1,0:T(8,128)(2,1)}, u32[]{:S(2)}) copy-start(bf16[256,512]{1,0:T(8,128)(2,1)} %text_ref.1) | copy-start | bytes 786436
  18.7 28.2 %copy-start.7 = (f32[1,256]{1,0:T(1,128)S(1)}, f32[1,256]{1,0:T(1,128)}, u32[]{:S(2)}) copy-start(f32[1,256]{1,0:T(1,128)} %teacher_ref.1) | copy-start | bytes 3076
  61.1 2.5 %collective-permute-start.2 = (bf16[4,832,128]{2,1,0:T(8,128)(2,1)S(1)}, bf16[4,832,128]{2,1,0:T(8,128)(2,1)S(1)}, u32[]{:S(2)}, u32[]{:S(2)}) collective-permute-start(bf16[4,832,128]{2,1,0:T(8,128)(2,1)S(1)} %get-tuple-element.44), channel_id=1, source_target_pairs={{0,32},{32,0},{64,96},{96,64},{128,160},{160,128},{192,224},{224,1... | collective-permute-start | bytes 2555912 | tf_op jit(solution)/shard_map/ppermute | solution.py:515
  100.6 9.1 %all-to-all-start.3 = ((f32[8,24,128]{2,1,0:T(8,128)}), f32[8,24,128]{2,1,0:T(8,128)S(1)}, u32[]{:S(2)}, u32[]{:S(2)}) async-start(f32[8,24,128]{2,1,0:T(8,128)} %get-tuple-element.48), calls=%async_computation.3 | async-start | bytes 196608 | tf_op jit(solution)/shard_map/all_to_all | solution.py:544
